TPU v7x, 32 devices: a whole 2x2x4 slice. The times are simulated.
32 devices in a mesh: dp: 8 (over z, x), mp: 4 (over y, core).
Axes of the slice: x: 2, y: 2, z: 4, core: 2. Of those that a mesh axis runs over, the one named last changes fastest.
Arguments:
- hidden_in: bfloat16 [16384, 768], P(('dp', 'mp')), may hold values from -6 to 6
- image_feats: bfloat16 [256, 257, 1408], P('dp'), may hold values from -6 to 6
- caption_lengths: int32 [256], P('dp'), may hold values from 5 to 32, as said below
- out_grad: bfloat16 [16384, 768], P(('dp', 'mp')), may hold values from -6 to 6
- proj_in: float32 [4, 768, 768], P(None, 'dp', 'mp')
- proj_in_moments: float32 [2, 4, 768, 768], P(None, None, 'dp', 'mp')
- proj_in_average: float32 [4, 768, 768], P(None, 'dp', 'mp')
- proj_out: float32 [2, 768, 768], P(None, ('mp', 'dp'))
- proj_out_moments: float32 [2, 2, 768, 768], P(None, None, ('mp', 'dp'))
- proj_out_average: float32 [2, 768, 768], P(None, ('mp', 'dp'))
- image_kv: float32 [2, 1408, 768], P(None, 'dp', 'mp')
- image_kv_moments: float32 [2, 2, 1408, 768], P(None, None, 'dp', 'mp')
- image_kv_average: float32 [2, 1408, 768], P(None, 'dp', 'mp')
- feed_up: float32 [768, 3072], P('dp', 'mp')
- feed_up_moments: float32 [2, 768, 3072], P(None, 'dp', 'mp')
- feed_up_average: float32 [768, 3072], P('dp', 'mp')
- feed_down: float32 [3072, 768], P(('mp', 'dp'))
- feed_down_moments: float32 [2, 3072, 768], P(None, ('mp', 'dp'))
- feed_down_average: float32 [3072, 768], P(('mp', 'dp'))
- norm_params: float32 [6, 768], P(None, ('mp', 'dp'))
- norm_params_moments: float32 [2, 6, 768], P(None, None, ('mp', 'dp'))
- norm_params_average: float32 [6, 768], P(None, ('mp', 'dp'))
Outputs:
- block_out: bfloat16 [16384, 768], P(('dp', 'mp'))
- input_grad: bfloat16 [16384, 768], P(('dp', 'mp'))
- new_proj_in: float32 [4, 768, 768], P(None, 'dp', 'mp')
- new_proj_in_moments: float32 [2, 4, 768, 768], P(None, None, 'dp', 'mp')
- new_proj_in_average: float32 [4, 768, 768], P(None, 'dp', 'mp')
- new_proj_out: float32 [2, 768, 768], P(None, ('mp', 'dp'))
- new_proj_out_moments: float32 [2, 2, 768, 768], P(None, None, ('mp', 'dp'))
- new_proj_out_average: float32 [2, 768, 768], P(None, ('mp', 'dp'))
- new_image_kv: float32 [2, 1408, 768], P(None, 'dp', 'mp')
- new_image_kv_moments: float32 [2, 2, 1408, 768], P(None, None, 'dp', 'mp')
- new_image_kv_average: float32 [2, 1408, 768], P(None, 'dp', 'mp')
- new_feed_up: float32 [768, 3072], P('dp', 'mp')
- new_feed_up_moments: float32 [2, 768, 3072], P(None, 'dp', 'mp')
- new_feed_up_average: float32 [768, 3072], P('dp', 'mp')
- new_feed_down: float32 [3072, 768], P(('mp', 'dp'))
- new_feed_down_moments: float32 [2, 3072, 768], P(None, ('mp', 'dp'))
- new_feed_down_average: float32 [3072, 768], P(('mp', 'dp'))
- new_norm_params: float32 [6, 768], P(None, ('mp', 'dp'))
- new_norm_params_moments: float32 [2, 6, 768], P(None, None, ('mp', 'dp'))
- new_norm_params_average: float32 [6, 768], P(None, ('mp', 'dp'))
- trust_ratios: float32 [16], replicated
- norm_values: float32 [2, 16], replicated
Inputs may be any that keep to these rules, and one draw needn't show every extreme that they name: `caption_lengths`: in every draw some caption has 32 tokens and some has 5.
All inputs are finite; a program needn't handle non-finite values.
Results may differ from a plain program's by a relative error of at most 0.025.
The roundings to bfloat16 on the way count: a program that leaves them out, or rounds other values in their place, can miss the bound.
Values may be sent and summed in bfloat16 or wider, within the bound.
No kernel may reach another device: no remote copies, remote signals or barrier semaphores. Data moves between devices by JAX's collectives and lax.ppermute only.
A program may use at most 192 MiB of HBM per device.

v0:
```python
import jax
import jax.numpy as jnp
from jax import lax
from jax.sharding import PartitionSpec as P

HEAD = 64
PATCHES = 257
QUERIES = 32
TEXT = 32
STEP = 10


NORM_EPSILON = 1e-06
ADAM_EPSILON = 1e-06
SQUARE_EPSILON = 1e-06
BETA_ONE = 0.9
BETA_TWO = 0.999
LEARN_RATE = 0.5
DECAY_RATE = 0.01
AVERAGE_RATE = 0.6
MASK_VALUE = -1e30


def layer_norm(inputs, gain, shift):
    centred = inputs - jnp.mean(inputs, axis=-1, keepdims=True)
    inverse = lax.rsqrt(jnp.mean(centred * centred, axis=-1, keepdims=True) + NORM_EPSILON)
    normed = centred * inverse
    return (normed * gain + shift, normed, inverse)


def norm_back(gradient, normed, inverse, gain):
    scaled = gradient * gain
    centre_term = jnp.mean(scaled, axis=-1, keepdims=True)
    normed_term = jnp.mean(scaled * normed, axis=-1, keepdims=True)
    return inverse * (scaled - centre_term - normed * normed_term)


def attn_scores(queries, key_rows, key_live):
    scale = queries.shape[-1] ** (-0.5)
    scores = (
        jnp.einsum("bqhe,bkhe->bhqk", queries, key_rows, preferred_element_type=jnp.float32) * scale
    )
    return jnp.where(key_live[:, None, None, :], scores, MASK_VALUE)


def attend_forward(queries, key_rows, value_rows, key_live):
    scores = attn_scores(queries, key_rows, key_live)
    row_max = jnp.max(scores, axis=-1, keepdims=True)
    exponents = jnp.exp(scores - row_max)
    totals = jnp.sum(exponents, axis=-1, keepdims=True)
    attn_probs = exponents / totals
    result = jnp.einsum(
        "bhqk,bkhe->bqhe",
        attn_probs.astype(jnp.bfloat16),
        value_rows,
        preferred_element_type=jnp.float32,
    )
    return (result.astype(jnp.bfloat16), row_max + jnp.log(totals))


def attend_backward(queries, key_rows, value_rows, key_live, log_total, grad_heads):
    scale = queries.shape[-1] ** (-0.5)
    attn_probs = jnp.exp(attn_scores(queries, key_rows, key_live) - log_total)
    grad_probs = jnp.einsum(
        "bqhe,bkhe->bhqk", grad_heads, value_rows, preferred_element_type=jnp.float32
    )
    grad_values = jnp.einsum(
        "bhqk,bqhe->bkhe",
        attn_probs.astype(jnp.bfloat16),
        grad_heads,
        preferred_element_type=jnp.float32,
    )
    inner_sum = jnp.sum(grad_probs * attn_probs, axis=-1, keepdims=True)
    grad_scores = (attn_probs * (grad_probs - inner_sum)).astype(jnp.bfloat16)
    grad_queries = (
        jnp.einsum("bhqk,bkhe->bqhe", grad_scores, key_rows, preferred_element_type=jnp.float32)
        * scale
    )
    grad_keys = (
        jnp.einsum("bhqk,bqhe->bkhe", grad_scores, queries, preferred_element_type=jnp.float32)
        * scale
    )
    return (
        grad_queries.astype(jnp.bfloat16),
        grad_keys.astype(jnp.bfloat16),
        grad_values.astype(jnp.bfloat16),
    )


def gelu_slope(inputs):
    cumulative = 0.5 * (1.0 + lax.erf(inputs * 0.7071067811865476))
    density = jnp.exp(-0.5 * inputs * inputs) * 0.3989422804014327
    return cumulative + inputs * density


def gather_rows(tokens):
    return lax.all_gather(tokens, "mp", axis=0, tiled=True)


def gather_grads(tokens):
    return lax.all_gather(tokens, "mp", axis=0, tiled=True)


def sum_rows(left_side, right_side):
    share_rows = left_side.shape[0] // lax.axis_size("mp")

    def partial_term(begin_row, row_count):
        return jnp.dot(left_side, right_side, preferred_element_type=jnp.float32)

    return lax.psum_scatter(
        partial_term(jnp.int32(0), share_rows * lax.axis_size("mp")),
        "mp",
        scatter_dimension=0,
        tiled=True,
    )


def sum_grads(left_side, right_side):
    share_rows = left_side.shape[0] // lax.axis_size("mp")

    def partial_term(begin_row, row_count):
        return jnp.einsum("tf,df->td", left_side, right_side, preferred_element_type=jnp.float32)

    return lax.psum_scatter(
        partial_term(jnp.int32(0), share_rows * lax.axis_size("mp")).astype(jnp.bfloat16),
        "mp",
        scatter_dimension=0,
        tiled=True,
    ).astype(jnp.float32)


def adam_step(weight, moments, gradient, decay_rate):
    moment_one = BETA_ONE * moments[0] + (1.0 - BETA_ONE) * gradient
    moment_two = BETA_TWO * moments[1] + (1.0 - BETA_TWO) * gradient * gradient
    update = (
        moment_one
        / (1.0 - BETA_ONE**STEP)
        / (jnp.sqrt(moment_two / (1.0 - BETA_TWO**STEP)) + ADAM_EPSILON)
        + decay_rate * weight
    )
    return (moment_one, moment_two, update)


def tensor_squares(values, per_slice):
    if per_slice:
        return jnp.sum(values * values, axis=tuple(range(1, values.ndim)))
    return jnp.sum(values * values)[None]


def per_device(
    hidden_in,
    image_feats,
    caption_lengths,
    out_grad,
    proj_in,
    proj_in_moments,
    proj_in_average,
    proj_out,
    proj_out_moments,
    proj_out_average,
    image_kv,
    image_kv_moments,
    image_kv_average,
    feed_up,
    feed_up_moments,
    feed_up_average,
    feed_down,
    feed_down_moments,
    feed_down_average,
    norm_params,
    norm_params_moments,
    norm_params_average,
):
    seq_len = QUERIES + TEXT
    model_ways = lax.axis_size("mp")
    items_all = caption_lengths.shape[0]
    items_here = items_all // model_ways
    features = hidden_in.shape[1]
    position = jnp.arange(seq_len)
    key_live = (position[None, :] < QUERIES) | (
        position[None, :] - QUERIES < caption_lengths[:, None]
    )
    local_live = lax.dynamic_slice_in_dim(
        key_live, lax.axis_index("mp") * items_here, items_here, 0
    )
    row_live = local_live.reshape(-1, 1).astype(jnp.float32)
    patch_live = jnp.ones((items_all, PATCHES), dtype=bool)
    gathered = (
        lax.all_gather(proj_in.astype(jnp.bfloat16), "dp", axis=1, tiled=True),
        lax.all_gather(proj_out.astype(jnp.bfloat16), "dp", axis=1, tiled=True),
        lax.all_gather(image_kv.astype(jnp.bfloat16), "dp", axis=1, tiled=True),
        lax.all_gather(feed_up.astype(jnp.bfloat16), "dp", axis=0, tiled=True),
        lax.all_gather(feed_down.astype(jnp.bfloat16), "dp", axis=0, tiled=True),
        lax.all_gather(norm_params.astype(jnp.bfloat16), "dp", axis=1, tiled=True),
    )
    in_weights, out_weights, image_weights, up_weights, down_weights, norm_part = gathered
    tokens_all, norm_gathered = (
        lax.all_gather(hidden_in, "mp", axis=0, tiled=True),
        lax.all_gather(norm_part, "mp", axis=1, tiled=True),
    )
    norm_float = norm_gathered.astype(jnp.float32)
    inner_width = in_weights.shape[2]
    heads_here = inner_width // HEAD

    def split_heads(values, length):
        return values.reshape(-1, length, heads_here, HEAD)

    self_proj = jnp.einsum(
        "td,kde->kte", tokens_all, in_weights[:3], preferred_element_type=jnp.float32
    ).astype(jnp.bfloat16)
    queries = split_heads(self_proj[0], seq_len)
    key_rows = split_heads(self_proj[1], seq_len)
    value_rows = split_heads(self_proj[2], seq_len)
    self_heads, self_total = attend_forward(queries, key_rows, value_rows, key_live)
    self_flat = self_heads.reshape(-1, inner_width)
    first_in = hidden_in.astype(jnp.float32) + sum_rows(self_flat, out_weights[0])
    after_one, normed_one, inverse_one = layer_norm(first_in, norm_float[0], norm_float[1])
    one_items = after_one.reshape(items_here, seq_len, features)
    one_query = one_items[:, :QUERIES].reshape(-1, features)
    query_all = gather_rows(one_query.astype(jnp.bfloat16))
    cross_queries = split_heads(
        jnp.dot(query_all, in_weights[3], preferred_element_type=jnp.float32).astype(jnp.bfloat16),
        QUERIES,
    )
    image_proj = jnp.einsum(
        "ipe,kec->kipc", image_feats, image_weights, preferred_element_type=jnp.float32
    ).astype(jnp.bfloat16)
    cross_keys = split_heads(image_proj[0], PATCHES)
    cross_values = split_heads(image_proj[1], PATCHES)
    cross_heads, cross_total = attend_forward(cross_queries, cross_keys, cross_values, patch_live)
    cross_flat = cross_heads.reshape(-1, inner_width)
    second_in = one_query + sum_rows(cross_flat, out_weights[1])
    after_two, normed_two, inverse_two = layer_norm(second_in, norm_float[2], norm_float[3])
    two_rows = jnp.concatenate(
        [after_two.reshape(items_here, QUERIES, features), one_items[:, QUERIES:]], axis=1
    ).reshape(-1, features)
    ffn_all = gather_rows(two_rows.astype(jnp.bfloat16))
    pre_act = jnp.dot(ffn_all, up_weights, preferred_element_type=jnp.float32)
    active = jax.nn.gelu(pre_act, approximate=False).astype(jnp.bfloat16)
    third_in = two_rows + sum_rows(active, down_weights)
    result, normed_three, inverse_three = layer_norm(third_in, norm_float[4], norm_float[5])
    block_out = result.astype(jnp.bfloat16)
    back_weights = (
        lax.all_gather(proj_in.astype(jnp.bfloat16), "dp", axis=1, tiled=True),
        lax.all_gather(proj_out.astype(jnp.bfloat16), "dp", axis=1, tiled=True),
        lax.all_gather(image_kv.astype(jnp.bfloat16), "dp", axis=1, tiled=True),
        lax.all_gather(feed_up.astype(jnp.bfloat16), "dp", axis=0, tiled=True),
        lax.all_gather(feed_down.astype(jnp.bfloat16), "dp", axis=0, tiled=True),
        lax.all_gather(norm_params.astype(jnp.bfloat16), "dp", axis=1, tiled=True),
    )
    back_in, back_out, back_image, back_up, back_down = back_weights[:5]
    out_slope = out_grad.astype(jnp.float32) * row_live
    gain_three = jnp.sum(out_slope * normed_three, axis=0)
    shift_three = jnp.sum(out_slope, axis=0)
    third_grad = norm_back(out_slope, normed_three, inverse_three, norm_float[4])
    ffn_grad_all = gather_grads(third_grad.astype(jnp.bfloat16))
    grad_active = jnp.einsum(
        "td,fd->tf", ffn_grad_all, back_down, preferred_element_type=jnp.float32
    )
    grad_down = jnp.einsum("tf,td->fd", active, ffn_grad_all, preferred_element_type=jnp.float32)
    grad_pre = (grad_active * gelu_slope(pre_act)).astype(jnp.bfloat16)
    grad_up = jnp.einsum("td,tf->df", ffn_all, grad_pre, preferred_element_type=jnp.float32)
    two_grad = third_grad + sum_grads(grad_pre, back_up)
    two_items = two_grad.reshape(items_here, seq_len, features)
    two_query = two_items[:, :QUERIES].reshape(-1, features)
    gain_two = jnp.sum(two_query * normed_two, axis=0)
    shift_two = jnp.sum(two_query, axis=0)
    second_grad = norm_back(two_query, normed_two, inverse_two, norm_float[2])
    cross_grad_all = gather_grads(second_grad.astype(jnp.bfloat16))
    cross_grad_heads = jnp.einsum(
        "qd,cd->qc", cross_grad_all, back_out[1], preferred_element_type=jnp.float32
    ).astype(jnp.bfloat16)
    grad_cross_out = jnp.einsum(
        "qc,qd->cd", cross_flat, cross_grad_all, preferred_element_type=jnp.float32
    )
    grad_cross_queries, grad_cross_keys, grad_cross_values = attend_backward(
        cross_queries,
        cross_keys,
        cross_values,
        patch_live,
        cross_total,
        split_heads(cross_grad_heads, QUERIES),
    )
    cross_query_flat = grad_cross_queries.reshape(-1, inner_width)
    grad_cross_query = jnp.einsum(
        "qd,qc->dc", query_all, cross_query_flat, preferred_element_type=jnp.float32
    )
    image_grads = jnp.stack([grad_cross_keys, grad_cross_values]).reshape(
        2, items_all, PATCHES, inner_width
    )
    grad_image = jnp.einsum(
        "ipe,kipc->kec", image_feats, image_grads, preferred_element_type=jnp.float32
    )
    one_query_grad = second_grad + sum_grads(cross_query_flat, back_in[3])
    one_grad = jnp.concatenate(
        [one_query_grad.reshape(items_here, QUERIES, features), two_items[:, QUERIES:]], axis=1
    ).reshape(-1, features)
    gain_one = jnp.sum(one_grad * normed_one, axis=0)
    shift_one = jnp.sum(one_grad, axis=0)
    first_grad = norm_back(one_grad, normed_one, inverse_one, norm_float[0])
    self_grad_all = gather_grads(first_grad.astype(jnp.bfloat16))
    self_grad_heads = jnp.einsum(
        "td,cd->tc", self_grad_all, back_out[0], preferred_element_type=jnp.float32
    ).astype(jnp.bfloat16)
    grad_self_out = jnp.einsum(
        "tc,td->cd", self_flat, self_grad_all, preferred_element_type=jnp.float32
    )
    grad_queries, grad_keys, grad_values = attend_backward(
        queries, key_rows, value_rows, key_live, self_total, split_heads(self_grad_heads, seq_len)
    )
    grad_proj = jnp.stack([grad_queries, grad_keys, grad_values]).reshape(3, -1, inner_width)
    grad_self_in = jnp.einsum(
        "td,kte->kde", tokens_all, grad_proj, preferred_element_type=jnp.float32
    )
    input_part = jnp.einsum(
        "kte,kde->td", grad_proj, back_in[:3], preferred_element_type=jnp.float32
    )
    norm_grad = jnp.stack([gain_one, shift_one, gain_two, shift_two, gain_three, shift_three])
    input_share, norm_share = (
        lax.psum_scatter(
            input_part.astype(jnp.bfloat16), "mp", scatter_dimension=0, tiled=True
        ).astype(jnp.float32),
        lax.psum_scatter(
            norm_grad.astype(jnp.bfloat16), "mp", scatter_dimension=1, tiled=True
        ).astype(jnp.float32),
    )
    input_grad = (first_grad + input_share).astype(jnp.bfloat16)
    in_shard, out_shard, image_shard, up_shard, down_shard, norm_shard = (
        lax.psum_scatter(
            jnp.concatenate([grad_self_in, grad_cross_query[None]], axis=0),
            "dp",
            scatter_dimension=1,
            tiled=True,
        ),
        lax.psum_scatter(
            jnp.stack([grad_self_out, grad_cross_out]), "dp", scatter_dimension=1, tiled=True
        ),
        lax.psum_scatter(grad_image, "dp", scatter_dimension=1, tiled=True),
        lax.psum_scatter(grad_up, "dp", scatter_dimension=0, tiled=True),
        lax.psum_scatter(grad_down, "dp", scatter_dimension=0, tiled=True),
        lax.psum_scatter(norm_share, "dp", scatter_dimension=1, tiled=True),
    )
    groups = [
        (proj_in, proj_in_moments, proj_in_average, in_shard, DECAY_RATE, True),
        (proj_out, proj_out_moments, proj_out_average, out_shard, DECAY_RATE, True),
        (image_kv, image_kv_moments, image_kv_average, image_shard, DECAY_RATE, True),
        (feed_up, feed_up_moments, feed_up_average, up_shard, DECAY_RATE, False),
        (feed_down, feed_down_moments, feed_down_average, down_shard, DECAY_RATE, False),
        (norm_params, norm_params_moments, norm_params_average, norm_shard, 0.0, True),
    ]
    updates = []
    weight_squares = []
    update_squares = []
    for weight, moments, average, gradient, decay_rate, per_slice in groups:
        moment_one, moment_two, update = adam_step(weight, moments, gradient, decay_rate)
        updates.append((moment_one, moment_two, update))
        weight_squares.append(tensor_squares(weight, per_slice))
        update_squares.append(tensor_squares(update, per_slice))
    squares = lax.psum(
        jnp.stack([jnp.concatenate(weight_squares), jnp.concatenate(update_squares)]), ("dp", "mp")
    )
    trust = jnp.sqrt(squares[0]) * lax.rsqrt(squares[1] + SQUARE_EPSILON)
    outputs = []
    offset = 0
    for group, stepped in zip(groups, updates):
        weight, moments, average, gradient, decay_rate, per_slice = group
        moment_one, moment_two, update = stepped
        slices = weight.shape[0] if per_slice else 1
        trust_part = trust[offset : offset + slices]
        if per_slice:
            trust_part = trust_part.reshape((slices,) + (1,) * (weight.ndim - 1))
        else:
            trust_part = trust_part[0]
        new_weight = weight - LEARN_RATE * trust_part * update
        outputs.append(new_weight)
        outputs.append(jnp.stack([moment_one, moment_two]))
        outputs.append(AVERAGE_RATE * average + (1.0 - AVERAGE_RATE) * new_weight)
        offset += slices
    return (
        block_out,
        input_grad,
        outputs[0],
        outputs[1],
        outputs[2],
        outputs[3],
        outputs[4],
        outputs[5],
        outputs[6],
        outputs[7],
        outputs[8],
        outputs[9],
        outputs[10],
        outputs[11],
        outputs[12],
        outputs[13],
        outputs[14],
        outputs[15],
        outputs[16],
        outputs[17],
        trust,
        jnp.sqrt(squares),
    )


def solution(mesh):
    return jax.shard_map(
        per_device,
        mesh=mesh,
        in_specs=(
            P(("dp", "mp"), None),
            P("dp", None, None),
            P("dp"),
            P(("dp", "mp"), None),
            P(None, "dp", "mp"),
            P(None, None, "dp", "mp"),
            P(None, "dp", "mp"),
            P(None, ("mp", "dp"), None),
            P(None, None, ("mp", "dp"), None),
            P(None, ("mp", "dp"), None),
            P(None, "dp", "mp"),
            P(None, None, "dp", "mp"),
            P(None, "dp", "mp"),
            P("dp", "mp"),
            P(None, "dp", "mp"),
            P("dp", "mp"),
            P(("mp", "dp"), None),
            P(None, ("mp", "dp"), None),
            P(("mp", "dp"), None),
            P(None, ("mp", "dp")),
            P(None, None, ("mp", "dp")),
            P(None, ("mp", "dp")),
        ),
        out_specs=(
            P(("dp", "mp"), None),
            P(("dp", "mp"), None),
            P(None, "dp", "mp"),
            P(None, None, "dp", "mp"),
            P(None, "dp", "mp"),
            P(None, ("mp", "dp"), None),
            P(None, None, ("mp", "dp"), None),
            P(None, ("mp", "dp"), None),
            P(None, "dp", "mp"),
            P(None, None, "dp", "mp"),
            P(None, "dp", "mp"),
            P("dp", "mp"),
            P(None, "dp", "mp"),
            P("dp", "mp"),
            P(("mp", "dp"), None),
            P(None, ("mp", "dp"), None),
            P(("mp", "dp"), None),
            P(None, ("mp", "dp")),
            P(None, None, ("mp", "dp")),
            P(None, ("mp", "dp")),
            P(),
            P(),
        ),
        check_vma=False,
    )
```

profile of v0, /device:TPU:0, one launch (start us, length us, event | category | flops | bytes accessed | tf_op | source)
XLA Modules:
  0.0 1208.8 jit_solution(7149293678888684778)
XLA Ops:
  11.7 36.0 %all_gather.45 = bf16[2,192,768]{2,1,0:T(8,128)(2,1)} all-gather(bf16[2,24,768]{2,1,0:T(8,128)(2,1)S(1)} %convert_element_type.185), channel_id=1, replica_groups=mesh['dp'=8,'mp'=4] {'dp'}, dimensions={1}, use_global_device_ids=true | all-gather | bytes 663552 | tf_op jit(solution)/shard_map/all_gather | solution.py:190
  47.6 11.4 all-gather.13.cloned.1.call-done
  61.6 26.8 %all-gather.15.cloned.1.call-done = bf16[2048,768]{1,0:T(8,128)(2,1)} async-done(((bf16[512,768]{1,0:T(8,128)(2,1)}), bf16[2048,768]{1,0:T(8,128)(2,1)}) %all-gather.15.cloned.1.call-update) | async-done | bytes 3145744 | tf_op jit(solution)/shard_map/all_gather | solution.py:198
  88.4 3.9 fusion.41
  100.8 4.8 fusion.121
  109.9 3.7 fusion.86
  115.9 26.1 %all-gather = bf16[8,24,6]{1,2,0:T(8,128)(2,1)S(1)} all-gather(bf16[1,24,6]{1,2,0:T(8,128)(2,1)S(1)} %convert_bitcast_fusion.1), channel_id=1, replica_groups=mesh['dp'=8,'mp'=4] {'dp'}, dimensions={0}, use_global_device_ids=true | all-gather | bytes 2592 | tf_op jit(solution)/shard_map/all_gather | solution.py:194
  142.1 5.2 all-gather.1
  147.5 24.8 %reduce-scatter.17.cloned.1.call-done = f32[512,768]{1,0:T(8,128)} async-done(((f32[2048,768]{1,0:T(8,128)}), f32[512,768]{1,0:T(8,128)}) %reduce-scatter.17.cloned.1.call-update) | async-done | bytes 1572880 | tf_op jit(solution)/shard_map/reduce_scatter | solution.py:110
  177.2 40.9 %all-gather.17.cloned.1.call-done = bf16[2,1408,192]{2,1,0:T(8,128)(2,1)} async-done(((bf16[2,176,192]{2,1,0:T(8,128)(2,1)}), bf16[2,1408,192]{2,1,0:T(8,128)(2,1)}) %all-gather.17.cloned.1.call-update) | async-done | bytes 1081360 | tf_op jit(solution)/shard_map/all_gather | solution.py:191
  218.2 20.6 %convert_bitcast_fusion = bf16[2,32,257,192]{3,2,1,0:T(8,128)(2,1)} fusion(bf16[32,257,1408]{2,0,1:T(8,128)(2,1)} %param.23, bf16[2,1408,192]{2,1,0:T(8,128)(2,1)} %all-gather.17.cloned.1.call-done), kind=kOutput, calls=%fused_computation.12 | convolution fusion | flops 8896131072 | bytes 30556160 | tf_op jit(solution)/shard_map/ipe,kec->kipc/dot_general | solution.py:225
  238.7 5.9 fusion.115
  244.6 7.4 copy.266
  252.0 7.4 copy.263
  269.3 3.7 multiply_reduce_fusion.1
  282.4 35.6 %reduce-scatter.19.cloned.1.call-done = f32[256,768]{1,0:T(8,128)} async-done(((f32[1024,768]{1,0:T(8,128)}), f32[256,768]{1,0:T(8,128)}) %reduce-scatter.19.cloned.1.call-update) | async-done | bytes 786448 | tf_op jit(solution)/shard_map/reduce_scatter | solution.py:110
  324.2 37.6 %all-gather.23.cloned.1.call-done = bf16[768,768]{1,0:T(8,128)(2,1)} async-done(((bf16[96,768]{1,0:T(8,128)(2,1)}), bf16[768,768]{1,0:T(8,128)(2,1)}) %all-gather.23.cloned.1.call-update) | async-done | bytes 1179664 | tf_op jit(solution)/shard_map/all_gather | solution.py:192
  361.8 29.5 %all-gather.21.cloned.1.call-done = bf16[2048,768]{1,0:T(8,128)(2,1)} async-done(((bf16[512,768]{1,0:T(8,128)(2,1)}), bf16[2048,768]{1,0:T(8,128)(2,1)}) %all-gather.21.cloned.1.call-update) | async-done | bytes 3145744 | tf_op jit(solution)/shard_map/all_gather | solution.py:97
  391.3 18.2 %fusion.11 = (bf16[2048,768]{1,0:T(8,128)(2,1)}, f32[2048,768]{1,0:T(8,128)}) fusion(bf16[2048,768]{1,0:T(8,128)(2,1)} %all-gather.21.cloned.1.call-done, bf16[768,768]{1,0:T(8,128)(2,1)} %all-gather.23.cloned.1.call-done), kind=kOutput, calls=%fused_computation.15 | convolution fusion | flops 2518155264 | bytes 13762560 | tf_op jit(solution)/shard_map/dot_general | solution.py:238
  409.5 25.7 %all-gather.25.cloned.1.call-done = bf16[768,768]{1,0:T(8,128)(2,1)} async-done(((bf16[96,768]{1,0:T(8,128)(2,1)}), bf16[768,768]{1,0:T(8,128)(2,1)}) %all-gather.25.cloned.1.call-update) | async-done | bytes 1179664 | tf_op jit(solution)/shard_map/all_gather | solution.py:193
  435.2 7.5 fusion.122
  442.8 57.1 %reduce-scatter.21.cloned.1.call-done = f32[512,768]{1,0:T(8,128)} async-done(((f32[2048,768]{1,0:T(8,128)}), f32[512,768]{1,0:T(8,128)}) %reduce-scatter.21.cloned.1.call-update) | async-done | bytes 1572880 | tf_op jit(solution)/shard_map/reduce_scatter | solution.py:110
  506.3 28.7 %all-gather.27.cloned.1.call-done = bf16[2048,768]{1,0:T(8,128)(2,1)} async-done(((bf16[512,768]{1,0:T(8,128)(2,1)}), bf16[2048,768]{1,0:T(8,128)(2,1)}) %all-gather.27.cloned.1.call-update) | async-done | bytes 3145744 | tf_op jit(solution)/shard_map/all_gather | solution.py:101
  535.0 6.9 fusion.17
  543.5 4.0 convolution_convert_fusion
  547.7 38.1 %reduce-scatter.23.cloned.1.call-done = bf16[512,768]{1,0:T(8,128)(2,1)} async-done(((bf16[2048,768]{1,0:T(8,128)(2,1)}), bf16[512,768]{1,0:T(8,128)(2,1)}) %reduce-scatter.23.cloned.1.call-update) | async-done | bytes 786448 | tf_op jit(solution)/shard_map/reduce_scatter | solution.py:124
  594.1 19.7 %all-gather.29.cloned.1.call-done = bf16[1024,768]{1,0:T(8,128)(2,1)} async-done(((bf16[256,768]{1,0:T(8,128)(2,1)}), bf16[1024,768]{1,0:T(8,128)(2,1)}) %all-gather.29.cloned.1.call-update) | async-done | bytes 1572880 | tf_op jit(solution)/shard_map/all_gather | solution.py:101
  620.8 5.7 multiply_reduce_fusion
  627.9 5.0 fusion.76
  639.2 27.8 %reduce-scatter.25.cloned.1.call-done = bf16[256,768]{1,0:T(8,128)(2,1)} async-done(((bf16[1024,768]{1,0:T(8,128)(2,1)}), bf16[256,768]{1,0:T(8,128)(2,1)}) %reduce-scatter.25.cloned.1.call-update) | async-done | bytes 393232 | tf_op jit(solution)/shard_map/reduce_scatter | solution.py:124
  676.1 6.9 fusion.124
  683.0 7.6 fusion.123
  690.7 6.0 convolution_convert_fusion.1
  696.7 7.6 copy.292
  704.3 3.6 multiply_convert_fusion
  707.9 7.5 copy.291
  715.4 50.8 %fusion.36 = f32[2,1408,192]{1,2,0:T(8,128)S(1)} fusion(bf16[32,257,1408]{2,0,1:T(8,128)(2,1)} %param.23, bf16[1,32,257,192]{3,2,1,0:T(8,128)(2,1)} %copy.292, bf16[1,32,257,192]{3,2,1,0:T(8,128)(2,1)} %copy.291), kind=kOutput, calls=%fused_computation.60 | convolution fusion | flops 8896131072 | bytes 31637504 | tf_op jit(solution)/shard_map/ipe,kipc->kec/dot_general | solution.py:291
  782.3 3.7 reshape.345
  786.0 3.8 multiply_reduce_fusion.2
  796.6 3.6 fusion.64
  822.9 6.2 bitcast_convert_fusion
  838.8 10.4 reduce-scatter.31.cloned.1.call-done
  852.8 121.8 %all-reduce.4.cloned.1.call-done = f32[2,1408,192]{2,0,1:T(2,128)} async-done(((f32[2,1408,192]{2,0,1:T(2,128)}), f32[2,1408,192]{2,0,1:T(2,128)}) %all-reduce.4.cloned.1.call-update) | async-done | bytes 2162704
  979.1 17.3 %reduce-scatter.37.cloned.1.call-done = bf16[192,6]{1,0:T(8,128)(2,1)} async-done(((bf16[768,6]{1,0:T(8,128)(2,1)}), bf16[192,6]{1,0:T(8,128)(2,1)}) %reduce-scatter.37.cloned.1.call-update) | async-done | bytes 2320
  997.4 22.0 %all-reduce.1 = f32[6,192]{1,0:T(8,128)S(1)} all-reduce(bf16[6,192]{1,0:T(8,128)(2,1)S(1)} %copy.321), channel_id=14, replica_groups=mesh['dp'=8,'mp'=4] {'dp'}, use_global_device_ids=true, to_apply=%region_48.49.clone | all-reduce | flops 1152 | bytes 6912
  1020.1 43.6 %reduce-scatter.29.cloned.1.call-done = f32[2,24,768]{2,1,0:T(8,128)} async-done(((f32[2,192,768]{2,1,0:T(8,128)}), f32[2,24,768]{2,1,0:T(8,128)}) %reduce-scatter.29.cloned.1.call-update) | async-done | bytes 147472 | tf_op jit(solution)/shard_map/reduce_scatter | solution.py:335
  1067.1 68.2 %reduce-scatter.35.cloned.1.call-done = f32[96,768]{1,0:T(8,128)} async-done(((f32[768,768]{1,0:T(8,128)}), f32[96,768]{1,0:T(8,128)}) %reduce-scatter.35.cloned.1.call-update) | async-done | bytes 294928
  1141.3 39.4 %psum.7 = f32[2,16]{1,0:T(2,128)S(1)} all-reduce(f32[2,16]{1,0:T(2,128)S(1)} %pad_maximum_fusion.10), channel_id=1, replica_groups=mesh['dp'=8,'mp'=4] {'dp','mp'}, use_global_device_ids=true, to_apply=%region_50.51 | all-reduce | flops 32 | bytes 256 | tf_op jit(solution)/shard_map/psum | solution.py:359
  (357 shorter events, 184.7 us)
Async XLA Ops:
  7.2 51.8 %all-gather.13.cloned.1.call-start = ((), (), s32[]{:S(2)}) async-start(), calls=%async_computation.11 | async-start | bytes 1769472 | tf_op jit(solution)/shard_map/all_gather | solution.py:189
  9.2 79.2 %all-gather.15.cloned.1.call-start = ((), (), s32[]{:S(2)}) async-start(), calls=%async_computation.12 | async-start | bytes 3932160 | tf_op jit(solution)/shard_map/all_gather | solution.py:198
  9.9 162.3 %reduce-scatter.17.cloned.1.call-start = ((), (), s32[]{:S(2)}) async-start(), calls=%async_computation.13 | async-start | bytes 7864320 | tf_op jit(solution)/shard_map/reduce_scatter | solution.py:110
  61.6 26.8 %copy-start.43 = (bf16[3,768,192]{1,2,0:T(8,128)(2,1)}, bf16[3,768,192]{1,2,0:T(8,128)(2,1)S(1)}, u32[]{:S(2)}) copy-start(bf16[3,768,192]{1,2,0:T(8,128)(2,1)S(1)} %copy.328) | copy-start | bytes 2654212
  100.8 5.7 copy-start.14
  113.6 58.6 %copy-start.21 = (bf16[512,768]{1,0:T(8,128)(2,1)S(1)}, bf16[512,768]{1,0:T(8,128)(2,1)}, u32[]{:S(2)}) copy-start(bf16[512,768]{1,0:T(8,128)(2,1)} %param.22) | copy-start | bytes 2359300
  113.6 104.5 %all-gather.17.cloned.1.call-start = ((), (), s32[]{:S(2)}) async-start(), calls=%async_computation.14 | async-start | bytes 1622016 | tf_op jit(solution)/shard_map/all_gather | solution.py:191
  115.9 146.4 %all-gather.19.cloned.1.call-start = ((), (), s32[]{:S(2)}) async-start(), calls=%async_computation.15 | async-start | bytes 1966080 | tf_op jit(solution)/shard_map/all_gather | solution.py:97
  177.2 140.8 %reduce-scatter.19.cloned.1.call-start = ((), (), s32[]{:S(2)}) async-start(), calls=%async_computation.16 | async-start | bytes 3932160 | tf_op jit(solution)/shard_map/reduce_scatter | solution.py:110
  262.2 7.1 copy-start.41
  269.3 5.2 slice-start.2
  269.3 5.2 slice-start.3
  281.5 80.3 %all-gather.23.cloned.1.call-start = ((), (), s32[]{:S(2)}) async-start(), calls=%async_computation.18 | async-start | bytes 1327104 | tf_op jit(solution)/shard_map/all_gather | solution.py:192
  282.3 109.0 %all-gather.21.cloned.1.call-start = ((), (), s32[]{:S(2)}) async-start(), calls=%async_computation.17 | async-start | bytes 3932160 | tf_op jit(solution)/shard_map/all_gather | solution.py:97
  323.4 111.7 %all-gather.25.cloned.1.call-start = ((), (), s32[]{:S(2)}) async-start(), calls=%async_computation.19 | async-start | bytes 1327104 | tf_op jit(solution)/shard_map/all_gather | solution.py:193
  324.2 175.7 %reduce-scatter.21.cloned.1.call-start = ((), (), s32[]{:S(2)}) async-start(), calls=%async_computation.20 | async-start | bytes 7864320 | tf_op jit(solution)/shard_map/reduce_scatter | solution.py:110
  442.7 92.3 %all-gather.27.cloned.1.call-start = ((), (), s32[]{:S(2)}) async-start(), calls=%async_computation.21 | async-start | bytes 3932160 | tf_op jit(solution)/shard_map/all_gather | solution.py:101
  506.3 79.4 %reduce-scatter.23.cloned.1.call-start = ((), (), s32[]{:S(2)}) async-start(), calls=%async_computation.22 | async-start | bytes 3932160 | tf_op jit(solution)/shard_map/reduce_scatter | solution.py:124
  535.0 8.6 copy-start.67
  547.6 66.2 %all-gather.29.cloned.1.call-start = ((), (), s32[]{:S(2)}) async-start(), calls=%async_computation.23 | async-start | bytes 1966080 | tf_op jit(solution)/shard_map/all_gather | solution.py:101
  589.4 24.5 %copy-start.31 = (bf16[2,192,768]{2,1,0:T(8,128)(2,1)S(1)}, bf16[2,192,768]{2,1,0:T(8,128)(2,1)}, u32[]{:S(2)}) copy-start(bf16[2,192,768]{2,1,0:T(8,128)(2,1)} %all_gather.45) | copy-start | bytes 1769476
  594.0 73.0 %reduce-scatter.25.cloned.1.call-start = ((), (), s32[]{:S(2)}) async-start(), calls=%async_computation.24 | async-start | bytes 1966080 | tf_op jit(solution)/shard_map/reduce_scatter | solution.py:124
  618.3 8.3 slice-start
  620.8 5.7 slice-start.1
  627.9 5.0 copy-start.3
  636.9 33.4 %copy-start.34 = (bf16[1024,192]{1,0:T(8,128)(2,1)}, bf16[1024,192]{1,0:T(8,128)(2,1)S(1)}, u32[]{:S(2)}) copy-start(bf16[1024,192]{1,0:T(8,128)(2,1)S(1)} %reshape.342) | copy-start | bytes 1179652
  638.7 137.5 %all-gather.31.cloned.1.call-start = ((), (), s32[]{:S(2)}) async-start(), calls=%async_computation.25 | async-start | bytes 3932160 | tf_op jit(solution)/shard_map/all_gather | solution.py:101
  676.0 159.2 %reduce-scatter.33.cloned.1.call-start = ((), (), s32[]{:S(2)}) async-start(), calls=%async_computation.29 | async-start | bytes 2654208 | tf_op jit(solution)/shard_map/reduce_scatter | solution.py:340
  683.0 166.3 %reduce-scatter.31.cloned.1.call-start = ((), (), s32[]{:S(2)}) async-start(), calls=%async_computation.28 | async-start | bytes 2654208 | tf_op jit(solution)/shard_map/reduce_scatter | solution.py:339
  690.6 284.0 %all-reduce.4.cloned.1.call-start = ((), (), s32[]{:S(2)}) async-start(), calls=%async_computation.32 | async-start | bytes 5767168
  696.7 7.6 copy-start.4
  696.7 7.6 copy-start.13
  769.7 226.8 %reduce-scatter.37.cloned.1.call-start = ((), (), s32[]{:S(2)}) async-start(), calls=%async_computation.31 | async-start | bytes 245760
  771.1 5.1 copy-start.10
  776.1 287.7 %reduce-scatter.29.cloned.1.call-start = ((), (), s32[]{:S(2)}) async-start(), calls=%async_computation.27 | async-start | bytes 1327104 | tf_op jit(solution)/shard_map/reduce_scatter | solution.py:335
  786.0 349.3 %reduce-scatter.35.cloned.1.call-start = ((), (), s32[]{:S(2)}) async-start(), calls=%async_computation.30 | async-start | bytes 2654208
  822.7 376.9 %reduce-scatter.27.cloned.1.call-start = ((), (), s32[]{:S(2)}) async-start(), calls=%async_computation.26 | async-start | bytes 3932160 | tf_op jit(solution)/shard_map/reduce_scatter | solution.py:320
  830.1 5.1 copy-start.27
  832.5 16.8 %copy-start.29 = (f32[96,768]{1,0:T(8,128)S(1)}, f32[96,768]{1,0:T(8,128)}, u32[]{:S(2)}) copy-start(f32[96,768]{1,0:T(8,128)} %param.35) | copy-start | bytes 884740
  835.2 139.5 %copy-start.20 = (f32[2,176,192]{2,1,0:T(8,128)S(1)}, f32[2,176,192]{2,1,0:T(8,128)}, u32[]{:S(2)}) copy-start(f32[2,176,192]{2,1,0:T(8,128)} %param.32) | copy-start | bytes 811012
  852.0 167.3 %copy-start.56 = (f32[6,24]{1,0:T(8,128)S(1)}, f32[6,24]{1,0:T(8,128)}, u32[]{:S(2)}) copy-start(f32[6,24]{1,0:T(8,128)} %param.41) | copy-start | bytes 1732
  852.0 211.8 %copy-start.40 = (f32[2,24,768]{2,1,0:T(8,128)S(1)}, f32[2,24,768]{2,1,0:T(8,128)}, u32[]{:S(2)}) copy-start(f32[2,24,768]{2,1,0:T(8,128)} %param.29) | copy-start | bytes 442372
  974.6 91.1 %copy-start.65 = (f32[2]{0:T(128)S(1)}, f32[2]{0:T(128)}, u32[]{:S(2)}) copy-start(f32[2]{0:T(128)} %get-tuple-element.219) | copy-start | bytes 28
  1136.8 46.5 %copy-start.39 = (f32[2,176,192]{2,0,1:T(2,128)S(1)}, f32[2,176,192]{2,0,1:T(2,128)}, u32[]{:S(2)}) copy-start(f32[2,176,192]{2,0,1:T(2,128)} %get-tuple-element.170) | copy-start | bytes 811012
  1138.1 48.4 %copy-start.37 = (f32[1,4,96,192]{2,3,1,0:T(8,128)S(1)}, f32[1,4,96,192]{2,3,1,0:T(8,128)}, u32[]{:S(2)}) copy-start(f32[1,4,96,192]{2,3,1,0:T(8,128)} %get-tuple-element.209) | copy-start | bytes 884740
  1138.1 48.4 %copy-start.38 = (f32[1,4,96,192]{2,3,1,0:T(8,128)S(1)}, f32[1,4,96,192]{2,3,1,0:T(8,128)}, u32[]{:S(2)}) copy-start(f32[1,4,96,192]{2,3,1,0:T(8,128)} %get-tuple-element.210) | copy-start | bytes 884740
  1186.5 6.7 copy-start.64
  1187.8 11.8 copy-start.15
  (48 other events, 139.0 us)
Sparse Core Ops, SparseCore 0:
  10.8 48.1 all-gather.12
  60.6 27.8 all-gather.14
  113.7 58.4 reduce-scatter.16
  175.1 43.0 all-gather.16
  220.2 17.9 all-gather.18
  281.7 36.2 reduce-scatter.18
  320.7 41.0 all-gather.22
  364.0 27.2 all-gather.20
  394.1 41.0 all-gather.24
  442.8 57.1 reduce-scatter.20
  506.4 28.5 all-gather.26
  547.7 37.9 reduce-scatter.22
  594.1 19.6 all-gather.28
  638.8 28.1 reduce-scatter.24
  676.2 28.5 all-gather.30
  708.5 68.9 reduce-scatter.32
  781.2 68.0 reduce-scatter.30
  853.2 121.3 all-reduce.3
  977.7 18.7 reduce-scatter.36
  999.7 64.0 reduce-scatter.28
  1067.3 67.9 reduce-scatter.34
  1137.8 37.1 reduce-scatter.26
where the time goes:
time: 1220 us; the launch traced here: 1210 us
  waiting for transfers between devices  666 us (55%)
  matrix products  200 us (16%)
  blocking collectives  129 us (11%)
  local copies, waits for them, and re-layouts  121 us (10%)
  other arithmetic  72.3 us (6%)
  between operations  18.5 us (2%)
    unnamed x25, waiting for transfers between devices  208 us
    reduce_scatter x3, waiting for transfers between devices, sum_rows(): lax.psum_scatter(partial_term(jnp.int32(0), share_rows * lax.axis_size('m...  118 us
    reduce_scatter x2, waiting for transfers between devices, sum_grads(): lax.psum_scatter(partial_term(jnp.int32(0), share_rows * lax.axis_size('m...  65.9 us
    dot_general x1, matrix products, per_device(): jnp.einsum('ipe,kipc->kec', image_feats, image_grads, preferred_element_t...  50.8 us
    all_gather x3, waiting for transfers between devices, gather_grads(): return lax.all_gather(tokens, 'mp', axis=0, tiled=True)  48.4 us
    reduce_scatter x1, waiting for transfers between devices, per_device(): lax.psum_scatter(jnp.stack([grad_self_out, grad_cross_out]), 'dp', scatte...  43.6 us
    all_gather x1, waiting for transfers between devices, per_device(): lax.all_gather(image_kv.astype(jnp.bfloat16), 'dp', axis=1, tiled=True)  40.9 us
    psum x1, blocking collectives, per_device(): lax.psum(jnp.stack([jnp.concatenate(weight_squares), jnp.concatenate(upda...  39.4 us
  transfers between devices with their start and end apart: 22, of which 18 were waited for; matrix products, arithmetic and copies ran while one was open for 22% of the time, Pallas kernels for 0%

commit v1 on v0

v1 whole, which is shorter than its diff:
```python
import jax
import jax.numpy as jnp
from jax import lax
from jax.experimental import pallas as pl
from jax.experimental.pallas import tpu as pltpu
from jax.sharding import PartitionSpec as P

HEAD = 64
PATCHES = 257
QUERIES = 32
TEXT = 32
SEQ = QUERIES + TEXT
STEP = 10


NORM_EPSILON = 1e-06
ADAM_EPSILON = 1e-06
SQUARE_EPSILON = 1e-06
BETA_ONE = 0.9
BETA_TWO = 0.999
LEARN_RATE = 0.5
DECAY_RATE = 0.01
AVERAGE_RATE = 0.6
MASK_VALUE = -1e30

AXES = ("dp", "mp")
GROUPS = 8
MODEL = 4
SLOTS = 16
NORM_ROWS = 8
BLOCK = 256
WIDE = 256
VMEM_LIMIT = 60 * 1024 * 1024

BF16 = jnp.bfloat16
F32 = jnp.float32


def dot_nn(left_side, right_side):
    return lax.dot_general(
        left_side, right_side, (((1,), (0,)), ((), ())), preferred_element_type=F32
    )


def dot_nt(left_side, right_side):
    return lax.dot_general(
        left_side, right_side, (((1,), (1,)), ((), ())), preferred_element_type=F32
    )


def dot_tn(left_side, right_side):
    return lax.dot_general(
        left_side, right_side, (((0,), (0,)), ((), ())), preferred_element_type=F32
    )


def normalise(inputs):
    centred = inputs - jnp.mean(inputs, axis=-1, keepdims=True)
    inverse = lax.rsqrt(jnp.mean(centred * centred, axis=-1, keepdims=True) + NORM_EPSILON)
    return centred * inverse, inverse


def norm_back(gradient, normed, inverse, gain):
    scaled = gradient * gain
    centre_term = jnp.mean(scaled, axis=-1, keepdims=True)
    normed_term = jnp.mean(scaled * normed, axis=-1, keepdims=True)
    return inverse * (scaled - centre_term - normed * normed_term)


def slot_x(place, block, y_rel):
    return place[block] * 8 + y_rel * 4 + place[GROUPS + block]


def slot_y(place, block, y_rel):
    return y_rel * 8 + place[block] * 4 + place[GROUPS + block]


def softmax(scores):
    exponents = jnp.exp(scores - jnp.max(scores, axis=-1, keepdims=True))
    return exponents / jnp.sum(exponents, axis=-1, keepdims=True)


def block_mask(lengths, first_item):
    per_block = BLOCK // SEQ
    row = lax.broadcasted_iota(jnp.int32, (BLOCK, BLOCK), 0)
    column = lax.broadcasted_iota(jnp.int32, (BLOCK, BLOCK), 1)
    row_item, column_item = lax.shift_right_logical(row, 6), lax.shift_right_logical(column, 6)
    slot = column - column_item * SEQ
    limit = jnp.zeros((BLOCK, BLOCK), jnp.int32)
    for item in range(per_block):
        limit = jnp.where(column_item == item, lengths[first_item + item] + QUERIES, limit)
    return (row_item == column_item) & (slot < limit)


def self_forward_kernel(
    place,
    lengths,
    hidden,
    in_own,
    in_other,
    out_own,
    out_other,
    first_in,
    qkv,
    heads,
    w_qkv,
    w_cross,
    w_self_out,
    w_cross_out,
    norm,
    self_rows,
    cross_rows,
):
    rows, features = hidden.shape
    width = features // MODEL
    block_rows = features // GROUPS
    out_rows = width // GROUPS
    norm_sum = jnp.zeros((NORM_ROWS, features), F32)
    for block in range(GROUPS):
        pieces = []
        for model in range(MODEL):
            side, y_rel = divmod(model, 2)
            pieces.append((in_own, in_other)[side][slot_x(place, block, y_rel)])
            out_piece = (out_own, out_other)[side][slot_y(place, block, y_rel)].astype(F32)
            begin = model * width + block * out_rows
            self_rows[begin : begin + out_rows, :] = out_piece[:out_rows]
            cross_rows[begin : begin + out_rows, :] = out_piece[out_rows : 2 * out_rows]
            norm_sum = norm_sum + out_piece[2 * out_rows :]
        begin = block * block_rows
        for kind in range(4):
            joined = jnp.concatenate(
                [piece[:, kind * width : (kind + 1) * width] for piece in pieces], axis=1
            )
            if kind < 3:
                w_qkv[begin : begin + block_rows, kind * features : (kind + 1) * features] = joined
            else:
                w_cross[begin : begin + block_rows, :] = joined
    norm[...] = norm_sum
    w_self_out[...] = self_rows[...].astype(BF16)
    w_cross_out[...] = cross_rows[...].astype(BF16)
    tokens = hidden[...]
    for kind in range(3):
        columns = slice(kind * features, (kind + 1) * features)
        qkv[:, columns] = dot_nn(tokens, w_qkv[:, columns]).astype(BF16)
    scale = HEAD ** (-0.5)
    for begin in range(0, rows, BLOCK):
        span = slice(begin, begin + BLOCK)
        mask = block_mask(lengths, begin // SEQ)
        for pair in range(features // (2 * HEAD)):
            results = []
            for head in (2 * pair, 2 * pair + 1):
                parts = [
                    qkv[span, kind * features + head * HEAD : kind * features + (head + 1) * HEAD]
                    for kind in range(3)
                ]
                scores = jnp.where(mask, dot_nt(parts[0], parts[1]) * scale, MASK_VALUE)
                results.append(dot_nn(softmax(scores).astype(BF16), parts[2]).astype(BF16))
            heads[span, pair * 2 * HEAD : (pair + 1) * 2 * HEAD] = jnp.concatenate(results, axis=1)
    first_in[...] = tokens.astype(F32) + dot_nn(heads[...], w_self_out[...])


def assemble_image(place, image_own, image_other, weight):
    block_rows = image_own.shape[1]
    width = image_own.shape[2] // 2
    features = width * MODEL
    for block in range(GROUPS):
        pieces = []
        for model in range(MODEL):
            side, y_rel = divmod(model, 2)
            pieces.append((image_own, image_other)[side][slot_y(place, block, y_rel)])
        begin = block * block_rows
        for kind in range(2):
            weight[begin : begin + block_rows, kind * features : (kind + 1) * features] = (
                jnp.concatenate(
                    [piece[:, kind * width : (kind + 1) * width] for piece in pieces], axis=1
                )
            )


def image_forward_kernel(place, feats, image_own, image_other, key_values, weight):
    @pl.when(pl.program_id(0) == 0)
    def _():
        assemble_image(place, image_own, image_other, weight)

    key_values[0] = dot_nn(feats[0], weight[...]).astype(BF16)


def head_rows(values, head_mask):
    stacked = jnp.concatenate([values] * (WIDE // HEAD), axis=0)
    return jnp.where(head_mask, stacked, jnp.zeros_like(stacked))


def fold_heads(values, head_mask):
    kept = jnp.where(head_mask, values, 0.0)
    count = WIDE // HEAD
    size = values.shape[0] // count
    total = kept[:size]
    for index in range(1, count):
        total = total + kept[index * size : (index + 1) * size]
    return total


def query_head_mask():
    shape = (QUERIES * (WIDE // HEAD), WIDE)
    row = lax.broadcasted_iota(jnp.int32, shape, 0)
    column = lax.broadcasted_iota(jnp.int32, shape, 1)
    return lax.shift_right_logical(row, 5) == lax.shift_right_logical(column, 6)


def query_rows(values):
    items = values.shape[0] // SEQ
    return jnp.concatenate(
        [values[item * SEQ : item * SEQ + QUERIES] for item in range(items)], axis=0
    )


def cross_forward_kernel(first_in, norm, w_cross, w_cross_out, key_values, second_in, queries, heads):
    features = first_in.shape[1]
    items = key_values.shape[0]
    normed, _ = normalise(query_rows(first_in[...]))
    one_query = normed * norm[0:1, :] + norm[1:2, :]
    queries[...] = dot_nn(one_query.astype(BF16), w_cross[...]).astype(BF16)
    head_mask = query_head_mask()
    scale = HEAD ** (-0.5)

    @pl.loop(0, items)
    def _(item):
        span = pl.ds(pl.multiple_of(item * QUERIES, QUERIES), QUERIES)
        for begin in range(0, features, WIDE):
            columns = slice(begin, begin + WIDE)
            value_columns = slice(features + begin, features + begin + WIDE)
            expanded = head_rows(queries[span, columns], head_mask)
            probs = softmax(dot_nt(expanded, key_values[item, :, columns]) * scale)
            mixed = dot_nn(probs.astype(BF16), key_values[item, :, value_columns])
            heads[span, columns] = fold_heads(mixed, head_mask).astype(BF16)

    second_in[...] = one_query + dot_nn(heads[...], w_cross_out[...])


def gelu_cumulative(inputs):
    return 0.5 * (1.0 + lax.erf(inputs * 0.7071067811865476))


def feed_kernel(
    place,
    lengths,
    first_in,
    second_in,
    norm,
    out_grad,
    up_own,
    up_other,
    down_own,
    down_other,
    block_out,
    two_grad,
    up_keep,
    up_send,
    down_keep,
    down_send,
    norm_grads,
    w_up,
    w_down,
    two_rows,
    pre_act,
    active,
):
    rows, features = first_in.shape
    items = rows // SEQ
    hidden_width = up_own.shape[2]
    up_rows = up_own.shape[1]
    down_rows = down_own.shape[1]
    for block in range(GROUPS):
        for model in range(MODEL):
            side, y_rel = divmod(model, 2)
            w_up[
                block * up_rows : (block + 1) * up_rows,
                model * hidden_width : (model + 1) * hidden_width,
            ] = (up_own, up_other)[side][slot_x(place, block, y_rel)]
            begin = model * hidden_width + block * down_rows
            w_down[begin : begin + down_rows, :] = (down_own, down_other)[side][
                slot_y(place, block, y_rel)
            ]
    normed_one, _ = normalise(first_in[...])
    after_one = normed_one * norm[0:1, :] + norm[1:2, :]
    normed_two, _ = normalise(second_in[...])
    after_two = normed_two * norm[2:3, :] + norm[3:4, :]
    for item in range(items):
        begin = item * SEQ
        two_rows[begin : begin + QUERIES, :] = after_two[item * QUERIES : (item + 1) * QUERIES]
        two_rows[begin + QUERIES : begin + SEQ, :] = after_one[begin + QUERIES : begin + SEQ]
    feed_in = two_rows[...].astype(BF16)
    third_in = two_rows[...]
    for model in range(MODEL):
        columns = slice(model * hidden_width, (model + 1) * hidden_width)
        pre = dot_nn(feed_in, w_up[:, columns])
        pre_act[:, columns] = pre
        act = (pre * gelu_cumulative(pre)).astype(BF16)
        active[:, columns] = act
        third_in = third_in + dot_nn(act, w_down[columns, :])
    normed, inverse = normalise(third_in)
    block_out[...] = (normed * norm[4:5, :] + norm[5:6, :]).astype(BF16)
    position = lax.broadcasted_iota(jnp.int32, (SEQ, features), 0)
    slope = jnp.concatenate(
        [
            jnp.where(
                position < lengths[item] + QUERIES,
                out_grad[item * SEQ : (item + 1) * SEQ, :].astype(F32),
                0.0,
            )
            for item in range(items)
        ],
        axis=0,
    )
    norm_grads[...] = jnp.zeros_like(norm_grads)
    norm_grads[4:5, :] = jnp.sum(slope * normed, axis=0, keepdims=True)
    norm_grads[5:6, :] = jnp.sum(slope, axis=0, keepdims=True)
    third_grad = norm_back(slope, normed, inverse, norm[4:5, :])
    grad_rows = third_grad.astype(BF16)
    two_grad[...] = third_grad
    for model in range(MODEL):
        side, y_rel = divmod(model, 2)
        columns = slice(model * hidden_width, (model + 1) * hidden_width)
        grad_down = dot_tn(active[:, columns], grad_rows).astype(BF16)
        for block in range(GROUPS):
            (down_keep, down_send)[side][slot_y(place, block, y_rel)] = grad_down[
                block * down_rows : (block + 1) * down_rows
            ]
        pre = pre_act[:, columns]
        density = jnp.exp(-0.5 * pre * pre) * 0.3989422804014327
        slope_part = gelu_cumulative(pre) + pre * density
        grad_pre = (dot_nt(grad_rows, w_down[columns, :]) * slope_part).astype(BF16)
        grad_up = dot_tn(feed_in, grad_pre).astype(BF16)
        for block in range(GROUPS):
            (up_keep, up_send)[side][slot_x(place, block, y_rel)] = grad_up[
                block * up_rows : (block + 1) * up_rows
            ]
        two_grad[...] += dot_nt(grad_pre, w_up[:, columns])


def cross_backward_kernel(
    two_grad,
    first_in,
    second_in,
    norm,
    w_cross,
    w_cross_out,
    queries,
    heads,
    key_values,
    norm_grads_in,
    grad_key_values,
    grad_cross,
    grad_cross_out,
    one_query_grad,
    norm_grads,
    head_grads,
    query_grads,
):
    features = first_in.shape[1]
    items = key_values.shape[0]
    two_query = query_rows(two_grad[...])
    normed, inverse = normalise(second_in[...])
    norm_grads[...] = norm_grads_in[...]
    norm_grads[2:3, :] = jnp.sum(two_query * normed, axis=0, keepdims=True)
    norm_grads[3:4, :] = jnp.sum(two_query, axis=0, keepdims=True)
    second_grad = norm_back(two_query, normed, inverse, norm[2:3, :])
    grad_rows = second_grad.astype(BF16)
    head_grads[...] = dot_nt(grad_rows, w_cross_out[...]).astype(BF16)
    grad_cross_out[...] = dot_tn(heads[...], grad_rows).astype(BF16)
    head_mask = query_head_mask()
    scale = HEAD ** (-0.5)

    @pl.loop(0, items)
    def _(item):
        span = pl.ds(pl.multiple_of(item * QUERIES, QUERIES), QUERIES)
        for begin in range(0, features, WIDE):
            columns = slice(begin, begin + WIDE)
            value_columns = slice(features + begin, features + begin + WIDE)
            expanded = head_rows(queries[span, columns], head_mask)
            expanded_grad = head_rows(head_grads[span, columns], head_mask)
            keys = key_values[item, :, columns]
            probs = softmax(dot_nt(expanded, keys) * scale)
            grad_probs = dot_nt(expanded_grad, key_values[item, :, value_columns])
            inner = jnp.sum(grad_probs * probs, axis=-1, keepdims=True)
            grad_scores = (probs * (grad_probs - inner)).astype(BF16)
            grad_key_values[item, :, value_columns] = dot_tn(
                probs.astype(BF16), expanded_grad
            ).astype(BF16)
            grad_key_values[item, :, columns] = (dot_tn(grad_scores, expanded) * scale).astype(BF16)
            query_grads[span, columns] = (
                fold_heads(dot_nn(grad_scores, keys), head_mask) * scale
            ).astype(BF16)

    normed_one, _ = normalise(query_rows(first_in[...]))
    query_in = (normed_one * norm[0:1, :] + norm[1:2, :]).astype(BF16)
    grad_cross[...] = dot_tn(query_in, query_grads[...]).astype(BF16)
    one_query_grad[...] = second_grad + dot_nt(query_grads[...], w_cross[...])


def image_backward_kernel(place, feats, grad_key_values, image_keep, image_send, total):
    block_rows = image_keep.shape[1]
    width = image_keep.shape[2] // 2
    features = width * MODEL

    @pl.when(pl.program_id(0) == 0)
    def _():
        total[...] = jnp.zeros_like(total)

    total[...] += dot_tn(feats[0], grad_key_values[0])

    @pl.when(pl.program_id(0) == pl.num_programs(0) - 1)
    def _():
        for block in range(GROUPS):
            span = slice(block * block_rows, (block + 1) * block_rows)
            for model in range(MODEL):
                side, y_rel = divmod(model, 2)
                piece = jnp.concatenate(
                    [
                        total[span, begin + model * width : begin + (model + 1) * width]
                        for begin in (0, features)
                    ],
                    axis=1,
                )
                (image_keep, image_send)[side][slot_y(place, block, y_rel)] = piece.astype(BF16)


def self_backward_kernel(
    place,
    lengths,
    one_query_grad,
    two_grad,
    first_in,
    norm,
    hidden,
    qkv,
    heads,
    w_qkv,
    w_self_out,
    grad_cross,
    grad_cross_out,
    norm_grads_in,
    input_grad,
    in_keep,
    in_send,
    out_keep,
    out_send,
    one_grad,
    head_grads,
    grad_qkv,
    grad_weights,
):
    rows, features = hidden.shape
    items = rows // SEQ
    width = features // MODEL
    block_rows = features // GROUPS
    out_rows = width // GROUPS
    for item in range(items):
        begin = item * SEQ
        one_grad[begin : begin + QUERIES, :] = one_query_grad[
            item * QUERIES : (item + 1) * QUERIES, :
        ]
        one_grad[begin + QUERIES : begin + SEQ, :] = two_grad[begin + QUERIES : begin + SEQ, :]
    normed, inverse = normalise(first_in[...])
    gradient = one_grad[...]
    norm_total = norm_grads_in[...] + jnp.concatenate(
        [
            jnp.sum(gradient * normed, axis=0, keepdims=True),
            jnp.sum(gradient, axis=0, keepdims=True),
            jnp.zeros((NORM_ROWS - 2, features), F32),
        ],
        axis=0,
    )
    first_grad = norm_back(gradient, normed, inverse, norm[0:1, :])
    one_grad[...] = first_grad
    grad_rows = first_grad.astype(BF16)
    head_grads[...] = dot_nt(grad_rows, w_self_out[...]).astype(BF16)
    scale = HEAD ** (-0.5)
    for begin in range(0, rows, BLOCK):
        span = slice(begin, begin + BLOCK)
        mask = block_mask(lengths, begin // SEQ)
        for pair in range(features // (2 * HEAD)):
            results = [[], [], []]
            for head in (2 * pair, 2 * pair + 1):
                queries, key_rows, value_rows = [
                    qkv[span, kind * features + head * HEAD : kind * features + (head + 1) * HEAD]
                    for kind in range(3)
                ]
                head_grad = head_grads[span, head * HEAD : (head + 1) * HEAD]
                probs = softmax(jnp.where(mask, dot_nt(queries, key_rows) * scale, MASK_VALUE))
                grad_probs = dot_nt(head_grad, value_rows)
                inner = jnp.sum(grad_probs * probs, axis=-1, keepdims=True)
                grad_scores = (probs * (grad_probs - inner)).astype(BF16)
                results[0].append((dot_nn(grad_scores, key_rows) * scale).astype(BF16))
                results[1].append((dot_tn(grad_scores, queries) * scale).astype(BF16))
                results[2].append(dot_tn(probs.astype(BF16), head_grad).astype(BF16))
            for kind in range(3):
                first = kind * features + pair * 2 * HEAD
                grad_qkv[span, first : first + 2 * HEAD] = jnp.concatenate(results[kind], axis=1)
    tokens = hidden[...]
    total = one_grad[...]
    for kind in range(3):
        columns = slice(kind * features, (kind + 1) * features)
        total = total + dot_nt(grad_qkv[:, columns], w_qkv[:, columns])
        grad_weights[:, columns] = dot_tn(tokens, grad_qkv[:, columns]).astype(BF16)
    input_grad[...] = total.astype(BF16)
    for block in range(GROUPS):
        span = slice(block * block_rows, (block + 1) * block_rows)
        for model in range(MODEL):
            side, y_rel = divmod(model, 2)
            columns = slice(model * width, (model + 1) * width)
            piece = [
                grad_weights[
                    span, kind * features + model * width : kind * features + (model + 1) * width
                ]
                for kind in range(3)
            ]
            piece.append(grad_cross[span, columns])
            (in_keep, in_send)[side][slot_x(place, block, y_rel)] = jnp.concatenate(piece, axis=1)
    grad_self_out = dot_tn(heads[...], grad_rows)
    grad_other_out = grad_cross_out[...].astype(F32)
    for block in range(GROUPS):
        for model in range(MODEL):
            side, y_rel = divmod(model, 2)
            begin = model * width + block * out_rows
            piece = jnp.concatenate(
                [
                    grad_self_out[begin : begin + out_rows],
                    grad_other_out[begin : begin + out_rows],
                    norm_total,
                ],
                axis=0,
            )
            (out_keep, out_send)[side][slot_y(place, block, y_rel)] = piece.astype(BF16)


SCALARS = pl.BlockSpec(memory_space=pltpu.SMEM)
WHOLE = pl.BlockSpec(memory_space=pltpu.VMEM)


def local_call(kernel, scalars, arrays, out_shapes, scratch, flops, name):
    size = sum(a.size * a.dtype.itemsize for a in arrays)
    size += sum(a.size * a.dtype.itemsize for a in out_shapes)
    return pl.pallas_call(
        kernel,
        out_shape=tuple(out_shapes),
        in_specs=[SCALARS] * len(scalars) + [WHOLE] * len(arrays),
        out_specs=tuple([WHOLE] * len(out_shapes)),
        scratch_shapes=scratch,
        compiler_params=pltpu.CompilerParams(vmem_limit_bytes=VMEM_LIMIT),
        cost_estimate=pl.CostEstimate(flops=flops, bytes_accessed=size, transcendentals=0),
        name=name,
    )(*scalars, *arrays)


def shape_of(*dims, dtype=BF16):
    return jax.ShapeDtypeStruct(dims, dtype)


class Direct:
    def __init__(self, dp, mp):
        self.count = dp * mp
        self.mp = mp
        self.depth = dp // 2
        index = lax.axis_index("dp")
        block = jnp.arange(GROUPS, dtype=jnp.int32)
        along_x = (block % 2) ^ (index % 2)
        along_z = (index // 2 - block // 2) % self.depth
        self.place = jnp.concatenate([along_x, along_z]).astype(jnp.int32)

    def hop(self, values, flip):
        return lax.ppermute(values, AXES, [(i, i ^ flip) for i in range(self.count)])

    def hop_core(self, values):
        return self.hop(values, 1)

    def hop_y(self, values):
        return self.hop(values, 2)

    def hop_x(self, values):
        return self.hop(values, self.mp)

    def hop_z(self, values):
        step = 2 * self.mp
        return lax.ppermute(values, AXES, [(i, (i + step) % self.count) for i in range(self.count)])

    def collect(self, piece, x_last):
        ring = [piece]
        for _ in range(self.depth - 1):
            ring.append(self.hop_z(ring[-1]))
        held = jnp.stack(ring)
        for hop in (self.hop_y, self.hop_x) if x_last else (self.hop_x, self.hop_y):
            held = jnp.concatenate([held, hop(held)])
        return held, self.hop_core(held)

    def scatter(self, keep, send, x_first):
        total = add(keep, self.hop_core(send))
        for hop in (self.hop_x, self.hop_y) if x_first else (self.hop_y, self.hop_x):
            half = total.shape[0] // 2
            total = add(total[:half], hop(total[half:]))
        carried = self.hop_z(total[1])
        for index in range(2, self.depth):
            carried = self.hop_z(add(total[index], carried))
        return total[0].astype(F32) + carried.astype(F32)


class Plain:
    def __init__(self, dp, mp):
        self.dp = dp
        self.mp = mp
        block = jnp.arange(GROUPS, dtype=jnp.int32)
        self.place = jnp.concatenate([block % 2, block // 2]).astype(jnp.int32)

    def collect(self, piece, x_last):
        rows, width = piece.shape
        blocks = lax.all_gather(piece, AXES, axis=0).reshape(self.dp, self.mp, rows, width)
        blocks = blocks.transpose(1, 0, 2, 3).reshape(2, 2, 4, 2, rows * self.dp // GROUPS, width)
        order = (0, 3, 1, 2, 4, 5) if x_last else (0, 1, 3, 2, 4, 5)
        blocks = blocks.transpose(order).reshape(2, SLOTS, rows * self.dp // GROUPS, width)
        return blocks[0], blocks[1]

    def scatter(self, keep, send, x_first):
        _, rows, width = keep.shape
        both = jnp.stack([keep, send])
        if x_first:
            both = both.reshape(2, 2, 2, 4, rows, width).transpose(0, 2, 3, 1, 4, 5)
        else:
            both = both.reshape(2, 2, 2, 4, rows, width).transpose(0, 1, 3, 2, 4, 5)
        both = both.reshape(self.mp, self.dp, rows * GROUPS // self.dp, width)
        both = both.transpose(1, 0, 2, 3).reshape(-1, width)
        return lax.psum_scatter(both.astype(F32), AXES, scatter_dimension=0, tiled=True)


def add(left_side, right_side):
    return (left_side.astype(F32) + right_side.astype(F32)).astype(BF16)


def adam_step(weight, moments, gradient, decay_rate):
    moment_one = BETA_ONE * moments[0] + (1.0 - BETA_ONE) * gradient
    moment_two = BETA_TWO * moments[1] + (1.0 - BETA_TWO) * gradient * gradient
    update = (
        moment_one
        / (1.0 - BETA_ONE**STEP)
        / (jnp.sqrt(moment_two / (1.0 - BETA_TWO**STEP)) + ADAM_EPSILON)
        + decay_rate * weight
    )
    return (moment_one, moment_two, update)


def tensor_squares(values, per_slice):
    if per_slice:
        return jnp.sum(values * values, axis=tuple(range(1, values.ndim)))
    return jnp.sum(values * values)[None]


def per_device(
    hidden_in,
    image_feats,
    caption_lengths,
    out_grad,
    proj_in,
    proj_in_moments,
    proj_in_average,
    proj_out,
    proj_out_moments,
    proj_out_average,
    image_kv,
    image_kv_moments,
    image_kv_average,
    feed_up,
    feed_up_moments,
    feed_up_average,
    feed_down,
    feed_down_moments,
    feed_down_average,
    norm_params,
    norm_params_moments,
    norm_params_average,
):
    data_ways, model_ways = lax.axis_size("dp"), lax.axis_size("mp")
    data_index, model_index = lax.axis_index("dp"), lax.axis_index("mp")
    rows, features = hidden_in.shape
    items = rows // SEQ
    patches, encoded = image_feats.shape[1:]
    hidden_width = feed_up.shape[1] * model_ways
    width = features // model_ways
    own_norm = norm_params.shape[1]
    norm_begin = (model_index * data_ways + data_index) * own_norm
    direct = data_ways == GROUPS and model_ways == MODEL
    moves = (Direct if direct else Plain)(data_ways, model_ways)
    place = moves.place
    lengths = lax.dynamic_slice_in_dim(caption_lengths, model_index * items, items, 0)
    first_item = (model_index * items).astype(jnp.int32)

    image_piece = jnp.concatenate([image_kv[0], image_kv[1]], axis=1).astype(BF16)
    in_piece = jnp.concatenate([proj_in[kind] for kind in range(4)], axis=1).astype(BF16)
    norm_rows = lax.dynamic_update_slice(
        jnp.zeros((NORM_ROWS, features), F32), norm_params, (0, norm_begin)
    ).astype(BF16)
    in_own, in_other = moves.collect(in_piece, True)
    if direct:
        out_piece = jnp.concatenate(
            [proj_out[0].astype(BF16), proj_out[1].astype(BF16), norm_rows], axis=0
        )
        out_own, out_other = moves.collect(out_piece, False)
    else:
        parts = [moves.collect(proj_out[kind].astype(BF16), False) for kind in range(2)]
        norm_all = lax.psum(norm_rows.astype(F32), AXES).astype(BF16)
        norm_first = jnp.zeros((SLOTS, NORM_ROWS, features), BF16).at[0].set(norm_all)
        out_own = jnp.concatenate([parts[0][0], parts[1][0], norm_first], axis=1)
        out_other = jnp.concatenate(
            [parts[0][1], parts[1][1], jnp.zeros_like(norm_first)], axis=1
        )
    image_own, image_other = moves.collect(image_piece, False)
    up_own, up_other = moves.collect(feed_up.astype(BF16), True)
    down_own, down_other = moves.collect(feed_down.astype(BF16), False)

    first_in, qkv, heads, w_qkv, w_cross, w_self_out, w_cross_out, norm = local_call(
        self_forward_kernel,
        (place, lengths),
        (hidden_in, in_own, in_other, out_own, out_other),
        (
            shape_of(rows, features, dtype=F32),
            shape_of(rows, 3 * features),
            shape_of(rows, features),
            shape_of(features, 3 * features),
            shape_of(features, features),
            shape_of(features, features),
            shape_of(features, features),
            shape_of(NORM_ROWS, features, dtype=F32),
        ),
        [pltpu.VMEM((features, features), F32), pltpu.VMEM((features, features), F32)],
        10 * rows * features * features,
        "self_forward",
    )
    image_place = jnp.concatenate([place, first_item[None]])
    feats_spec = pl.BlockSpec(
        (1, patches, encoded), lambda item, where: (where[2 * GROUPS] + item, 0, 0)
    )
    item_spec = pl.BlockSpec((1, patches, 2 * features), lambda item, where: (item, 0, 0))
    piece_spec = pl.BlockSpec(image_own.shape, lambda item, where: (0, 0, 0))
    image_cost = pl.CostEstimate(
        flops=4 * items * patches * encoded * features,
        bytes_accessed=2 * items * patches * (encoded + 2 * features) + 4 * encoded * features,
        transcendentals=0,
    )
    key_values = pl.pallas_call(
        image_forward_kernel,
        out_shape=shape_of(items, patches, 2 * features),
        grid_spec=pltpu.PrefetchScalarGridSpec(
            num_scalar_prefetch=1,
            grid=(items,),
            in_specs=[feats_spec, piece_spec, piece_spec],
            out_specs=item_spec,
            scratch_shapes=[pltpu.VMEM((encoded, 2 * features), BF16)],
        ),
        compiler_params=pltpu.CompilerParams(vmem_limit_bytes=VMEM_LIMIT),
        cost_estimate=image_cost,
        name="image_forward",
    )(image_place, image_feats, image_own, image_other)
    query_count = items * QUERIES
    second_in, cross_queries, cross_heads = local_call(
        cross_forward_kernel,
        (),
        (first_in, norm, w_cross, w_cross_out, key_values),
        (
            shape_of(query_count, features, dtype=F32),
            shape_of(query_count, features),
            shape_of(query_count, features),
        ),
        [],
        4 * query_count * features * features,
        "cross_forward",
    )
    piece_shape = up_own.shape
    block_out, two_grad, up_keep, up_send, down_keep, down_send, norm_grads = local_call(
        feed_kernel,
        (place, lengths),
        (
            first_in,
            second_in,
            norm,
            out_grad,
            up_own,
            up_other,
            down_own,
            down_other,
        ),
        (
            shape_of(rows, features),
            shape_of(rows, features, dtype=F32),
            shape_of(*piece_shape),
            shape_of(*piece_shape),
            shape_of(*down_own.shape),
            shape_of(*down_own.shape),
            shape_of(NORM_ROWS, features, dtype=F32),
        ),
        [
            pltpu.VMEM((features, hidden_width), BF16),
            pltpu.VMEM((hidden_width, features), BF16),
            pltpu.VMEM((rows, features), F32),
            pltpu.VMEM((rows, hidden_width), F32),
            pltpu.VMEM((rows, hidden_width), BF16),
        ],
        12 * rows * features * hidden_width,
        "feed",
    )
    up_shard = moves.scatter(up_keep, up_send, True)
    down_shard = moves.scatter(down_keep, down_send, False)

    grad_key_values, grad_cross, grad_cross_out, one_query_grad, norm_grads = local_call(
        cross_backward_kernel,
        (),
        (
            two_grad,
            first_in,
            second_in,
            norm,
            w_cross,
            w_cross_out,
            cross_queries,
            cross_heads,
            key_values,
            norm_grads,
        ),
        (
            shape_of(items, patches, 2 * features),
            shape_of(features, features),
            shape_of(features, features),
            shape_of(query_count, features, dtype=F32),
            shape_of(NORM_ROWS, features, dtype=F32),
        ),
        [pltpu.VMEM((query_count, features), BF16), pltpu.VMEM((query_count, features), BF16)],
        8 * query_count * features * features,
        "cross_backward",
    )
    image_keep, image_send = pl.pallas_call(
        image_backward_kernel,
        out_shape=(shape_of(*image_own.shape), shape_of(*image_own.shape)),
        grid_spec=pltpu.PrefetchScalarGridSpec(
            num_scalar_prefetch=1,
            grid=(items,),
            in_specs=[feats_spec, item_spec],
            out_specs=(piece_spec, piece_spec),
            scratch_shapes=[pltpu.VMEM((encoded, 2 * features), F32)],
        ),
        compiler_params=pltpu.CompilerParams(vmem_limit_bytes=VMEM_LIMIT),
        cost_estimate=image_cost,
        name="image_backward",
    )(image_place, image_feats, grad_key_values)
    image_shard = moves.scatter(image_keep, image_send, False)
    input_grad, in_keep, in_send, out_keep, out_send = local_call(
        self_backward_kernel,
        (place, lengths),
        (
            one_query_grad,
            two_grad,
            first_in,
            norm,
            hidden_in,
            qkv,
            heads,
            w_qkv,
            w_self_out,
            grad_cross,
            grad_cross_out,
            norm_grads,
        ),
        (
            shape_of(rows, features),
            shape_of(*in_own.shape),
            shape_of(*in_own.shape),
            shape_of(*out_own.shape),
            shape_of(*out_own.shape),
        ),
        [
            pltpu.VMEM((rows, features), F32),
            pltpu.VMEM((rows, features), BF16),
            pltpu.VMEM((rows, 3 * features), BF16),
            pltpu.VMEM((features, 3 * features), BF16),
        ],
        20 * rows * features * features,
        "self_backward",
    )
    in_shard = moves.scatter(in_keep, in_send, True)
    out_rows = proj_out.shape[1]
    if direct:
        out_sum = moves.scatter(out_keep, out_send, False)
        norm_sum = out_sum[2 * out_rows :]
        out_shard = jnp.stack([out_sum[:out_rows], out_sum[out_rows : 2 * out_rows]])
    else:
        piece = width // GROUPS
        norm_sum = lax.psum(out_keep[0, 2 * piece :].astype(F32), AXES)
        out_shard = jnp.stack(
            [
                moves.scatter(
                    out_keep[:, kind * piece : (kind + 1) * piece],
                    out_send[:, kind * piece : (kind + 1) * piece],
                    False,
                )
                for kind in range(2)
            ]
        )
    norm_shard = lax.dynamic_slice(norm_sum, (0, norm_begin), norm_params.shape)
    in_shard = jnp.stack([in_shard[:, kind * width : (kind + 1) * width] for kind in range(4)])
    image_shard = jnp.stack([image_shard[:, :width], image_shard[:, width:]])

    groups = [
        (proj_in, proj_in_moments, proj_in_average, in_shard, DECAY_RATE, True),
        (proj_out, proj_out_moments, proj_out_average, out_shard, DECAY_RATE, True),
        (image_kv, image_kv_moments, image_kv_average, image_shard, DECAY_RATE, True),
        (feed_up, feed_up_moments, feed_up_average, up_shard, DECAY_RATE, False),
        (feed_down, feed_down_moments, feed_down_average, down_shard, DECAY_RATE, False),
        (norm_params, norm_params_moments, norm_params_average, norm_shard, 0.0, True),
    ]
    updates = []
    weight_squares = []
    update_squares = []
    for weight, moments, average, gradient, decay_rate, per_slice in groups:
        moment_one, moment_two, update = adam_step(weight, moments, gradient, decay_rate)
        updates.append((moment_one, moment_two, update))
        weight_squares.append(tensor_squares(weight, per_slice))
        update_squares.append(tensor_squares(update, per_slice))
    own_squares = jnp.stack([jnp.concatenate(weight_squares), jnp.concatenate(update_squares)])
    ways = data_ways * model_ways
    copies = jnp.broadcast_to(own_squares[None], (ways,) + own_squares.shape)
    squares = jnp.sum(lax.all_to_all(copies, AXES, 0, 0, tiled=True), axis=0)
    trust = jnp.sqrt(squares[0]) * lax.rsqrt(squares[1] + SQUARE_EPSILON)
    outputs = []
    offset = 0
    for group, stepped in zip(groups, updates):
        weight, moments, average, gradient, decay_rate, per_slice = group
        moment_one, moment_two, update = stepped
        slices = weight.shape[0] if per_slice else 1
        trust_part = trust[offset : offset + slices]
        if per_slice:
            trust_part = trust_part.reshape((slices,) + (1,) * (weight.ndim - 1))
        else:
            trust_part = trust_part[0]
        new_weight = weight - LEARN_RATE * trust_part * update
        outputs.append(new_weight)
        outputs.append(jnp.stack([moment_one, moment_two]))
        outputs.append(AVERAGE_RATE * average + (1.0 - AVERAGE_RATE) * new_weight)
        offset += slices
    return (block_out, input_grad, *outputs, trust, jnp.sqrt(squares))


def solution(mesh):
    rows = P(AXES, None)
    by_column = P(None, "dp", "mp")
    by_row = P(None, ("mp", "dp"), None)
    weights = (
        by_column,
        P(None, None, "dp", "mp"),
        by_column,
        by_row,
        P(None, None, ("mp", "dp"), None),
        by_row,
        by_column,
        P(None, None, "dp", "mp"),
        by_column,
        P("dp", "mp"),
        P(None, "dp", "mp"),
        P("dp", "mp"),
        P(("mp", "dp"), None),
        P(None, ("mp", "dp"), None),
        P(("mp", "dp"), None),
        P(None, ("mp", "dp")),
        P(None, None, ("mp", "dp")),
        P(None, ("mp", "dp")),
    )
    return jax.shard_map(
        per_device,
        mesh=mesh,
        in_specs=(rows, P("dp", None, None), P("dp"), rows, *weights),
        out_specs=(rows, rows, *weights, P(), P()),
        check_vma=False,
    )
```

time: 1220 us -> 505 us (0.41)
  waiting for transfers between devices: 666 us -> 205 us
  matrix products: 200 us -> 0 us
  Pallas kernels: 0 us -> 155 us
  blocking collectives: 129 us -> 0 us
  local copies, waits for them, and re-layouts: 121 us -> 53.4 us
  starting transfers between devices: 1.93 us -> 55.1 us
  other arithmetic: 72.3 us -> 28.7 us
  between operations: 18.5 us -> 3.09 us
    reduce_scatter x9 -> x0, waiting for transfers between devices: 237 us -> none  [the longest x3 118 us: sum_rows(): lax.psum_scatter(partial_term(jnp.int32(0), share_rows * lax.axis_size('m...]
    all_gather x10 -> x0, waiting for transfers between devices: 220 us -> none  [the longest x3 48.4 us: gather_grads(): return lax.all_gather(tokens, 'mp', axis=0, tiled=True)]
    unnamed x25 -> x0, waiting for transfers between devices: 208 us -> none
    ppermute x0 -> x60, waiting for transfers between devices: none -> 203 us  [the longest x30 141 us: hop(): lax.ppermute(values, AXES, [(i, i ^ flip) for i in range(self.count)])]
    dot_general x32 -> x0, matrix products: 200 us -> none  [the longest x1 50.8 us: per_device(): jnp.einsum('ipe,kipc->kec', image_feats, image_grads, preferred_element_t...]
    pallas_call x0 -> x7, Pallas kernels: none -> 155 us  [the longest x5 113 us: local_call(): pl.pallas_call(kernel, out_shape=tuple(out_shapes), in_specs=[SCALARS] *...]
    all_gather x3 -> x0, blocking collectives: 67.2 us -> none  [the longest x1 36 us: per_device(): lax.all_gather(proj_out.astype(jnp.bfloat16), 'dp', axis=1, tiled=True)]
    ppermute x0 -> x60, starting transfers between devices: none -> 52.2 us  [the longest x30 33.8 us: hop(): lax.ppermute(values, AXES, [(i, i ^ flip) for i in range(self.count)])]
  transfers between devices with their start and end apart: 22 -> 61, of which waited for: 18 -> 34; matrix products, arithmetic and copies ran while one was open for 22% -> 14% of each run, Pallas kernels for 0% -> 15%
where the time goes in v1:
time: 505 us; the launch traced here: 501 us
  waiting for transfers between devices  205 us (41%)
  Pallas kernels  155 us (31%)
  starting transfers between devices  55.1 us (11%)
  local copies, waits for them, and re-layouts  53.4 us (11%)
  other arithmetic  28.7 us (6%)
    ppermute x30, waiting for transfers between devices, hop(): lax.ppermute(values, AXES, [(i, i ^ flip) for i in range(self.count)])  141 us
    pallas_call x5, Pallas kernels, local_call(): pl.pallas_call(kernel, out_shape=tuple(out_shapes), in_specs=[SCALARS] *...  113 us
    ppermute x30, waiting for transfers between devices, hop_z(): lax.ppermute(values, AXES, [(i, (i + step) % self.count) for i in range(s...  62.1 us
    unnamed x79, local copies, waits for them, and re-layouts  35.9 us
    ppermute x30, starting transfers between devices, hop(): lax.ppermute(values, AXES, [(i, i ^ flip) for i in range(self.count)])  33.8 us
    pallas_call x1, Pallas kernels, per_device(): pl.pallas_call(image_backward_kernel, out_shape=(shape_of(*image_own.shap...  25.2 us
    ppermute x30, starting transfers between devices, hop_z(): lax.ppermute(values, AXES, [(i, (i + step) % self.count) for i in range(s...  18.4 us
    pallas_call x1, Pallas kernels, per_device(): pl.pallas_call(image_forward_kernel, out_shape=shape_of(items, patches, 2...  16.8 us
  transfers between devices with their start and end apart: 61, of which 34 were waited for; matrix products, arithmetic and copies ran while one was open for 14% of the time, Pallas kernels for 15%

profile of v1, /device:TPU:0, one launch (start us, length us, event | category | flops | bytes accessed | tf_op | source)
XLA Modules:
  0.0 500.5 jit_solution(10965663862432952961)
XLA Ops:
  1.9 3.1 collective-permute-start.12
  7.7 1.8 collective-permute-start.6
  15.9 1.8 collective-permute-start.7
  21.6 3.0 collective-permute-done.18
  26.6 2.7 collective-permute-done.13
  30.0 2.5 collective-permute-done.1
  32.5 3.2 collective-permute-done.25
  35.6 3.2 collective-permute-done.19
  52.4 4.6 collective-permute-done.15
  63.6 6.0 %collective-permute-done.27 = bf16[4,96,768]{2,1,0:T(8,128)(2,1)S(1)} collective-permute-done((bf16[4,96,768]{2,1,0:T(8,128)(2,1)S(1)}, bf16[4,96,768]{2,1,0:T(8,128)(2,1)S(1)}, u32[]{:S(2)}, u32[]{:S(2)}) %collective-permute-start.27) | collective-permute-done | bytes 589856 | tf_op jit(solution)/shard_map/ppermute | solution.py:572
  72.2 1.7 collective-permute-done.21
  76.4 20.7 %collective-permute-done.16 = bf16[8,176,384]{2,1,0:T(8,128)(2,1)S(1)} collective-permute-done((bf16[8,176,384]{2,1,0:T(8,128)(2,1)S(1)}, bf16[8,176,384]{2,1,0:T(8,128)(2,1)S(1)}, u32[]{:S(2)}, u32[]{:S(2)}) %collective-permute-start.16) | collective-permute-done | bytes 1081376 | tf_op jit(solution)/shard_map/ppermute | solution.py:572
  101.2 23.4 %collective-permute-done.9 = bf16[4,56,768]{2,1,0:T(8,128)(2,1)S(1)} collective-permute-done((bf16[4,56,768]{2,1,0:T(8,128)(2,1)S(1)}, bf16[4,56,768]{2,1,0:T(8,128)(2,1)S(1)}, u32[]{:S(2)}, u32[]{:S(2)}) %collective-permute-start.9) | collective-permute-done | bytes 344096 | tf_op jit(solution)/shard_map/ppermute | solution.py:572
  129.0 10.2 %collective-permute-done.10 = bf16[8,56,768]{2,1,0:T(8,128)(2,1)S(1)} collective-permute-done((bf16[8,56,768]{2,1,0:T(8,128)(2,1)S(1)}, bf16[8,56,768]{2,1,0:T(8,128)(2,1)S(1)}, u32[]{:S(2)}, u32[]{:S(2)}) %collective-permute-start.10) | collective-permute-done | bytes 688160 | tf_op jit(solution)/shard_map/ppermute | solution.py:572
  139.4 25.0 %copy.54.feats = bf16[32,257,1408]{2,1,0:T(8,128)(2,1)} copy(bf16[32,257,1408]{2,0,1:T(8,128)(2,1)} %param.23) | data formatting | bytes 46317568 | tf_op args[1]
  166.2 16.8 %image_forward.1.key_values = bf16[8,257,1536]{2,1,0:T(8,128)(2,1)} custom-call(s32[17]{0:T(128)} %pad_add_fusion.1.place, bf16[32,257,1408]{2,1,0:T(8,128)(2,1)} %copy.54.feats, bf16[16,176,384]{2,1,0:T(8,128)(2,1)} %constant_dynamic-update-slice_fusion.27.image_own, bf16[16,176,384]{2,1,0:T(8,128)(2,1)} %collective-permute-done.17.image_other), custom_call_target="tpu_custom_call" | custom-call | flops 8892973056 | bytes 16431104 | tf_op jit(solution)/shard_map/image_forward/pallas_call | solution.py:747
  182.9 17.7 %self_forward.1 = (f32[512,768]{1,0:T(8,128)}, bf16[512,2304]{1,0:T(8,128)(2,1)}, bf16[512,768]{1,0:T(8,128)(2,1)}, bf16[768,2304]{1,0:T(8,128)(2,1)}, bf16[768,...) custom-call(s32[16]{0:T(128)} %pad_add_fusion.place, ...), custom_call_target="tpu_custom_call" | custom-call | flops 3019898880 | bytes 20078592 | tf_op jit(solution)/shard_map/self_forward/pallas_call | solution.py:544
  200.6 16.6 %cross_forward.1 = (f32[256,768]{1,0:T(8,128)}, bf16[256,768]{1,0:T(8,128)(2,1)}, bf16[256,768]{1,0:T(8,128)(2,1)}) custom-call(f32[512,768]{1,0:T(8,128)} %get-tuple-element.52.first_in, f32[8,768]{1,0:T(8,128)} %get-tuple-element.53.norm, bf16[768,768]{1,0:T(8,128)(2,1)} %get-tuple-element.54.w_cross, bf16[768,768]{1,0:T(8,128)(2,1)} %get-tuple-element.55.w_cross_out, ...), custom_call_target="tpu_custom_call" | custom-call | flops 603979776 | bytes 11845632 | tf_op jit(solution)/shard_map/cross_forward/pallas_call | solution.py:544
  217.2 26.1 %feed.1 = (bf16[512,768]{1,0:T(8,128)(2,1)}, f32[512,768]{1,0:T(8,128)}, bf16[16,96,768]{2,1,0:T(8,128)(2,1)}, bf16[16,96,768]{2,1,0:T(8,128)(2,1)}, bf16[16,96,...) custom-call(s32[16]{0:T(128)} %pad_add_fusion.place, s32[8]{0:T(128)} %dynamic_slice.6.lengths, ...), custom_call_target="tpu_custom_call" | custom-call | flops 14495514624 | bytes 24428544 | tf_op jit(solution)/shard_map/feed/pallas_call | solution.py:544
  243.2 24.6 %cross_backward.1 = (bf16[8,257,1536]{2,1,0:T(8,128)(2,1)}, bf16[768,768]{1,0:T(8,128)(2,1)}, bf16[768,768]{1,0:T(8,128)(2,1)}, f32[256,768]{1,0:T(8,128)}, f32[8,768]{1,0:T(8,128)}) custom-call(f32[512,768]{1,0:T(8,128)} %get-tuple-element.58.two_grad, f32[512,768]{1,0:T(8,128)} %get-tuple-element.52.first_in, f32[256,768]{1,0:T(8,128)} %get-tuple-element.56.second_in, ...), custom_call_target="tpu_custom_call" | custom-call | flops 1207959552 | bytes 22929408 | tf_op jit(solution)/shard_map/cross_backward/pallas_call | solution.py:544
  267.8 28.3 %self_backward.1 = (bf16[512,768]{1,0:T(8,128)(2,1)}, bf16[16,96,768]{2,1,0:T(8,128)(2,1)}, bf16[16,96,768]{2,1,0:T(8,128)(2,1)}, bf16[16,56,768]{2,1,0:T(8,128)(2,1)}, bf16[16,56,768]{2,1,0:T(8,128)(2,1)}) custom-call(s32[16]{0:T(128)} %pad_add_fusion.place, s32[8]{0:T(128)} %dynamic_slice.6.lengths, f32[256,768]{1,0:T(8,128)} %get-tuple-element.62.one_query_grad, ...), custom_call_target="tpu_custom_call" | custom-call | flops 6039797760 | bytes 23248896 | tf_op jit(solution)/shard_map/self_backward/pallas_call | solution.py:544
  296.3 25.2 %image_backward.1 = (bf16[16,176,384]{2,1,0:T(8,128)(2,1)}, bf16[16,176,384]{2,1,0:T(8,128)(2,1)}) custom-call(s32[17]{0:T(128)} %pad_add_fusion.1.place, bf16[32,257,1408]{2,1,0:T(8,128)(2,1)} %copy.54.feats, bf16[8,257,1536]{2,1,0:T(8,128)(2,1)} %get-tuple-element.75.grad_key_values), custom_call_target="tpu_custom_call" | custom-call | flops 8892973056 | bytes 16431104 | tf_op jit(solution)/shard_map/image_backward/pallas_call | solution.py:837
  322.1 1.8 add_convert_fusion.4
  324.0 1.7 collective-permute-start.37
  326.2 15.4 %collective-permute-done.37 = bf16[8,56,768]{2,1,0:T(8,128)(2,1)S(1)} collective-permute-done((bf16[8,56,768]{2,1,0:T(8,128)(2,1)S(1)}, bf16[8,56,768]{2,1,0:T(8,128)(2,1)S(1)}, u32[]{:S(2)}, u32[]{:S(2)}) %collective-permute-start.37) | collective-permute-done | bytes 688160 | tf_op jit(solution)/shard_map/ppermute | solution.py:572
  341.8 2.1 collective-permute-start.38
  344.6 1.7 collective-permute-start.43
  346.3 5.3 %collective-permute-done.38 = bf16[4,56,768]{2,1,0:T(8,128)(2,1)S(1)} collective-permute-done((bf16[4,56,768]{2,1,0:T(8,128)(2,1)S(1)}, bf16[4,56,768]{2,1,0:T(8,128)(2,1)S(1)}, u32[]{:S(2)}, u32[]{:S(2)}) %collective-permute-start.38) | collective-permute-done | bytes 344096 | tf_op jit(solution)/shard_map/ppermute | solution.py:572
  354.4 3.8 collective-permute-done.39
  359.1 1.8 collective-permute-start.49
  360.9 3.7 collective-permute-done.40
  365.5 1.8 collective-permute-start.31
  367.3 3.6 collective-permute-done.41
  372.9 1.8 collective-permute-start.44
  375.0 19.9 %collective-permute-done.55 = bf16[8,96,768]{2,1,0:T(8,128)(2,1)S(1)} collective-permute-done((bf16[8,96,768]{2,1,0:T(8,128)(2,1)S(1)}, bf16[8,96,768]{2,1,0:T(8,128)(2,1)S(1)}, u32[]{:S(2)}, u32[]{:S(2)}) %collective-permute-start.55) | collective-permute-done | bytes 1179680 | tf_op jit(solution)/shard_map/ppermute | solution.py:572
  395.6 29.3 %collective-permute-done.44 = bf16[4,176,384]{2,1,0:T(8,128)(2,1)S(1)} collective-permute-done((bf16[4,176,384]{2,1,0:T(8,128)(2,1)S(1)}, bf16[4,176,384]{2,1,0:T(8,128)(2,1)S(1)}, u32[]{:S(2)}, u32[]{:S(2)}) %collective-permute-start.44) | collective-permute-done | bytes 540704 | tf_op jit(solution)/shard_map/ppermute | solution.py:572
  427.2 4.8 collective-permute-done.45
  434.1 6.3 %collective-permute-done.46 = bf16[176,384]{1,0:T(8,128)(2,1)S(1)} collective-permute-done((bf16[176,384]{1,0:T(8,128)(2,1)S(1)}, bf16[176,384]{1,0:T(8,128)(2,1)S(1)}, u32[]{:S(2)}, u32[]{:S(2)}) %collective-permute-start.46) | collective-permute-done | bytes 135200 | tf_op jit(solution)/shard_map/ppermute | solution.py:585
  440.9 2.4 collective-permute-start.51
  443.3 3.6 collective-permute-done.32
  451.1 1.9 collective-permute-start.58
  454.3 3.1 collective-permute-done.33
  457.4 2.5 collective-permute-done.58
  460.0 6.0 %collective-permute-done.34 = bf16[96,768]{1,0:T(8,128)(2,1)S(1)} collective-permute-done((bf16[96,768]{1,0:T(8,128)(2,1)S(1)}, bf16[96,768]{1,0:T(8,128)(2,1)S(1)}, u32[]{:S(2)}, u32[]{:S(2)}) %collective-permute-start.34) | collective-permute-done | bytes 147488 | tf_op jit(solution)/shard_map/ppermute | solution.py:585
  466.2 6.8 %collective-permute-done.35 = bf16[96,768]{1,0:T(8,128)(2,1)S(1)} collective-permute-done((bf16[96,768]{1,0:T(8,128)(2,1)S(1)}, bf16[96,768]{1,0:T(8,128)(2,1)S(1)}, u32[]{:S(2)}, u32[]{:S(2)}) %collective-permute-start.35) | collective-permute-done | bytes 147488 | tf_op jit(solution)/shard_map/ppermute | solution.py:585
  481.7 2.9 all-to-all-start
  484.7 1.9 pad_maximum_fusion.6
  489.6 2.3 all-to-all-done
  (274 shorter events, 91.5 us)
Async XLA Ops:
  1.9 15.8 %collective-permute-start.12 = (bf16[176,384]{1,0:T(8,128)(2,1)S(1)}, bf16[176,384]{1,0:T(8,128)(2,1)S(1)}, u32[]{:S(2)}, u32[]{:S(2)}) collective-permute-start(bf16[176,384]{1,0:T(8,128)(2,1)S(1)} %pad_maximum_fusion.18), channel_id=1, source_target_pairs={{0,8},{1,9},{2,10},{3,11},{4,12},{5,13},{6,14},{7,15},{8,16},{9,17... | collective-permute-start | bytes 405512 | tf_op jit(solution)/shard_map/ppermute | solution.py:585
  9.6 10.4 %collective-permute-start = (bf16[96,768]{1,0:T(8,128)(2,1)S(1)}, bf16[96,768]{1,0:T(8,128)(2,1)S(1)}, u32[]{:S(2)}, u32[]{:S(2)}) collective-permute-start(bf16[96,768]{1,0:T(8,128)(2,1)S(1)} %pad_maximum_fusion.14), channel_id=1, source_target_pairs={{0,8},{1,9},{2,10},{3,11},{4,12},{5,13},{6,14},{7,15},{8,16},{9,17... | collective-permute-start | bytes 442376 | tf_op jit(solution)/shard_map/ppermute | solution.py:585
  11.4 13.2 %collective-permute-start.18 = (bf16[96,768]{1,0:T(8,128)(2,1)S(1)}, bf16[96,768]{1,0:T(8,128)(2,1)S(1)}, u32[]{:S(2)}, u32[]{:S(2)}) collective-permute-start(bf16[96,768]{1,0:T(8,128)(2,1)S(1)} %get-tuple-element.175), channel_id=1, source_target_pairs={{0,8},{1,9},{2,10},{3,11},{4,12},{5,13},{6,14},{7,15},{8,16},{9,17... | collective-permute-start | bytes 442376 | tf_op jit(solution)/shard_map/ppermute | solution.py:585
  15.9 60.5 %collective-permute-start.7 = (bf16[56,768]{1,0:T(8,128)(2,1)S(1)}, bf16[56,768]{1,0:T(8,128)(2,1)S(1)}, u32[]{:S(2)}, u32[]{:S(2)}) collective-permute-start(bf16[56,768]{1,0:T(8,128)(2,1)S(1)} %collective-permute-done.6), channel_id=1, source_target_pairs={{0,8},{1,9},{2,10},{3,11},{4,12},{5,13},{6,14},{7,15},{8,16},{9,17... | collective-permute-start | bytes 258056 | tf_op jit(solution)/shard_map/ppermute | solution.py:585
  17.7 11.6 %collective-permute-start.13 = (bf16[176,384]{1,0:T(8,128)(2,1)S(1)}, bf16[176,384]{1,0:T(8,128)(2,1)S(1)}, u32[]{:S(2)}, u32[]{:S(2)}) collective-permute-start(bf16[176,384]{1,0:T(8,128)(2,1)S(1)} %collective-permute-done.12), channel_id=1, source_target_pairs={{0,8},{1,9},{2,10},{3,11},{4,12},{5,13},{6,14},{7,15},{8,16},{9,17... | collective-permute-start | bytes 405512 | tf_op jit(solution)/shard_map/ppermute | solution.py:585
  19.9 12.5 %collective-permute-start.1 = (bf16[96,768]{1,0:T(8,128)(2,1)S(1)}, bf16[96,768]{1,0:T(8,128)(2,1)S(1)}, u32[]{:S(2)}, u32[]{:S(2)}) collective-permute-start(bf16[96,768]{1,0:T(8,128)(2,1)S(1)} %collective-permute-done), channel_id=1, source_target_pairs={{0,8},{1,9},{2,10},{3,11},{4,12},{5,13},{6,14},{7,15},{8,16},{9,17... | collective-permute-start | bytes 442376 | tf_op jit(solution)/shard_map/ppermute | solution.py:585
  21.4 14.2 %collective-permute-start.25 = (bf16[96,768]{1,0:T(8,128)(2,1)S(1)}, bf16[96,768]{1,0:T(8,128)(2,1)S(1)}, u32[]{:S(2)}, u32[]{:S(2)}) collective-permute-start(bf16[96,768]{1,0:T(8,128)(2,1)S(1)} %collective-permute-done.24), channel_id=1, source_target_pairs={{0,8},{1,9},{2,10},{3,11},{4,12},{5,13},{6,14},{7,15},{8,16},{9,17... | collective-permute-start | bytes 442376 | tf_op jit(solution)/shard_map/ppermute | solution.py:585
  24.5 14.2 %collective-permute-start.19 = (bf16[96,768]{1,0:T(8,128)(2,1)S(1)}, bf16[96,768]{1,0:T(8,128)(2,1)S(1)}, u32[]{:S(2)}, u32[]{:S(2)}) collective-permute-start(bf16[96,768]{1,0:T(8,128)(2,1)S(1)} %collective-permute-done.18), channel_id=1, source_target_pairs={{0,8},{1,9},{2,10},{3,11},{4,12},{5,13},{6,14},{7,15},{8,16},{9,17... | collective-permute-start | bytes 442376 | tf_op jit(solution)/shard_map/ppermute | solution.py:585
  29.3 12.4 %collective-permute-start.14 = (bf16[176,384]{1,0:T(8,128)(2,1)S(1)}, bf16[176,384]{1,0:T(8,128)(2,1)S(1)}, u32[]{:S(2)}, u32[]{:S(2)}) collective-permute-start(bf16[176,384]{1,0:T(8,128)(2,1)S(1)} %collective-permute-done.13), channel_id=1, source_target_pairs={{0,8},{1,9},{2,10},{3,11},{4,12},{5,13},{6,14},{7,15},{8,16},{9,17... | collective-permute-start | bytes 405512 | tf_op jit(solution)/shard_map/ppermute | solution.py:585
  32.4 12.4 %collective-permute-start.2 = (bf16[96,768]{1,0:T(8,128)(2,1)S(1)}, bf16[96,768]{1,0:T(8,128)(2,1)S(1)}, u32[]{:S(2)}, u32[]{:S(2)}) collective-permute-start(bf16[96,768]{1,0:T(8,128)(2,1)S(1)} %collective-permute-done.1), channel_id=1, source_target_pairs={{0,8},{1,9},{2,10},{3,11},{4,12},{5,13},{6,14},{7,15},{8,16},{9,17... | collective-permute-start | bytes 442376 | tf_op jit(solution)/shard_map/ppermute | solution.py:585
  35.6 12.4 %collective-permute-start.26 = (bf16[96,768]{1,0:T(8,128)(2,1)S(1)}, bf16[96,768]{1,0:T(8,128)(2,1)S(1)}, u32[]{:S(2)}, u32[]{:S(2)}) collective-permute-start(bf16[96,768]{1,0:T(8,128)(2,1)S(1)} %collective-permute-done.25), channel_id=1, source_target_pairs={{0,8},{1,9},{2,10},{3,11},{4,12},{5,13},{6,14},{7,15},{8,16},{9,17... | collective-permute-start | bytes 442376 | tf_op jit(solution)/shard_map/ppermute | solution.py:585
  38.8 11.3 %collective-permute-start.20 = (bf16[96,768]{1,0:T(8,128)(2,1)S(1)}, bf16[96,768]{1,0:T(8,128)(2,1)S(1)}, u32[]{:S(2)}, u32[]{:S(2)}) collective-permute-start(bf16[96,768]{1,0:T(8,128)(2,1)S(1)} %collective-permute-done.19), channel_id=1, source_target_pairs={{0,8},{1,9},{2,10},{3,11},{4,12},{5,13},{6,14},{7,15},{8,16},{9,17... | collective-permute-start | bytes 442376 | tf_op jit(solution)/shard_map/ppermute | solution.py:585
  41.8 15.3 %collective-permute-start.15 = (bf16[4,176,384]{2,1,0:T(8,128)(2,1)S(1)}, bf16[4,176,384]{2,1,0:T(8,128)(2,1)S(1)}, u32[]{:S(2)}, u32[]{:S(2)}) collective-permute-start(bf16[4,176,384]{2,1,0:T(8,128)(2,1)S(1)} %pad_maximum_fusion.7), channel_id=1, source_target_pairs={{0,4},{1,5},{2,6},{3,7},{4,0},{5,1},{6,2},{7,3},{8,12},{9,13},{10,... | collective-permute-start | bytes 1622024 | tf_op jit(solution)/shard_map/ppermute | solution.py:572
  44.9 16.3 %collective-permute-start.3 = (bf16[4,96,768]{2,1,0:T(8,128)(2,1)S(1)}, bf16[4,96,768]{2,1,0:T(8,128)(2,1)S(1)}, u32[]{:S(2)}, u32[]{:S(2)}) collective-permute-start(bf16[4,96,768]{2,1,0:T(8,128)(2,1)S(1)} %pad_maximum_fusion.2), channel_id=1, source_target_pairs={{0,2},{1,3},{2,0},{3,1},{4,6},{5,7},{6,4},{7,5},{8,10},{9,11},{10,... | collective-permute-start | bytes 1769480 | tf_op jit(solution)/shard_map/ppermute | solution.py:572
  48.1 21.6 %collective-permute-start.27 = (bf16[4,96,768]{2,1,0:T(8,128)(2,1)S(1)}, bf16[4,96,768]{2,1,0:T(8,128)(2,1)S(1)}, u32[]{:S(2)}, u32[]{:S(2)}) collective-permute-start(bf16[4,96,768]{2,1,0:T(8,128)(2,1)S(1)} %pad_maximum_fusion.4), channel_id=1, source_target_pairs={{0,4},{1,5},{2,6},{3,7},{4,0},{5,1},{6,2},{7,3},{8,12},{9,13},{10,... | collective-permute-start | bytes 1769480 | tf_op jit(solution)/shard_map/ppermute | solution.py:572
  50.1 23.8 %collective-permute-start.21 = (bf16[4,96,768]{2,1,0:T(8,128)(2,1)S(1)}, bf16[4,96,768]{2,1,0:T(8,128)(2,1)S(1)}, u32[]{:S(2)}, u32[]{:S(2)}) collective-permute-start(bf16[4,96,768]{2,1,0:T(8,128)(2,1)S(1)} %pad_maximum_fusion.3), channel_id=1, source_target_pairs={{0,2},{1,3},{2,0},{3,1},{4,6},{5,7},{6,4},{7,5},{8,10},{9,11},{10,... | collective-permute-start | bytes 1769480 | tf_op jit(solution)/shard_map/ppermute | solution.py:572
  57.9 39.1 %collective-permute-start.16 = (bf16[8,176,384]{2,1,0:T(8,128)(2,1)S(1)}, bf16[8,176,384]{2,1,0:T(8,128)(2,1)S(1)}, u32[]{:S(2)}, u32[]{:S(2)}) collective-permute-start(bf16[8,176,384]{2,1,0:T(8,128)(2,1)S(1)} %get-tuple-element.194), channel_id=1, source_target_pairs={{0,2},{1,3},{2,0},{3,1},{4,6},{5,7},{6,4},{7,5},{8,10},{9,11},{10,... | collective-permute-start | bytes 3244040 | tf_op jit(solution)/shard_map/ppermute | solution.py:572
  62.1 37.7 %collective-permute-start.4 = (bf16[8,96,768]{2,1,0:T(8,128)(2,1)S(1)}, bf16[8,96,768]{2,1,0:T(8,128)(2,1)S(1)}, u32[]{:S(2)}, u32[]{:S(2)}) collective-permute-start(bf16[8,96,768]{2,1,0:T(8,128)(2,1)S(1)} %get-tuple-element.192), channel_id=1, source_target_pairs={{0,4},{1,5},{2,6},{3,7},{4,0},{5,1},{6,2},{7,3},{8,12},{9,13},{10,... | collective-permute-start | bytes 3538952 | tf_op jit(solution)/shard_map/ppermute | solution.py:572
  70.6 55.7 %collective-permute-start.28 = (bf16[8,96,768]{2,1,0:T(8,128)(2,1)S(1)}, bf16[8,96,768]{2,1,0:T(8,128)(2,1)S(1)}, u32[]{:S(2)}, u32[]{:S(2)}) collective-permute-start(bf16[8,96,768]{2,1,0:T(8,128)(2,1)S(1)} %get-tuple-element.188), channel_id=1, source_target_pairs={{0,2},{1,3},{2,0},{3,1},{4,6},{5,7},{6,4},{7,5},{8,10},{9,11},{10,... | collective-permute-start | bytes 3538952 | tf_op jit(solution)/shard_map/ppermute | solution.py:572
  74.8 52.6 %collective-permute-start.22 = (bf16[8,96,768]{2,1,0:T(8,128)(2,1)S(1)}, bf16[8,96,768]{2,1,0:T(8,128)(2,1)S(1)}, u32[]{:S(2)}, u32[]{:S(2)}) collective-permute-start(bf16[8,96,768]{2,1,0:T(8,128)(2,1)S(1)} %get-tuple-element.190), channel_id=1, source_target_pairs={{0,4},{1,5},{2,6},{3,7},{4,0},{5,1},{6,2},{7,3},{8,12},{9,13},{10,... | collective-permute-start | bytes 3538952 | tf_op jit(solution)/shard_map/ppermute | solution.py:572
  76.3 21.9 %collective-permute-start.8 = (bf16[56,768]{1,0:T(8,128)(2,1)S(1)}, bf16[56,768]{1,0:T(8,128)(2,1)S(1)}, u32[]{:S(2)}, u32[]{:S(2)}) collective-permute-start(bf16[56,768]{1,0:T(8,128)(2,1)S(1)} %collective-permute-done.7), channel_id=1, source_target_pairs={{0,8},{1,9},{2,10},{3,11},{4,12},{5,13},{6,14},{7,15},{8,16},{9,17... | collective-permute-start | bytes 258056 | tf_op jit(solution)/shard_map/ppermute | solution.py:585
  98.2 68.0 %collective-permute-start.17 = (bf16[16,176,384]{2,1,0:T(8,128)(2,1)}, bf16[16,176,384]{2,1,0:T(8,128)(2,1)}, u32[]{:S(2)}, u32[]{:S(2)}) collective-permute-start(bf16[16,176,384]{2,1,0:T(8,128)(2,1)} %constant_dynamic-update-slice_fusion.27.image_own), channel_id=1, source_target_pairs={{0,1},{1,0},{2,3},{3,2},{4,5},{5,4},{6,7},{7,6},{8,9},{9,8},{10,11... | collective-permute-start | bytes 6488072 | tf_op jit(solution)/shard_map/ppermute | solution.py:572
  98.3 26.4 %collective-permute-start.9 = (bf16[4,56,768]{2,1,0:T(8,128)(2,1)S(1)}, bf16[4,56,768]{2,1,0:T(8,128)(2,1)S(1)}, u32[]{:S(2)}, u32[]{:S(2)}) collective-permute-start(bf16[4,56,768]{2,1,0:T(8,128)(2,1)S(1)} %pad_maximum_fusion.12), channel_id=1, source_target_pairs={{0,4},{1,5},{2,6},{3,7},{4,0},{5,1},{6,2},{7,3},{8,12},{9,13},{10,... | collective-permute-start | bytes 1032200 | tf_op jit(solution)/shard_map/ppermute | solution.py:572
  101.0 82.0 %collective-permute-start.5 = (bf16[16,96,768]{2,1,0:T(8,128)(2,1)}, bf16[16,96,768]{2,1,0:T(8,128)(2,1)}, u32[]{:S(2)}, u32[]{:S(2)}) collective-permute-start(bf16[16,96,768]{2,1,0:T(8,128)(2,1)} %constant_dynamic-update-slice_fusion.5.in_own), channel_id=1, source_target_pairs={{0,1},{1,0},{2,3},{3,2},{4,5},{5,4},{6,7},{7,6},{8,9},{9,8},{10,11... | collective-permute-start | bytes 7077896 | tf_op jit(solution)/shard_map/ppermute | solution.py:572
  124.7 14.5 %collective-permute-start.10 = (bf16[8,56,768]{2,1,0:T(8,128)(2,1)S(1)}, bf16[8,56,768]{2,1,0:T(8,128)(2,1)S(1)}, u32[]{:S(2)}, u32[]{:S(2)}) collective-permute-start(bf16[8,56,768]{2,1,0:T(8,128)(2,1)S(1)} %get-tuple-element.206), channel_id=1, source_target_pairs={{0,2},{1,3},{2,0},{3,1},{4,6},{5,7},{6,4},{7,5},{8,10},{9,11},{10,... | collective-permute-start | bytes 2064392 | tf_op jit(solution)/shard_map/ppermute | solution.py:572
  127.4 89.8 %collective-permute-start.29 = (bf16[16,96,768]{2,1,0:T(8,128)(2,1)}, bf16[16,96,768]{2,1,0:T(8,128)(2,1)}, u32[]{:S(2)}, u32[]{:S(2)}) collective-permute-start(bf16[16,96,768]{2,1,0:T(8,128)(2,1)} %constant_dynamic-update-slice_fusion.49.down_own), channel_id=1, source_target_pairs={{0,1},{1,0},{2,3},{3,2},{4,5},{5,4},{6,7},{7,6},{8,9},{9,8},{10,11... | collective-permute-start | bytes 7077896 | tf_op jit(solution)/shard_map/ppermute | solution.py:572
  128.5 88.7 %collective-permute-start.23 = (bf16[16,96,768]{2,1,0:T(8,128)(2,1)}, bf16[16,96,768]{2,1,0:T(8,128)(2,1)}, u32[]{:S(2)}, u32[]{:S(2)}) collective-permute-start(bf16[16,96,768]{2,1,0:T(8,128)(2,1)} %constant_dynamic-update-slice_fusion.38.up_own), channel_id=1, source_target_pairs={{0,1},{1,0},{2,3},{3,2},{4,5},{5,4},{6,7},{7,6},{8,9},{9,8},{10,11... | collective-permute-start | bytes 7077896 | tf_op jit(solution)/shard_map/ppermute | solution.py:572
  139.3 43.7 %collective-permute-start.11 = (bf16[16,56,768]{2,1,0:T(8,128)(2,1)S(1)}, bf16[16,56,768]{2,1,0:T(8,128)(2,1)}, u32[]{:S(2)}, u32[]{:S(2)}) collective-permute-start(bf16[16,56,768]{2,1,0:T(8,128)(2,1)S(1)} %constant_dynamic-update-slice_fusion.16.out_own), channel_id=1, source_target_pairs={{0,1},{1,0},{2,3},{3,2},{4,5},{5,4},{6,7},{7,6},{8,9},{9,8},{10,11... | collective-permute-start | bytes 4128776 | tf_op jit(solution)/shard_map/ppermute | solution.py:572
  296.1 26.0 %collective-permute-start.36 = (bf16[16,56,768]{2,1,0:T(8,128)(2,1)}, bf16[16,56,768]{2,1,0:T(8,128)(2,1)}, u32[]{:S(2)}, u32[]{:S(2)}) collective-permute-start(bf16[16,56,768]{2,1,0:T(8,128)(2,1)} %get-tuple-element.74), channel_id=1, source_target_pairs={{0,1},{1,0},{2,3},{3,2},{4,5},{5,4},{6,7},{7,6},{8,9},{9,8},{10,11... | collective-permute-start | bytes 4128776 | tf_op jit(solution)/shard_map/ppermute | solution.py:572
  321.5 22.4 %collective-permute-start.42 = (bf16[16,176,384]{2,1,0:T(8,128)(2,1)}, bf16[16,176,384]{2,1,0:T(8,128)(2,1)S(1)}, u32[]{:S(2)}, u32[]{:S(2)}) collective-permute-start(bf16[16,176,384]{2,1,0:T(8,128)(2,1)} %get-tuple-element.77), channel_id=1, source_target_pairs={{0,1},{1,0},{2,3},{3,2},{4,5},{5,4},{6,7},{7,6},{8,9},{9,8},{10,11... | collective-permute-start | bytes 6488072 | tf_op jit(solution)/shard_map/ppermute | solution.py:572
  321.8 30.1 %collective-permute-start.54 = (bf16[16,96,768]{2,1,0:T(8,128)(2,1)}, bf16[16,96,768]{2,1,0:T(8,128)(2,1)S(1)}, u32[]{:S(2)}, u32[]{:S(2)}) collective-permute-start(bf16[16,96,768]{2,1,0:T(8,128)(2,1)} %get-tuple-element.81), channel_id=1, source_target_pairs={{0,1},{1,0},{2,3},{3,2},{4,5},{5,4},{6,7},{7,6},{8,9},{9,8},{10,11... | collective-permute-start | bytes 7077896 | tf_op jit(solution)/shard_map/ppermute | solution.py:572
  324.0 17.7 %collective-permute-start.37 = (bf16[8,56,768]{2,1,0:T(8,128)(2,1)S(1)}, bf16[8,56,768]{2,1,0:T(8,128)(2,1)S(1)}, u32[]{:S(2)}, u32[]{:S(2)}) collective-permute-start(bf16[8,56,768]{2,1,0:T(8,128)(2,1)S(1)} %slice.331), channel_id=1, source_target_pairs={{0,2},{1,3},{2,0},{3,1},{4,6},{5,7},{6,4},{7,5},{8,10},{9,11},{10,... | collective-permute-start | bytes 2064392 | tf_op jit(solution)/shard_map/ppermute | solution.py:572
  325.6 32.6 %collective-permute-start.48 = (bf16[16,96,768]{2,1,0:T(8,128)(2,1)S(1)}, bf16[16,96,768]{2,1,0:T(8,128)(2,1)S(1)}, u32[]{:S(2)}, u32[]{:S(2)}) collective-permute-start(bf16[16,96,768]{2,1,0:T(8,128)(2,1)S(1)} %copy-done.27), channel_id=1, source_target_pairs={{0,1},{1,0},{2,3},{3,2},{4,5},{5,4},{6,7},{7,6},{8,9},{9,8},{10,11... | collective-permute-start | bytes 7077896 | tf_op jit(solution)/shard_map/ppermute | solution.py:572
  325.7 39.0 %collective-permute-start.30 = (bf16[16,96,768]{2,1,0:T(8,128)(2,1)S(1)}, bf16[16,96,768]{2,1,0:T(8,128)(2,1)S(1)}, u32[]{:S(2)}, u32[]{:S(2)}) collective-permute-start(bf16[16,96,768]{2,1,0:T(8,128)(2,1)S(1)} %copy-done.28), channel_id=1, source_target_pairs={{0,1},{1,0},{2,3},{3,2},{4,5},{5,4},{6,7},{7,6},{8,9},{9,8},{10,11... | collective-permute-start | bytes 7077896 | tf_op jit(solution)/shard_map/ppermute | solution.py:572
  344.6 28.0 %collective-permute-start.43 = (bf16[8,176,384]{2,1,0:T(8,128)(2,1)S(1)}, bf16[8,176,384]{2,1,0:T(8,128)(2,1)S(1)}, u32[]{:S(2)}, u32[]{:S(2)}) collective-permute-start(bf16[8,176,384]{2,1,0:T(8,128)(2,1)S(1)} %slice.341), channel_id=1, source_target_pairs={{0,2},{1,3},{2,0},{3,1},{4,6},{5,7},{6,4},{7,5},{8,10},{9,11},{10,... | collective-permute-start | bytes 3244040 | tf_op jit(solution)/shard_map/ppermute | solution.py:572
  352.7 42.1 %collective-permute-start.55 = (bf16[8,96,768]{2,1,0:T(8,128)(2,1)S(1)}, bf16[8,96,768]{2,1,0:T(8,128)(2,1)S(1)}, u32[]{:S(2)}, u32[]{:S(2)}) collective-permute-start(bf16[8,96,768]{2,1,0:T(8,128)(2,1)S(1)} %slice.359), channel_id=1, source_target_pairs={{0,2},{1,3},{2,0},{3,1},{4,6},{5,7},{6,4},{7,5},{8,10},{9,11},{10,... | collective-permute-start | bytes 3538952 | tf_op jit(solution)/shard_map/ppermute | solution.py:572
  359.1 66.1 %collective-permute-start.49 = (bf16[8,96,768]{2,1,0:T(8,128)(2,1)S(1)}, bf16[8,96,768]{2,1,0:T(8,128)(2,1)S(1)}, u32[]{:S(2)}, u32[]{:S(2)}) collective-permute-start(bf16[8,96,768]{2,1,0:T(8,128)(2,1)S(1)} %slice.351), channel_id=1, source_target_pairs={{0,4},{1,5},{2,6},{3,7},{4,0},{5,1},{6,2},{7,3},{8,12},{9,13},{10,... | collective-permute-start | bytes 3538952 | tf_op jit(solution)/shard_map/ppermute | solution.py:572
  365.5 66.6 %collective-permute-start.31 = (bf16[8,96,768]{2,1,0:T(8,128)(2,1)S(1)}, bf16[8,96,768]{2,1,0:T(8,128)(2,1)S(1)}, u32[]{:S(2)}, u32[]{:S(2)}) collective-permute-start(bf16[8,96,768]{2,1,0:T(8,128)(2,1)S(1)} %slice.319), channel_id=1, source_target_pairs={{0,4},{1,5},{2,6},{3,7},{4,0},{5,1},{6,2},{7,3},{8,12},{9,13},{10,... | collective-permute-start | bytes 3538952 | tf_op jit(solution)/shard_map/ppermute | solution.py:572
  372.9 52.0 %collective-permute-start.44 = (bf16[4,176,384]{2,1,0:T(8,128)(2,1)S(1)}, bf16[4,176,384]{2,1,0:T(8,128)(2,1)S(1)}, u32[]{:S(2)}, u32[]{:S(2)}) collective-permute-start(bf16[4,176,384]{2,1,0:T(8,128)(2,1)S(1)} %slice.343), channel_id=1, source_target_pairs={{0,4},{1,5},{2,6},{3,7},{4,0},{5,1},{6,2},{7,3},{8,12},{9,13},{10,... | collective-permute-start | bytes 1622024 | tf_op jit(solution)/shard_map/ppermute | solution.py:572
  395.2 45.3 %collective-permute-start.56 = (bf16[4,96,768]{2,1,0:T(8,128)(2,1)S(1)}, bf16[4,96,768]{2,1,0:T(8,128)(2,1)S(1)}, u32[]{:S(2)}, u32[]{:S(2)}) collective-permute-start(bf16[4,96,768]{2,1,0:T(8,128)(2,1)S(1)} %slice.361), channel_id=1, source_target_pairs={{0,4},{1,5},{2,6},{3,7},{4,0},{5,1},{6,2},{7,3},{8,12},{9,13},{10,... | collective-permute-start | bytes 1769480 | tf_op jit(solution)/shard_map/ppermute | solution.py:572
  425.5 15.2 %collective-permute-start.50 = (bf16[4,96,768]{2,1,0:T(8,128)(2,1)S(1)}, bf16[4,96,768]{2,1,0:T(8,128)(2,1)S(1)}, u32[]{:S(2)}, u32[]{:S(2)}) collective-permute-start(bf16[4,96,768]{2,1,0:T(8,128)(2,1)S(1)} %slice.353), channel_id=1, source_target_pairs={{0,2},{1,3},{2,0},{3,1},{4,6},{5,7},{6,4},{7,5},{8,10},{9,11},{10,... | collective-permute-start | bytes 1769480 | tf_op jit(solution)/shard_map/ppermute | solution.py:572
  432.4 14.4 %collective-permute-start.32 = (bf16[4,96,768]{2,1,0:T(8,128)(2,1)S(1)}, bf16[4,96,768]{2,1,0:T(8,128)(2,1)S(1)}, u32[]{:S(2)}, u32[]{:S(2)}) collective-permute-start(bf16[4,96,768]{2,1,0:T(8,128)(2,1)S(1)} %slice.321), channel_id=1, source_target_pairs={{0,2},{1,3},{2,0},{3,1},{4,6},{5,7},{6,4},{7,5},{8,10},{9,11},{10,... | collective-permute-start | bytes 1769480 | tf_op jit(solution)/shard_map/ppermute | solution.py:572
  440.6 10.4 %collective-permute-start.57 = (bf16[96,768]{1,0:T(8,128)(2,1)S(1)}, bf16[96,768]{1,0:T(8,128)(2,1)S(1)}, u32[]{:S(2)}, u32[]{:S(2)}) collective-permute-start(bf16[96,768]{1,0:T(8,128)(2,1)S(1)} %slice_bitcast_fusion.4), channel_id=1, source_target_pairs={{0,8},{1,9},{2,10},{3,11},{4,12},{5,13},{6,14},{7,15},{8,16},{9,17... | collective-permute-start | bytes 442376 | tf_op jit(solution)/shard_map/ppermute | solution.py:585
  440.9 13.3 %collective-permute-start.51 = (bf16[96,768]{1,0:T(8,128)(2,1)S(1)}, bf16[96,768]{1,0:T(8,128)(2,1)S(1)}, u32[]{:S(2)}, u32[]{:S(2)}) collective-permute-start(bf16[96,768]{1,0:T(8,128)(2,1)S(1)} %slice_bitcast_fusion.8), channel_id=1, source_target_pairs={{0,8},{1,9},{2,10},{3,11},{4,12},{5,13},{6,14},{7,15},{8,16},{9,17... | collective-permute-start | bytes 442376 | tf_op jit(solution)/shard_map/ppermute | solution.py:585
  447.1 10.3 %collective-permute-start.33 = (bf16[96,768]{1,0:T(8,128)(2,1)S(1)}, bf16[96,768]{1,0:T(8,128)(2,1)S(1)}, u32[]{:S(2)}, u32[]{:S(2)}) collective-permute-start(bf16[96,768]{1,0:T(8,128)(2,1)S(1)} %slice_bitcast_fusion.12), channel_id=1, source_target_pairs={{0,8},{1,9},{2,10},{3,11},{4,12},{5,13},{6,14},{7,15},{8,16},{9,17... | collective-permute-start | bytes 442376 | tf_op jit(solution)/shard_map/ppermute | solution.py:585
  454.2 11.9 %collective-permute-start.52 = (bf16[96,768]{1,0:T(8,128)(2,1)S(1)}, bf16[96,768]{1,0:T(8,128)(2,1)S(1)}, u32[]{:S(2)}, u32[]{:S(2)}) collective-permute-start(bf16[96,768]{1,0:T(8,128)(2,1)S(1)} %fusion.20), channel_id=1, source_target_pairs={{0,8},{1,9},{2,10},{3,11},{4,12},{5,13},{6,14},{7,15},{8,16},{9,17... | collective-permute-start | bytes 442376 | tf_op jit(solution)/shard_map/ppermute | solution.py:585
  460.0 14.0 %collective-permute-start.59 = (bf16[96,768]{1,0:T(8,128)(2,1)S(1)}, bf16[96,768]{1,0:T(8,128)(2,1)S(1)}, u32[]{:S(2)}, u32[]{:S(2)}) collective-permute-start(bf16[96,768]{1,0:T(8,128)(2,1)S(1)} %fusion.19), channel_id=1, source_target_pairs={{0,8},{1,9},{2,10},{3,11},{4,12},{5,13},{6,14},{7,15},{8,16},{9,17... | collective-permute-start | bytes 442376 | tf_op jit(solution)/shard_map/ppermute | solution.py:585
  481.7 10.2 %all-to-all-start = ((f32[32,2,16]{2,1,0:T(2,128)}), f32[32,2,16]{2,1,0:T(2,128)S(1)}, u32[]{:S(2)}, u32[]{:S(2)}) async-start(f32[32,2,16]{2,1,0:T(2,128)} %broadcast_in_dim.30), calls=%async_computation | async-start | bytes 65536 | tf_op jit(solution)/shard_map/all_to_all | solution.py:927
  (43 other events, 329.3 us)

commit v2 on v1

--- a/solution.py
+++ b/solution.py
@@ -30,7 +30,7 @@
 NORM_ROWS = 8
 BLOCK = 256
 WIDE = 256
-VMEM_LIMIT = 60 * 1024 * 1024
+MIB = 1024 * 1024
 
 BF16 = jnp.bfloat16
 F32 = jnp.float32
@@ -67,12 +67,8 @@
     return inverse * (scaled - centre_term - normed * normed_term)
 
 
-def slot_x(place, block, y_rel):
+def slot_of(place, block, y_rel):
     return place[block] * 8 + y_rel * 4 + place[GROUPS + block]
-
-
-def slot_y(place, block, y_rel):
-    return y_rel * 8 + place[block] * 4 + place[GROUPS + block]
 
 
 def softmax(scores):
@@ -96,10 +92,8 @@
     place,
     lengths,
     hidden,
-    in_own,
-    in_other,
-    out_own,
-    out_other,
+    begin_own,
+    begin_other,
     first_in,
     qkv,
     heads,
@@ -115,17 +109,24 @@
     width = features // MODEL
     block_rows = features // GROUPS
     out_rows = width // GROUPS
+    half, part = block_rows // 2, begin_own.shape[1] // 2
     norm_sum = jnp.zeros((NORM_ROWS, features), F32)
     for block in range(GROUPS):
         pieces = []
         for model in range(MODEL):
             side, y_rel = divmod(model, 2)
-            pieces.append((in_own, in_other)[side][slot_x(place, block, y_rel)])
-            out_piece = (out_own, out_other)[side][slot_y(place, block, y_rel)].astype(F32)
+            source, slot = (begin_own, begin_other)[side], slot_of(place, block, y_rel)
+            pieces.append(
+                jnp.concatenate(
+                    [source[slot, :half, :], source[slot, part : part + half, :]], axis=0
+                )
+            )
+            cross_part = source[slot, half:part, :].astype(F32)
+            self_part = source[slot, part + half :, :].astype(F32)
             begin = model * width + block * out_rows
-            self_rows[begin : begin + out_rows, :] = out_piece[:out_rows]
-            cross_rows[begin : begin + out_rows, :] = out_piece[out_rows : 2 * out_rows]
-            norm_sum = norm_sum + out_piece[2 * out_rows :]
+            cross_rows[begin : begin + out_rows, :] = cross_part[:out_rows]
+            self_rows[begin : begin + out_rows, :] = self_part[:out_rows]
+            norm_sum = norm_sum + self_part[out_rows:]
         begin = block * block_rows
         for kind in range(4):
             joined = jnp.concatenate(
@@ -167,7 +168,7 @@
         pieces = []
         for model in range(MODEL):
             side, y_rel = divmod(model, 2)
-            pieces.append((image_own, image_other)[side][slot_y(place, block, y_rel)])
+            pieces.append((image_own, image_other)[side][slot_of(place, block, y_rel)])
         begin = block * block_rows
         for kind in range(2):
             weight[begin : begin + block_rows, kind * features : (kind + 1) * features] = (
@@ -248,16 +249,12 @@
     second_in,
     norm,
     out_grad,
-    up_own,
-    up_other,
-    down_own,
-    down_other,
+    feed_own,
+    feed_other,
     block_out,
     two_grad,
-    up_keep,
-    up_send,
-    down_keep,
-    down_send,
+    feed_keep,
+    feed_send,
     norm_grads,
     w_up,
     w_down,
@@ -267,20 +264,18 @@
 ):
     rows, features = first_in.shape
     items = rows // SEQ
-    hidden_width = up_own.shape[2]
-    up_rows = up_own.shape[1]
-    down_rows = down_own.shape[1]
+    hidden_width = feed_own.shape[2]
+    up_rows = down_rows = feed_own.shape[1] // 2
     for block in range(GROUPS):
         for model in range(MODEL):
             side, y_rel = divmod(model, 2)
+            source, slot = (feed_own, feed_other)[side], slot_of(place, block, y_rel)
             w_up[
                 block * up_rows : (block + 1) * up_rows,
                 model * hidden_width : (model + 1) * hidden_width,
-            ] = (up_own, up_other)[side][slot_x(place, block, y_rel)]
+            ] = source[slot, :up_rows, :]
             begin = model * hidden_width + block * down_rows
-            w_down[begin : begin + down_rows, :] = (down_own, down_other)[side][
-                slot_y(place, block, y_rel)
-            ]
+            w_down[begin : begin + down_rows, :] = source[slot, up_rows:, :]
     normed_one, _ = normalise(first_in[...])
     after_one = normed_one * norm[0:1, :] + norm[1:2, :]
     normed_two, _ = normalise(second_in[...])
@@ -323,7 +318,7 @@
         columns = slice(model * hidden_width, (model + 1) * hidden_width)
         grad_down = dot_tn(active[:, columns], grad_rows).astype(BF16)
         for block in range(GROUPS):
-            (down_keep, down_send)[side][slot_y(place, block, y_rel)] = grad_down[
+            (feed_keep, feed_send)[side][slot_of(place, block, y_rel), up_rows:, :] = grad_down[
                 block * down_rows : (block + 1) * down_rows
             ]
         pre = pre_act[:, columns]
@@ -332,7 +327,7 @@
         grad_pre = (dot_nt(grad_rows, w_down[columns, :]) * slope_part).astype(BF16)
         grad_up = dot_tn(feed_in, grad_pre).astype(BF16)
         for block in range(GROUPS):
-            (up_keep, up_send)[side][slot_x(place, block, y_rel)] = grad_up[
+            (feed_keep, feed_send)[side][slot_of(place, block, y_rel), :up_rows, :] = grad_up[
                 block * up_rows : (block + 1) * up_rows
             ]
         two_grad[...] += dot_nt(grad_pre, w_up[:, columns])
@@ -398,10 +393,15 @@
     one_query_grad[...] = second_grad + dot_nt(query_grads[...], w_cross[...])
 
 
-def image_backward_kernel(place, feats, grad_key_values, image_keep, image_send, total):
-    block_rows = image_keep.shape[1]
-    width = image_keep.shape[2] // 2
-    features = width * MODEL
+def image_backward_kernel(
+    place, feats, grad_key_values, grad_cross, grad_cross_out, keep, send, total
+):
+    features = grad_cross.shape[1]
+    width = features // MODEL
+    image_rows = feats.shape[2] // GROUPS
+    half = image_rows // 2
+    block_rows = features // GROUPS
+    out_rows = width // GROUPS
 
     @pl.when(pl.program_id(0) == 0)
     def _():
@@ -412,17 +412,30 @@
     @pl.when(pl.program_id(0) == pl.num_programs(0) - 1)
     def _():
         for block in range(GROUPS):
-            span = slice(block * block_rows, (block + 1) * block_rows)
+            cross_rows = grad_cross[block * block_rows : (block + 1) * block_rows, :].astype(F32)
             for model in range(MODEL):
                 side, y_rel = divmod(model, 2)
-                piece = jnp.concatenate(
+                columns = slice(model * width, (model + 1) * width)
+                image_part = [
+                    total[begin : begin + half, kind + model * width : kind + (model + 1) * width]
+                    for begin in (block * image_rows, block * image_rows + half)
+                    for kind in (0, features)
+                ]
+                cross_part = [
+                    cross_rows[part * out_rows : (part + 1) * out_rows, columns]
+                    for part in range(MODEL)
+                ]
+                begin = model * width + (block // 2) * 2 * out_rows
+                out_part = grad_cross_out[begin : begin + 2 * out_rows, :].astype(F32)
+                begin = (block % 2) * out_rows
+                (keep, send)[side][slot_of(place, block, y_rel)] = jnp.concatenate(
                     [
-                        total[span, begin + model * width : begin + (model + 1) * width]
-                        for begin in (0, features)
+                        jnp.concatenate(image_part, axis=1),
+                        jnp.concatenate(cross_part, axis=1),
+                        out_part[begin : begin + out_rows],
                     ],
-                    axis=1,
-                )
-                (image_keep, image_send)[side][slot_y(place, block, y_rel)] = piece.astype(BF16)
+                    axis=0,
+                ).astype(BF16)
 
 
 def self_backward_kernel(
@@ -437,14 +450,10 @@
     heads,
     w_qkv,
     w_self_out,
-    grad_cross,
-    grad_cross_out,
     norm_grads_in,
     input_grad,
     in_keep,
     in_send,
-    out_keep,
-    out_send,
     one_grad,
     head_grads,
     grad_qkv,
@@ -504,41 +513,36 @@
         total = total + dot_nt(grad_qkv[:, columns], w_qkv[:, columns])
         grad_weights[:, columns] = dot_tn(tokens, grad_qkv[:, columns]).astype(BF16)
     input_grad[...] = total.astype(BF16)
+    grad_out = dot_tn(heads[...], grad_rows)
+    norm_rows = norm_total.astype(BF16)
     for block in range(GROUPS):
         span = slice(block * block_rows, (block + 1) * block_rows)
         for model in range(MODEL):
             side, y_rel = divmod(model, 2)
-            columns = slice(model * width, (model + 1) * width)
             piece = [
                 grad_weights[
                     span, kind * features + model * width : kind * features + (model + 1) * width
                 ]
                 for kind in range(3)
             ]
-            piece.append(grad_cross[span, columns])
-            (in_keep, in_send)[side][slot_x(place, block, y_rel)] = jnp.concatenate(piece, axis=1)
-    grad_self_out = dot_tn(heads[...], grad_rows)
-    grad_other_out = grad_cross_out[...].astype(F32)
-    for block in range(GROUPS):
-        for model in range(MODEL):
-            side, y_rel = divmod(model, 2)
             begin = model * width + block * out_rows
-            piece = jnp.concatenate(
-                [
-                    grad_self_out[begin : begin + out_rows],
-                    grad_other_out[begin : begin + out_rows],
-                    norm_total,
-                ],
-                axis=0,
+            out_part = grad_out[begin : begin + out_rows]
+            piece.append(
+                jnp.concatenate(
+                    [out_part[:, part * width : (part + 1) * width] for part in range(MODEL)],
+                    axis=0,
+                ).astype(BF16)
             )
-            (out_keep, out_send)[side][slot_y(place, block, y_rel)] = piece.astype(BF16)
+            target, slot = (in_keep, in_send)[side], slot_of(place, block, y_rel)
+            target[slot, :block_rows, :] = jnp.concatenate(piece, axis=1)
+            target[slot, block_rows:, :] = norm_rows
 
 
 SCALARS = pl.BlockSpec(memory_space=pltpu.SMEM)
 WHOLE = pl.BlockSpec(memory_space=pltpu.VMEM)
 
 
-def local_call(kernel, scalars, arrays, out_shapes, scratch, flops, name):
+def local_call(kernel, scalars, arrays, out_shapes, scratch, flops, name, limit):
     size = sum(a.size * a.dtype.itemsize for a in arrays)
     size += sum(a.size * a.dtype.itemsize for a in out_shapes)
     return pl.pallas_call(
@@ -547,7 +551,7 @@
         in_specs=[SCALARS] * len(scalars) + [WHOLE] * len(arrays),
         out_specs=tuple([WHOLE] * len(out_shapes)),
         scratch_shapes=scratch,
-        compiler_params=pltpu.CompilerParams(vmem_limit_bytes=VMEM_LIMIT),
+        compiler_params=pltpu.CompilerParams(vmem_limit_bytes=limit * MIB),
         cost_estimate=pl.CostEstimate(flops=flops, bytes_accessed=size, transcendentals=0),
         name=name,
     )(*scalars, *arrays)
@@ -580,28 +584,71 @@
     def hop_x(self, values):
         return self.hop(values, self.mp)
 
-    def hop_z(self, values):
-        step = 2 * self.mp
+    def hop_z(self, values, distance):
+        step = 2 * self.mp * distance
         return lax.ppermute(values, AXES, [(i, (i + step) % self.count) for i in range(self.count)])
 
-    def collect(self, piece, x_last):
-        ring = [piece]
-        for _ in range(self.depth - 1):
-            ring.append(self.hop_z(ring[-1]))
-        held = jnp.stack(ring)
-        for hop in (self.hop_y, self.hop_x) if x_last else (self.hop_x, self.hop_y):
-            held = jnp.concatenate([held, hop(held)])
-        return held, self.hop_core(held)
-
-    def scatter(self, keep, send, x_first):
-        total = add(keep, self.hop_core(send))
-        for hop in (self.hop_x, self.hop_y) if x_first else (self.hop_y, self.hop_x):
-            half = total.shape[0] // 2
-            total = add(total[:half], hop(total[half:]))
-        carried = self.hop_z(total[1])
-        for index in range(2, self.depth):
-            carried = self.hop_z(add(total[index], carried))
-        return total[0].astype(F32) + carried.astype(F32)
+    def spread_z(self, piece):
+        return jnp.stack([piece] + [self.hop_z(piece, step) for step in range(1, self.depth)])
+
+
+    def spread_first(self, held, split):
+        return self.hop_y(held[:, :split]), self.hop_x(held[:, split:])
+
+    def join_first(self, held, split, others):
+        return jnp.stack([held[:, :split], others[0]]), jnp.stack([held[:, split:], others[1]])
+
+    def spread_second(self, parts):
+        return self.hop_x(parts[0]), self.hop_y(parts[1])
+
+    def join_second(self, parts, others):
+        left = jnp.stack([parts[0], others[0]])
+        right = jnp.stack([parts[1], others[1]]).transpose(1, 0, 2, 3, 4)
+        whole = jnp.concatenate([left, right], axis=3)
+        return whole.reshape(SLOTS, *whole.shape[3:])
+
+
+    def fold_core(self, keep, send):
+        return [keep, self.hop_core(send)]
+
+    def fold_first(self, parts, split):
+        parts = [part.reshape(2, 2, 4, *part.shape[1:]) for part in parts]
+        left = [part[:, :, :, :split] for part in parts]
+        right = [part[:, :, :, split:] for part in parts]
+        return (
+            [part[0] for part in left] + [self.hop_x(total([part[1] for part in left]))],
+            [part[:, 0] for part in right] + [self.hop_y(total([part[:, 1] for part in right]))],
+        )
+
+    def fold_second(self, parts):
+        left, right = parts
+        left_other = self.hop_y(total([part[1] for part in left]))
+        right_other = self.hop_x(total([part[1] for part in right]))
+        return (
+            [part[0] for part in left] + [left_other],
+            [part[0] for part in right] + [right_other],
+        )
+
+    def fold_z(self, parts):
+        left, right = parts
+        parts = [
+            total([part[step] for part in left], [part[step] for part in right])
+            for step in range(self.depth)
+        ]
+        own = jnp.concatenate(
+            [total([part[0] for part in side], dtype=F32) for side in (left, right)], axis=0
+        )
+        return [own] + [self.hop_z(parts[step], -step) for step in range(1, self.depth)]
+
+
+def total(*sides, dtype=BF16):
+    sums = []
+    for parts in sides:
+        result = parts[0].astype(F32)
+        for part in parts[1:]:
+            result = result + part.astype(F32)
+        sums.append(result.astype(dtype))
+    return sums[0] if len(sums) == 1 else jnp.concatenate(sums, axis=0)
 
 
 class Plain:
@@ -611,28 +658,429 @@
         block = jnp.arange(GROUPS, dtype=jnp.int32)
         self.place = jnp.concatenate([block % 2, block // 2]).astype(jnp.int32)
 
-    def collect(self, piece, x_last):
+    def collect(self, piece):
         rows, width = piece.shape
         blocks = lax.all_gather(piece, AXES, axis=0).reshape(self.dp, self.mp, rows, width)
-        blocks = blocks.transpose(1, 0, 2, 3).reshape(2, 2, 4, 2, rows * self.dp // GROUPS, width)
-        order = (0, 3, 1, 2, 4, 5) if x_last else (0, 1, 3, 2, 4, 5)
-        blocks = blocks.transpose(order).reshape(2, SLOTS, rows * self.dp // GROUPS, width)
-        return blocks[0], blocks[1]
-
-    def scatter(self, keep, send, x_first):
-        _, rows, width = keep.shape
-        both = jnp.stack([keep, send])
-        if x_first:
-            both = both.reshape(2, 2, 2, 4, rows, width).transpose(0, 2, 3, 1, 4, 5)
-        else:
-            both = both.reshape(2, 2, 2, 4, rows, width).transpose(0, 1, 3, 2, 4, 5)
+        rows = rows * self.dp // GROUPS
+        blocks = blocks.transpose(1, 0, 2, 3).reshape(2, 2, 4, 2, rows, width)
+        blocks = blocks.transpose(0, 3, 1, 2, 4, 5).reshape(2, SLOTS, rows, width)
+        return blocks
+
+    def scatter(self, both):
+        rows, width = both.shape[2:]
+        both = both.reshape(2, 2, 2, 4, rows, width).transpose(0, 2, 3, 1, 4, 5)
         both = both.reshape(self.mp, self.dp, rows * GROUPS // self.dp, width)
         both = both.transpose(1, 0, 2, 3).reshape(-1, width)
         return lax.psum_scatter(both.astype(F32), AXES, scatter_dimension=0, tiled=True)
 
 
+def tie(*arrays):
+    return lax.optimization_barrier(arrays)
+
+
+def tie(*arrays):
+    return lax.optimization_barrier(arrays)
+
+
 def add(left_side, right_side):
     return (left_side.astype(F32) + right_side.astype(F32)).astype(BF16)
+
+
+def self_forward(place, lengths, hidden, begin):
+    rows, features = hidden.shape
+    return local_call(
+        self_forward_kernel,
+        (place, lengths),
+        (hidden, *begin),
+        (
+            shape_of(rows, features, dtype=F32),
+            shape_of(rows, 3 * features),
+            shape_of(rows, features),
+            shape_of(features, 3 * features),
+            shape_of(features, features),
+            shape_of(features, features),
+            shape_of(features, features),
+            shape_of(NORM_ROWS, features, dtype=F32),
+        ),
+        [pltpu.VMEM((features, features), F32), pltpu.VMEM((features, features), F32)],
+        10 * rows * features * features,
+        "self_forward",
+        30,
+    )
+
+
+def image_forward(place, feats, image):
+    items, patches, encoded = feats.shape
+    features = image[0].shape[2] // 2 * MODEL
+    piece_spec = pl.BlockSpec(image[0].shape, lambda item, where: (0, 0, 0))
+    return pl.pallas_call(
+        image_forward_kernel,
+        out_shape=shape_of(items, patches, 2 * features),
+        grid_spec=pltpu.PrefetchScalarGridSpec(
+            num_scalar_prefetch=1,
+            grid=(items,),
+            in_specs=[
+                pl.BlockSpec((1, patches, encoded), lambda item, where: (item, 0, 0)),
+                piece_spec,
+                piece_spec,
+            ],
+            out_specs=pl.BlockSpec((1, patches, 2 * features), lambda item, where: (item, 0, 0)),
+            scratch_shapes=[pltpu.VMEM((encoded, 2 * features), BF16)],
+        ),
+        compiler_params=pltpu.CompilerParams(vmem_limit_bytes=24 * MIB),
+        cost_estimate=image_cost(items, patches, encoded, features),
+        name="image_forward",
+    )(place, feats, *image)
+
+
+def image_cost(items, patches, encoded, features):
+    return pl.CostEstimate(
+        flops=4 * items * patches * encoded * features,
+        bytes_accessed=2 * items * patches * (encoded + 2 * features) + 4 * encoded * features,
+        transcendentals=0,
+    )
+
+
+def image_backward(place, feats, grad_key_values, grad_cross, grad_cross_out):
+    items, patches, encoded = feats.shape
+    features = grad_cross.shape[1]
+    rows = encoded // GROUPS // 2 + 2 * (features // MODEL // GROUPS)
+    piece = (SLOTS, rows, features)
+    square_spec = pl.BlockSpec((features, features), lambda item, where: (0, 0))
+    piece_spec = pl.BlockSpec(piece, lambda item, where: (0, 0, 0))
+    return pl.pallas_call(
+        image_backward_kernel,
+        out_shape=(shape_of(*piece), shape_of(*piece)),
+        grid_spec=pltpu.PrefetchScalarGridSpec(
+            num_scalar_prefetch=1,
+            grid=(items,),
+            in_specs=[
+                pl.BlockSpec((1, patches, encoded), lambda item, where: (item, 0, 0)),
+                pl.BlockSpec((1, patches, 2 * features), lambda item, where: (item, 0, 0)),
+                square_spec,
+                square_spec,
+            ],
+            out_specs=(piece_spec, piece_spec),
+            scratch_shapes=[pltpu.VMEM((encoded, 2 * features), F32)],
+        ),
+        compiler_params=pltpu.CompilerParams(vmem_limit_bytes=32 * MIB),
+        cost_estimate=image_cost(items, patches, encoded, features),
+        name="image_backward",
+    )(place, feats, grad_key_values, grad_cross, grad_cross_out)
+
+
+def cross_forward(first_in, norm, w_cross, w_cross_out, key_values):
+    features = first_in.shape[1]
+    queries = first_in.shape[0] // SEQ * QUERIES
+    return local_call(
+        cross_forward_kernel,
+        (),
+        (first_in, norm, w_cross, w_cross_out, key_values),
+        (
+            shape_of(queries, features, dtype=F32),
+            shape_of(queries, features),
+            shape_of(queries, features),
+        ),
+        [],
+        4 * queries * features * features,
+        "cross_forward",
+        18,
+    )
+
+
+def feed(place, lengths, first_in, second_in, norm, out_grad, weights):
+    rows, features = first_in.shape
+    hidden_width = weights[0].shape[2] * MODEL
+    return local_call(
+        feed_kernel,
+        (place, lengths),
+        (first_in, second_in, norm, out_grad, *weights),
+        (
+            shape_of(rows, features),
+            shape_of(rows, features, dtype=F32),
+            shape_of(*weights[0].shape),
+            shape_of(*weights[0].shape),
+            shape_of(NORM_ROWS, features, dtype=F32),
+        ),
+        [
+            pltpu.VMEM((features, hidden_width), BF16),
+            pltpu.VMEM((hidden_width, features), BF16),
+            pltpu.VMEM((rows, features), F32),
+            pltpu.VMEM((rows, hidden_width), F32),
+            pltpu.VMEM((rows, hidden_width), BF16),
+        ],
+        12 * rows * features * hidden_width,
+        "feed",
+        60,
+    )
+
+
+def cross_backward(two_grad, first_in, second_in, norm, w_cross, w_cross_out, queries, heads, key_values, norm_grads):
+    features = first_in.shape[1]
+    query_count = queries.shape[0]
+    return local_call(
+        cross_backward_kernel,
+        (),
+        (
+            two_grad,
+            first_in,
+            second_in,
+            norm,
+            w_cross,
+            w_cross_out,
+            queries,
+            heads,
+            key_values,
+            norm_grads,
+        ),
+        (
+            shape_of(*key_values.shape),
+            shape_of(features, features),
+            shape_of(features, features),
+            shape_of(query_count, features, dtype=F32),
+            shape_of(NORM_ROWS, features, dtype=F32),
+        ),
+        [pltpu.VMEM((query_count, features), BF16), pltpu.VMEM((query_count, features), BF16)],
+        8 * query_count * features * features,
+        "cross_backward",
+        28,
+    )
+
+
+def self_backward(place, lengths, one_query_grad, two_grad, first_in, norm, hidden, qkv, heads, w_qkv, w_self_out, norm_grads):
+    rows, features = hidden.shape
+    piece = (SLOTS, features // GROUPS + NORM_ROWS, features)
+    return local_call(
+        self_backward_kernel,
+        (place, lengths),
+        (
+            one_query_grad,
+            two_grad,
+            first_in,
+            norm,
+            hidden,
+            qkv,
+            heads,
+            w_qkv,
+            w_self_out,
+            norm_grads,
+        ),
+        (shape_of(rows, features), shape_of(*piece), shape_of(*piece)),
+        [
+            pltpu.VMEM((rows, features), F32),
+            pltpu.VMEM((rows, features), BF16),
+            pltpu.VMEM((rows, 3 * features), BF16),
+            pltpu.VMEM((features, 3 * features), BF16),
+        ],
+        20 * rows * features * features,
+        "self_backward",
+        34,
+    )
+
+
+def run_direct(hidden, feats, lengths, out_grad, image, begin, weights):
+    moves = Direct(lax.axis_size("dp"), lax.axis_size("mp"))
+    place = moves.place
+    begin_split = begin.shape[0] // 2
+    image_split = image.shape[0] * 96 // 176
+    feed_split = weights.shape[0] // 2
+
+    begin = moves.spread_z(begin)
+    begin, image = tie(begin, image)
+    begin_others = moves.spread_first(begin, begin_split)
+    image = moves.spread_z(image)
+    begin_others, image, weights = tie(begin_others, image, weights)
+    begin_parts = moves.join_first(begin, begin_split, begin_others)
+    begin_others = moves.spread_second(begin_parts)
+    image_others = moves.spread_first(image, image_split)
+    weights = moves.spread_z(weights)
+    begin_others, image_others, weights = tie(begin_others, image_others, weights)
+
+    image_parts = moves.join_first(image, image_split, image_others)
+    image_others = moves.spread_second(image_parts)
+    weight_others = moves.spread_first(weights, feed_split)
+    begin = moves.join_second(begin_parts, begin_others)
+    begin_other = moves.hop_core(begin)
+    first_in, qkv, heads, w_qkv, w_cross, w_self_out, w_cross_out, norm = self_forward(
+        place, lengths, hidden, (begin, begin_other)
+    )
+    first_in, image_others, weight_others = tie(first_in, image_others, weight_others)
+    image = moves.join_second(image_parts, image_others)
+    weight_parts = moves.join_first(weights, feed_split, weight_others)
+    image_other = moves.hop_core(image)
+    image_other, weight_parts, first_in = tie(image_other, weight_parts, first_in)
+    weight_others = moves.spread_second(weight_parts)
+    key_values = image_forward(place, feats, (image, image_other))
+    second_in, cross_queries, cross_heads = cross_forward(
+        first_in, norm, w_cross, w_cross_out, key_values
+    )
+    second_in, weight_others = tie(second_in, weight_others)
+    weights = moves.join_second(weight_parts, weight_others)
+    weights_other = moves.hop_core(weights)
+    block_out, two_grad, feed_keep, feed_send, norm_grads = feed(
+        place, lengths, first_in, second_in, norm, out_grad, (weights, weights_other)
+    )
+
+    feed_sums = moves.fold_core(feed_keep, feed_send)
+    grad_key_values, grad_cross, grad_cross_out, one_query_grad, norm_grads = cross_backward(
+        two_grad,
+        first_in,
+        second_in,
+        norm,
+        w_cross,
+        w_cross_out,
+        cross_queries,
+        cross_heads,
+        key_values,
+        norm_grads,
+    )
+    grad_key_values, feed_sums = tie(grad_key_values, feed_sums)
+    feed_sums = moves.fold_first(feed_sums, feed_split)
+    image_keep, image_send = image_backward(
+        place, feats, grad_key_values, grad_cross, grad_cross_out
+    )
+    one_query_grad, image_keep, image_send, feed_sums = tie(
+        one_query_grad, image_keep, image_send, feed_sums
+    )
+    image_sums = moves.fold_core(image_keep, image_send)
+    one_query_grad, image_sums = tie(one_query_grad, image_sums)
+    image_sums = moves.fold_first(image_sums, 64)
+    feed_sums = moves.fold_second(feed_sums)
+    input_grad, in_keep, in_send = self_backward(
+        place,
+        lengths,
+        one_query_grad,
+        two_grad,
+        first_in,
+        norm,
+        hidden,
+        qkv,
+        heads,
+        w_qkv,
+        w_self_out,
+        norm_grads,
+    )
+    in_keep, in_send, feed_sums, image_sums = tie(in_keep, in_send, feed_sums, image_sums)
+    in_sums = moves.fold_core(in_keep, in_send)
+    feed_sums = moves.fold_z(feed_sums)
+    image_sums = moves.fold_second(image_sums)
+    in_sums, image_sums = tie(in_sums, image_sums)
+    in_sums = moves.fold_first(in_sums, 48)
+    in_sums, feed_sums, image_sums = tie(in_sums, feed_sums, image_sums)
+    image_sums = moves.fold_z(image_sums)
+    in_sums = moves.fold_second(in_sums)
+    feed_sum = total(feed_sums, dtype=F32)
+    in_sums, image_sums = tie(in_sums, image_sums)
+    in_sum = total(moves.fold_z(in_sums), dtype=F32)
+    image_sum = total(image_sums, dtype=F32)
+    return block_out, input_grad, in_sum, image_sum, feed_sum
+
+
+def run_plain(hidden, feats, lengths, out_grad, image, begin, weights):
+    moves = Plain(lax.axis_size("dp"), lax.axis_size("mp"))
+    place = moves.place
+    features = hidden.shape[1]
+    width = features // MODEL
+    block_rows, out_rows = features // GROUPS, width // GROUPS
+    own_in, own_out = block_rows * GROUPS // moves.dp, out_rows * GROUPS // moves.dp
+    half = block_rows // 2
+    part = begin.shape[0] - NORM_ROWS
+    inward = moves.collect(begin[:own_in])
+    cross_out = moves.collect(begin[own_in : own_in + own_out])
+    self_out = moves.collect(begin[own_in + own_out : part])
+    norm_all = lax.psum(begin[part:].astype(F32), AXES).astype(BF16)
+    norm_first = jnp.zeros((2, SLOTS, NORM_ROWS, features), BF16).at[0, 0].set(norm_all)
+    begin = jnp.concatenate(
+        [
+            inward[:, :, :half],
+            cross_out,
+            jnp.zeros_like(norm_first),
+            inward[:, :, half:],
+            self_out,
+            norm_first,
+        ],
+        axis=2,
+    )
+    image = moves.collect(image)
+    own_up = weights.shape[0] // 2
+    weights = jnp.concatenate(
+        [moves.collect(weights[:own_up]), moves.collect(weights[own_up:])], axis=2
+    )
+    first_in, qkv, heads, w_qkv, w_cross, w_self_out, w_cross_out, norm = self_forward(
+        place, lengths, hidden, (begin[0], begin[1])
+    )
+    key_values = image_forward(place, feats, (image[0], image[1]))
+    second_in, cross_queries, cross_heads = cross_forward(
+        first_in, norm, w_cross, w_cross_out, key_values
+    )
+    block_out, two_grad, feed_keep, feed_send, norm_grads = feed(
+        place, lengths, first_in, second_in, norm, out_grad, (weights[0], weights[1])
+    )
+    grad_key_values, grad_cross, grad_cross_out, one_query_grad, norm_grads = cross_backward(
+        two_grad,
+        first_in,
+        second_in,
+        norm,
+        w_cross,
+        w_cross_out,
+        cross_queries,
+        cross_heads,
+        key_values,
+        norm_grads,
+    )
+    image_keep, image_send = image_backward(
+        place, feats, grad_key_values, grad_cross, grad_cross_out
+    )
+    input_grad, in_keep, in_send = self_backward(
+        place,
+        lengths,
+        one_query_grad,
+        two_grad,
+        first_in,
+        norm,
+        hidden,
+        qkv,
+        heads,
+        w_qkv,
+        w_self_out,
+        norm_grads,
+    )
+
+    def beside(values):
+        count = values.shape[-2] // MODEL
+        return jnp.concatenate(
+            [values[..., part * count : (part + 1) * count, :] for part in range(MODEL)], axis=-1
+        )
+
+    def below(values):
+        count = values.shape[-1] // MODEL
+        return jnp.concatenate(
+            [values[..., part * count : (part + 1) * count] for part in range(MODEL)], axis=-2
+        )
+
+    grads = jnp.stack([in_keep, in_send])
+    in_part = moves.scatter(grads[:, :, :block_rows, : 3 * width])
+    self_out = moves.scatter(beside(grads[:, :, :block_rows, 3 * width :]))
+    norm_sum = lax.psum(in_keep[0, block_rows:].astype(F32), AXES)
+    in_sum = jnp.concatenate([jnp.concatenate([in_part, below(self_out)], axis=1), norm_sum])
+    grads = jnp.stack([image_keep, image_send])
+    image_rows = grads.shape[2] - 2 * out_rows
+    image_part = grads[:, :, :image_rows]
+    image_part = jnp.concatenate(
+        [image_part[..., : features // 2], image_part[..., features // 2 :]], axis=2
+    )
+    image_part = moves.scatter(image_part)
+    image_half = image_part.shape[0] // 2
+    image_part = jnp.concatenate([image_part[:image_half], image_part[image_half:]], axis=1)
+    cross_query = moves.scatter(below(grads[:, :, image_rows : image_rows + out_rows]))
+    cross_out = moves.scatter(grads[:, :, image_rows + out_rows :])
+    image_sum = jnp.concatenate([image_part, beside(cross_query), cross_out])
+    grads = jnp.stack([feed_keep, feed_send])
+    feed_half = grads.shape[2] // 2
+    feed_sum = jnp.concatenate(
+        [moves.scatter(grads[:, :, :feed_half]), moves.scatter(grads[:, :, feed_half:])]
+    )
+    return block_out, input_grad, in_sum, image_sum, feed_sum
 
 
 def adam_step(weight, moments, gradient, decay_rate):
@@ -681,229 +1129,71 @@
     data_index, model_index = lax.axis_index("dp"), lax.axis_index("mp")
     rows, features = hidden_in.shape
     items = rows // SEQ
-    patches, encoded = image_feats.shape[1:]
-    hidden_width = feed_up.shape[1] * model_ways
     width = features // model_ways
     own_norm = norm_params.shape[1]
     norm_begin = (model_index * data_ways + data_index) * own_norm
-    direct = data_ways == GROUPS and model_ways == MODEL
-    moves = (Direct if direct else Plain)(data_ways, model_ways)
-    place = moves.place
     lengths = lax.dynamic_slice_in_dim(caption_lengths, model_index * items, items, 0)
-    first_item = (model_index * items).astype(jnp.int32)
-
+    feats = lax.dynamic_slice_in_dim(image_feats, model_index * items, items, 0)
     image_piece = jnp.concatenate([image_kv[0], image_kv[1]], axis=1).astype(BF16)
     in_piece = jnp.concatenate([proj_in[kind] for kind in range(4)], axis=1).astype(BF16)
+    out_pieces = [proj_out[kind].astype(BF16) for kind in range(2)]
+    feed_piece = jnp.concatenate([feed_up, feed_down], axis=0).astype(BF16)
     norm_rows = lax.dynamic_update_slice(
         jnp.zeros((NORM_ROWS, features), F32), norm_params, (0, norm_begin)
     ).astype(BF16)
-    in_own, in_other = moves.collect(in_piece, True)
+    own_in, own_out, own_image = proj_in.shape[1], proj_out.shape[1], image_kv.shape[1]
+    direct = data_ways == GROUPS and model_ways == MODEL
     if direct:
-        out_piece = jnp.concatenate(
-            [proj_out[0].astype(BF16), proj_out[1].astype(BF16), norm_rows], axis=0
+        run, half = run_direct, own_in // 2
+        begin_piece = jnp.concatenate(
+            [
+                in_piece[:half],
+                out_pieces[1],
+                jnp.zeros_like(norm_rows),
+                in_piece[half:],
+                out_pieces[0],
+                norm_rows,
+            ],
+            axis=0,
         )
-        out_own, out_other = moves.collect(out_piece, False)
     else:
-        parts = [moves.collect(proj_out[kind].astype(BF16), False) for kind in range(2)]
-        norm_all = lax.psum(norm_rows.astype(F32), AXES).astype(BF16)
-        norm_first = jnp.zeros((SLOTS, NORM_ROWS, features), BF16).at[0].set(norm_all)
-        out_own = jnp.concatenate([parts[0][0], parts[1][0], norm_first], axis=1)
-        out_other = jnp.concatenate(
-            [parts[0][1], parts[1][1], jnp.zeros_like(norm_first)], axis=1
+        run = run_plain
+        begin_piece = jnp.concatenate(
+            [in_piece, out_pieces[1], out_pieces[0], norm_rows], axis=0
         )
-    image_own, image_other = moves.collect(image_piece, False)
-    up_own, up_other = moves.collect(feed_up.astype(BF16), True)
-    down_own, down_other = moves.collect(feed_down.astype(BF16), False)
-
-    first_in, qkv, heads, w_qkv, w_cross, w_self_out, w_cross_out, norm = local_call(
-        self_forward_kernel,
-        (place, lengths),
-        (hidden_in, in_own, in_other, out_own, out_other),
-        (
-            shape_of(rows, features, dtype=F32),
-            shape_of(rows, 3 * features),
-            shape_of(rows, features),
-            shape_of(features, 3 * features),
-            shape_of(features, features),
-            shape_of(features, features),
-            shape_of(features, features),
-            shape_of(NORM_ROWS, features, dtype=F32),
-        ),
-        [pltpu.VMEM((features, features), F32), pltpu.VMEM((features, features), F32)],
-        10 * rows * features * features,
-        "self_forward",
-    )
-    image_place = jnp.concatenate([place, first_item[None]])
-    feats_spec = pl.BlockSpec(
-        (1, patches, encoded), lambda item, where: (where[2 * GROUPS] + item, 0, 0)
-    )
-    item_spec = pl.BlockSpec((1, patches, 2 * features), lambda item, where: (item, 0, 0))
-    piece_spec = pl.BlockSpec(image_own.shape, lambda item, where: (0, 0, 0))
-    image_cost = pl.CostEstimate(
-        flops=4 * items * patches * encoded * features,
-        bytes_accessed=2 * items * patches * (encoded + 2 * features) + 4 * encoded * features,
-        transcendentals=0,
-    )
-    key_values = pl.pallas_call(
-        image_forward_kernel,
-        out_shape=shape_of(items, patches, 2 * features),
-        grid_spec=pltpu.PrefetchScalarGridSpec(
-            num_scalar_prefetch=1,
-            grid=(items,),
-            in_specs=[feats_spec, piece_spec, piece_spec],
-            out_specs=item_spec,
-            scratch_shapes=[pltpu.VMEM((encoded, 2 * features), BF16)],
-        ),
-        compiler_params=pltpu.CompilerParams(vmem_limit_bytes=VMEM_LIMIT),
-        cost_estimate=image_cost,
-        name="image_forward",
-    )(image_place, image_feats, image_own, image_other)
-    query_count = items * QUERIES
-    second_in, cross_queries, cross_heads = local_call(
-        cross_forward_kernel,
-        (),
-        (first_in, norm, w_cross, w_cross_out, key_values),
-        (
-            shape_of(query_count, features, dtype=F32),
-            shape_of(query_count, features),
-            shape_of(query_count, features),
-        ),
-        [],
-        4 * query_count * features * features,
-        "cross_forward",
-    )
-    piece_shape = up_own.shape
-    block_out, two_grad, up_keep, up_send, down_keep, down_send, norm_grads = local_call(
-        feed_kernel,
-        (place, lengths),
-        (
-            first_in,
-            second_in,
-            norm,
-            out_grad,
-            up_own,
-            up_other,
-            down_own,
-            down_other,
-        ),
-        (
-            shape_of(rows, features),
-            shape_of(rows, features, dtype=F32),
-            shape_of(*piece_shape),
-            shape_of(*piece_shape),
-            shape_of(*down_own.shape),
-            shape_of(*down_own.shape),
-            shape_of(NORM_ROWS, features, dtype=F32),
-        ),
+    block_out, input_grad, in_sum, image_sum, feed_sum = run(
+        hidden_in, feats, lengths, out_grad, image_piece, begin_piece, feed_piece
+    )
+    half = own_image // 2
+    image_shard = jnp.stack(
         [
-            pltpu.VMEM((features, hidden_width), BF16),
-            pltpu.VMEM((hidden_width, features), BF16),
-            pltpu.VMEM((rows, features), F32),
-            pltpu.VMEM((rows, hidden_width), F32),
-            pltpu.VMEM((rows, hidden_width), BF16),
-        ],
-        12 * rows * features * hidden_width,
-        "feed",
-    )
-    up_shard = moves.scatter(up_keep, up_send, True)
-    down_shard = moves.scatter(down_keep, down_send, False)
-
-    grad_key_values, grad_cross, grad_cross_out, one_query_grad, norm_grads = local_call(
-        cross_backward_kernel,
-        (),
-        (
-            two_grad,
-            first_in,
-            second_in,
-            norm,
-            w_cross,
-            w_cross_out,
-            cross_queries,
-            cross_heads,
-            key_values,
-            norm_grads,
-        ),
-        (
-            shape_of(items, patches, 2 * features),
-            shape_of(features, features),
-            shape_of(features, features),
-            shape_of(query_count, features, dtype=F32),
-            shape_of(NORM_ROWS, features, dtype=F32),
-        ),
-        [pltpu.VMEM((query_count, features), BF16), pltpu.VMEM((query_count, features), BF16)],
-        8 * query_count * features * features,
-        "cross_backward",
-    )
-    image_keep, image_send = pl.pallas_call(
-        image_backward_kernel,
-        out_shape=(shape_of(*image_own.shape), shape_of(*image_own.shape)),
-        grid_spec=pltpu.PrefetchScalarGridSpec(
-            num_scalar_prefetch=1,
-            grid=(items,),
-            in_specs=[feats_spec, item_spec],
-            out_specs=(piece_spec, piece_spec),
-            scratch_shapes=[pltpu.VMEM((encoded, 2 * features), F32)],
-        ),
-        compiler_params=pltpu.CompilerParams(vmem_limit_bytes=VMEM_LIMIT),
-        cost_estimate=image_cost,
-        name="image_backward",
-    )(image_place, image_feats, grad_key_values)
-    image_shard = moves.scatter(image_keep, image_send, False)
-    input_grad, in_keep, in_send, out_keep, out_send = local_call(
-        self_backward_kernel,
-        (place, lengths),
-        (
-            one_query_grad,
-            two_grad,
-            first_in,
-            norm,
-            hidden_in,
-            qkv,
-            heads,
-            w_qkv,
-            w_self_out,
-            grad_cross,
-            grad_cross_out,
-            norm_grads,
-        ),
-        (
-            shape_of(rows, features),
-            shape_of(*in_own.shape),
-            shape_of(*in_own.shape),
-            shape_of(*out_own.shape),
-            shape_of(*out_own.shape),
-        ),
-        [
-            pltpu.VMEM((rows, features), F32),
-            pltpu.VMEM((rows, features), BF16),
-            pltpu.VMEM((rows, 3 * features), BF16),
-            pltpu.VMEM((features, 3 * features), BF16),
-        ],
-        20 * rows * features * features,
-        "self_backward",
-    )
-    in_shard = moves.scatter(in_keep, in_send, True)
-    out_rows = proj_out.shape[1]
-    if direct:
-        out_sum = moves.scatter(out_keep, out_send, False)
-        norm_sum = out_sum[2 * out_rows :]
-        out_shard = jnp.stack([out_sum[:out_rows], out_sum[out_rows : 2 * out_rows]])
-    else:
-        piece = width // GROUPS
-        norm_sum = lax.psum(out_keep[0, 2 * piece :].astype(F32), AXES)
-        out_shard = jnp.stack(
-            [
-                moves.scatter(
-                    out_keep[:, kind * piece : (kind + 1) * piece],
-                    out_send[:, kind * piece : (kind + 1) * piece],
-                    False,
-                )
-                for kind in range(2)
-            ]
-        )
-    norm_shard = lax.dynamic_slice(norm_sum, (0, norm_begin), norm_params.shape)
-    in_shard = jnp.stack([in_shard[:, kind * width : (kind + 1) * width] for kind in range(4)])
-    image_shard = jnp.stack([image_shard[:, :width], image_shard[:, width:]])
+            jnp.concatenate(
+                [
+                    image_sum[:half, (2 * part + kind) * width : (2 * part + kind + 1) * width]
+                    for part in range(2)
+                ],
+                axis=0,
+            )
+            for kind in range(2)
+        ]
+    )
+    cross_query = image_sum[half : half + own_out]
+    in_shard = jnp.stack(
+        [in_sum[:own_in, kind * width : (kind + 1) * width] for kind in range(3)]
+        + [
+            jnp.concatenate(
+                [cross_query[:, part * width : (part + 1) * width] for part in range(MODEL)],
+                axis=0,
+            )
+        ]
+    )
+    self_out = jnp.concatenate(
+        [in_sum[part * own_out : (part + 1) * own_out, 3 * width :] for part in range(MODEL)],
+        axis=1,
+    )
+    out_shard = jnp.stack([self_out, image_sum[half + own_out :]])
+    up_shard, down_shard = feed_sum[: feed_up.shape[0]], feed_sum[feed_up.shape[0] :]
+    norm_shard = lax.dynamic_slice(in_sum[own_in:], (0, norm_begin), norm_params.shape)
 
     groups = [
         (proj_in, proj_in_moments, proj_in_average, in_shard, DECAY_RATE, True),

time: 505 us -> 406 us (0.80)
  waiting for transfers between devices: 205 us -> 109 us
  Pallas kernels: 155 us -> 126 us
  other arithmetic: 28.7 us -> 50.6 us
  starting transfers between devices: 55.1 us -> 71.1 us
  local copies, waits for them, and re-layouts: 53.4 us -> 41.3 us
    ppermute x30, waiting for transfers between devices: 141 us -> 42.9 us  [hop(): lax.ppermute(values, AXES, [(i, i ^ flip) for i in range(self.count)])]
    pallas_call x5, Pallas kernels: 113 us -> 90.4 us  [local_call(): pl.pallas_call(kernel, out_shape=tuple(out_shapes), in_specs=[SCALARS] *...]
    ppermute x30 -> x18, starting transfers between devices: 18.4 us -> 39.9 us  [hop_z(): lax.ppermute(values, AXES, [(i, (i + step) % self.count) for i in range(s...]
    unnamed x79 -> x121, local copies, waits for them, and re-layouts: 35.9 us -> 18.8 us
    pallas_call x2, Pallas kernels: 42 us -> 35.9 us  [the longest x1 22.1 us: image_backward(): pl.pallas_call(image_backward_kernel, out_shape=(shape_of(*piece), shape_...]
    squeeze x5 -> x32, local copies, waits for them, and re-layouts: 0.06 us -> 6.08 us  [the longest x18 2.67 us: fold_second(): part[0]]
    ppermute x30, starting transfers between devices: 33.8 us -> 27.9 us  [hop(): lax.ppermute(values, AXES, [(i, i ^ flip) for i in range(self.count)])]
    reduce_sum x5 -> x7, other arithmetic: 2.5 us -> 8.1 us  [tensor_squares(): return jnp.sum(values * values, axis=tuple(range(1, values.ndim)))]
  transfers between devices with their start and end apart: 61 -> 49, of which waited for: 34 -> 23; matrix products, arithmetic and copies ran while one was open for 14% -> 8% of each run, Pallas kernels for 15% -> 25%
where the time goes in v2:
time: 406 us; the launch traced here: 401 us
  Pallas kernels  126 us (31%)
  waiting for transfers between devices  109 us (27%)
  starting transfers between devices  71.1 us (18%)
  other arithmetic  50.6 us (12%)
  local copies, waits for them, and re-layouts  41.3 us (10%)
    pallas_call x5, Pallas kernels, local_call(): pl.pallas_call(kernel, out_shape=tuple(out_shapes), in_specs=[SCALARS] *...  90.4 us
    ppermute x18, waiting for transfers between devices, hop_z(): lax.ppermute(values, AXES, [(i, (i + step) % self.count) for i in range(s...  63.2 us
    ppermute x30, waiting for transfers between devices, hop(): lax.ppermute(values, AXES, [(i, i ^ flip) for i in range(self.count)])  42.9 us
    ppermute x18, starting transfers between devices, hop_z(): lax.ppermute(values, AXES, [(i, (i + step) % self.count) for i in range(s...  39.9 us
    ppermute x30, starting transfers between devices, hop(): lax.ppermute(values, AXES, [(i, i ^ flip) for i in range(self.count)])  27.9 us
    pallas_call x1, Pallas kernels, image_backward(): pl.pallas_call(image_backward_kernel, out_shape=(shape_of(*piece), shape_...  22.1 us
    unnamed x121, local copies, waits for them, and re-layouts  18.8 us
    pallas_call x1, Pallas kernels, image_forward(): pl.pallas_call(image_forward_kernel, out_shape=shape_of(items, patches, 2...  13.8 us
  transfers between devices with their start and end apart: 49, of which 23 were waited for; matrix products, arithmetic and copies ran while one was open for 8% of the time, Pallas kernels for 25%

profile of v2, /device:TPU:0, one launch (start us, length us, event | category | flops | bytes accessed | tf_op | source)
XLA Modules:
  0.0 401.5 jit_solution(7162299435319371432)
XLA Ops:
  5.8 3.2 collective-permute-start
  9.1 2.6 collective-permute-start.1
  13.8 4.2 %collective-permute-done = bf16[160,768]{1,0:T(8,128)(2,1)S(1)} collective-permute-done((bf16[160,768]{1,0:T(8,128)(2,1)S(1)}, bf16[160,768]{1,0:T(8,128)(2,1)S(1)}, u32[]{:S(2)}, u32[]{:S(2)}) %collective-permute-start) | collective-permute-done | bytes 245792 | tf_op jit(solution)/shard_map/ppermute | solution.py:589
  18.0 9.7 %collective-permute-done.1 = bf16[160,768]{1,0:T(8,128)(2,1)S(1)} collective-permute-done((bf16[160,768]{1,0:T(8,128)(2,1)S(1)}, bf16[160,768]{1,0:T(8,128)(2,1)S(1)}, u32[]{:S(2)}, u32[]{:S(2)}) %collective-permute-start.1) | collective-permute-done | bytes 245792 | tf_op jit(solution)/shard_map/ppermute | solution.py:589
  31.1 5.7 %collective-permute-start.5 = (bf16[176,384]{1,0:T(8,128)(2,1)S(1)}, bf16[176,384]{1,0:T(8,128)(2,1)S(1)}, u32[]{:S(2)}, u32[]{:S(2)}) collective-permute-start(bf16[176,384]{1,0:T(8,128)(2,1)S(1)} %pad_maximum_fusion.38), channel_id=1, source_target_pairs={{0,8},{1,9},{2,10},{3,11},{4,12},{5,13},{6,14},{7,15},{8,16},{9,17... | collective-permute-start | bytes 405512 | tf_op jit(solution)/shard_map/ppermute | solution.py:589
  39.3 3.1 collective-permute-done.5
  42.3 4.2 %collective-permute-done.6 = bf16[176,384]{1,0:T(8,128)(2,1)S(1)} collective-permute-done((bf16[176,384]{1,0:T(8,128)(2,1)S(1)}, bf16[176,384]{1,0:T(8,128)(2,1)S(1)}, u32[]{:S(2)}, u32[]{:S(2)}) %collective-permute-start.6) | collective-permute-done | bytes 135200 | tf_op jit(solution)/shard_map/ppermute | solution.py:589
  48.1 3.4 collective-permute-start.12
  53.9 6.8 %collective-permute-done.12 = bf16[192,768]{1,0:T(8,128)(2,1)S(1)} collective-permute-done((bf16[192,768]{1,0:T(8,128)(2,1)S(1)}, bf16[192,768]{1,0:T(8,128)(2,1)S(1)}, u32[]{:S(2)}, u32[]{:S(2)}) %collective-permute-start.12) | collective-permute-done | bytes 294944 | tf_op jit(solution)/shard_map/ppermute | solution.py:589
  62.2 8.7 %collective-permute-done.13 = bf16[192,768]{1,0:T(8,128)(2,1)S(1)} collective-permute-done((bf16[192,768]{1,0:T(8,128)(2,1)S(1)}, bf16[192,768]{1,0:T(8,128)(2,1)S(1)}, u32[]{:S(2)}, u32[]{:S(2)}) %collective-permute-start.13) | collective-permute-done | bytes 294944 | tf_op jit(solution)/shard_map/ppermute | solution.py:589
  72.6 6.1 %collective-permute-done.11 = bf16[4,80,384]{2,1,0:T(8,128)(2,1)S(1)} collective-permute-done((bf16[4,80,384]{2,1,0:T(8,128)(2,1)S(1)}, bf16[4,80,384]{2,1,0:T(8,128)(2,1)S(1)}, u32[]{:S(2)}, u32[]{:S(2)}) %collective-permute-start.11) | collective-permute-done | bytes 245792 | tf_op jit(solution)/shard_map/ppermute | solution.py:576
  79.6 2.2 copy.90
  86.6 2.3 collective-permute-done.15.begin_other
  88.9 13.6 %self_forward.1 = (f32[512,768]{1,0:T(8,128)S(1)}, bf16[512,2304]{1,0:T(8,128)(2,1)S(1)}, bf16[512,768]{1,0:T(8,128)(2,1)S(1)}, bf16[768,2304]{1,0:T(8,128)(2,1)...) custom-call(s32[16]{0:T(128)S(1)} %pad_add_fusion.place, ...), custom_call_target="tpu_custom_call" | custom-call | flops 3019898880 | bytes 20471808 | tf_op jit(solution)/shard_map/self_forward/pallas_call | solution.py:548
  106.2 3.6 collective-permute-done.17
  113.0 2.0 collective-permute-done.20.image_other
  118.0 3.1 constant_dynamic-slice_fusion
  121.8 13.8 %image_forward.1.key_values = bf16[8,257,1536]{2,1,0:T(8,128)(2,1)S(1)} custom-call(s32[16]{0:T(128)S(1)} %pad_add_fusion.place, bf16[8,257,1408]{2,1,0:T(8,128)(2,1)S(1)} %copy.106.feats, bf16[16,176,384]{2,1,0:T(8,128)(2,1)S(1)} %bitcast.380, bf16[16,176,384]{2,1,0:T(8,128)(2,1)S(1)} %collective-permute-done.20.image_other), custom_call_target="tpu_custom_call" | custom-call | flops 8892973056 | bytes 16431104 | tf_op jit(solution)/shard_map/image_forward/pallas_call | solution.py:716
  135.7 11.2 %cross_forward.1 = (f32[256,768]{1,0:T(8,128)S(1)}, bf16[256,768]{1,0:T(8,128)(2,1)S(1)}, bf16[256,768]{1,0:T(8,128)(2,1)S(1)}) custom-call(f32[512,768]{1,0:T(8,128)S(1)} %get-tuple-element.159.first_in, f32[8,768]{1,0:T(8,128)S(1)} %get-tuple-element.160.norm, bf16[768,768]{1,0:T(8,128)(2,1)S(1)} %get-tuple-element.161.w_cross, ...), custom_call_target="tpu_custom_call" | custom-call | flops 603979776 | bytes 11845632 | tf_op jit(solution)/shard_map/cross_forward/pallas_call | solution.py:548
  153.4 2.2 copy-done.31
  155.7 8.0 %collective-permute-done.23.feed_other = bf16[16,192,768]{2,1,0:T(8,128)(2,1)} collective-permute-done((bf16[16,192,768]{2,1,0:T(8,128)(2,1)S(1)}, bf16[16,192,768]{2,1,0:T(8,128)(2,1)}, u32[]{:S(2)}, u32[]{:S(2)}) %collective-permute-start.23) | collective-permute-done | bytes 4718624 | tf_op jit(solution)/shard_map/ppermute | solution.py:576
  163.7 26.4 %feed.1 = (bf16[512,768]{1,0:T(8,128)(2,1)}, f32[512,768]{1,0:T(8,128)}, bf16[16,192,768]{2,1,0:T(8,128)(2,1)}, bf16[16,192,768]{2,1,0:T(8,128)(2,1)}, f32[8,768]{1,0:T(8,128)}) custom-call(s32[16]{0:T(128)} %copy-done.20, s32[8]{0:T(128)} %copy-done.18, f32[512,768]{1,0:T(8,128)} %copy-done.2, f32[256,768]{1,0:T(8,128)} %copy-done.7, f32[8,768]{1,0:T(8,128)} %copy-done.13, ...), custom_call_target="tpu_custom_call" | custom-call | flops 14495514624 | bytes 24428544 | tf_op jit(solution)/shard_map/feed/pallas_call | solution.py:548
  190.3 2.8 copy-done.1
  198.4 17.0 %cross_backward.1 = (bf16[8,257,1536]{2,1,0:T(8,128)(2,1)S(1)}, bf16[768,768]{1,0:T(8,128)(2,1)S(1)}, bf16[768,768]{1,0:T(8,128)(2,1)S(1)}, f32[256,768]{1,0:T(8,128)S(1)}, f32[8,768]{1,0:T(8,128)S(1)}) custom-call(f32[512,768]{1,0:T(8,128)S(1)} %copy-done.5, f32[512,768]{1,0:T(8,128)S(1)} %copy-done.3, f32[256,768]{1,0:T(8,128)S(1)} %copy-done.8, ...), custom_call_target="tpu_custom_call" | custom-call | flops 1207959552 | bytes 22929408 | tf_op jit(solution)/shard_map/cross_backward/pallas_call | solution.py:548
  215.4 2.8 fusion.1
  224.1 22.1 %image_backward.1 = (bf16[16,136,768]{2,1,0:T(8,128)(2,1)S(1)}, bf16[16,136,768]{2,1,0:T(8,128)(2,1)S(1)}) custom-call(s32[16]{0:T(128)S(1)} %copy-done.21, bf16[8,257,1408]{2,1,0:T(8,128)(2,1)S(1)} %bitcast.370, bf16[8,257,1536]{2,1,0:T(8,128)(2,1)S(1)} %get-tuple-element.179.grad_key_values, bf16[768,768]{1,0:T(8,128)(2,1)S(1)} %get-tuple-element.180.grad_cross, ...), custom_call_target="tpu_custom_call" | custom-call | flops 8892973056 | bytes 16431104 | tf_op jit(solution)/shard_map/image_backward/pallas_call | solution.py:751
  246.2 3.9 collective-permute-done.26
  250.7 2.1 fusion.6
  253.3 2.1 fusion.5
  264.0 22.1 %self_backward.1 = (bf16[512,768]{1,0:T(8,128)(2,1)}, bf16[16,104,768]{2,1,0:T(8,128)(2,1)S(1)}, bf16[16,104,768]{2,1,0:T(8,128)(2,1)S(1)}) custom-call(s32[16]{0:T(128)S(1)} %copy-done.21, s32[8]{0:T(128)S(1)} %copy-done.19, f32[256,768]{1,0:T(8,128)S(1)} %get-tuple-element.189.one_query_grad, f32[512,768]{1,0:T(8,128)S(1)} %copy-done.6, ...), custom_call_target="tpu_custom_call" | custom-call | flops 6039797760 | bytes 18530304 | tf_op jit(solution)/shard_map/self_backward/pallas_call | solution.py:548
  286.2 3.8 collective-permute-done.31
  292.9 4.6 %collective-permute-start.39 = (bf16[192,768]{1,0:T(8,128)(2,1)S(1)}, bf16[192,768]{1,0:T(8,128)(2,1)S(1)}, u32[]{:S(2)}, u32[]{:S(2)}) collective-permute-start(bf16[192,768]{1,0:T(8,128)(2,1)S(1)} %pad_maximum_fusion.25), channel_id=1, source_target_pairs={{0,8},{1,9},{2,10},{3,11},{4,12},{5,13},{6,14},{7,15},{8,16},{9,17... | collective-permute-start | bytes 884744 | tf_op jit(solution)/shard_map/ppermute | solution.py:589
  297.6 3.4 collective-permute-start.38
  304.8 8.9 %collective-permute-done.33 = bf16[4,64,768]{2,1,0:T(8,128)(2,1)S(1)} collective-permute-done((bf16[4,64,768]{2,1,0:T(8,128)(2,1)S(1)}, bf16[4,64,768]{2,1,0:T(8,128)(2,1)S(1)}, u32[]{:S(2)}, u32[]{:S(2)}) %collective-permute-start.33) | collective-permute-done | bytes 393248 | tf_op jit(solution)/shard_map/ppermute | solution.py:576
  316.9 3.9 collective-permute-done.38
  320.8 6.2 %collective-permute-done.37 = bf16[192,768]{1,0:T(8,128)(2,1)S(1)} collective-permute-done((bf16[192,768]{1,0:T(8,128)(2,1)S(1)}, bf16[192,768]{1,0:T(8,128)(2,1)S(1)}, u32[]{:S(2)}, u32[]{:S(2)}) %collective-permute-start.37) | collective-permute-done | bytes 294944 | tf_op jit(solution)/shard_map/ppermute | solution.py:589
  327.0 2.7 collective-permute-done.35
  333.5 2.6 collective-permute-start.42
  338.6 1.9 fusion.63
  342.2 5.4 %collective-permute-done.43 = bf16[136,768]{1,0:T(8,128)(2,1)S(1)} collective-permute-done((bf16[136,768]{1,0:T(8,128)(2,1)S(1)}, bf16[136,768]{1,0:T(8,128)(2,1)S(1)}, u32[]{:S(2)}, u32[]{:S(2)}) %collective-permute-start.43) | collective-permute-done | bytes 208928 | tf_op jit(solution)/shard_map/ppermute | solution.py:589
  348.3 4.8 %collective-permute-start.45 = (bf16[104,768]{1,0:T(8,128)(2,1)S(1)}, bf16[104,768]{1,0:T(8,128)(2,1)S(1)}, u32[]{:S(2)}, u32[]{:S(2)}) collective-permute-start(bf16[104,768]{1,0:T(8,128)(2,1)S(1)} %pad_maximum_fusion.32), channel_id=1, source_target_pairs={{0,24},{1,25},{2,26},{3,27},{4,28},{5,29},{6,30},{7,31},{8,0},{9,1... | collective-permute-start | bytes 479240 | tf_op jit(solution)/shard_map/ppermute | solution.py:589
  357.6 10.6 %collective-permute-done.46 = bf16[104,768]{1,0:T(8,128)(2,1)S(1)} collective-permute-done((bf16[104,768]{1,0:T(8,128)(2,1)S(1)}, bf16[104,768]{1,0:T(8,128)(2,1)S(1)}, u32[]{:S(2)}, u32[]{:S(2)}) %collective-permute-start.46) | collective-permute-done | bytes 159776 | tf_op jit(solution)/shard_map/ppermute | solution.py:589
  372.9 2.6 concatenate.149
  375.6 2.6 concatenate.166
  379.5 3.3 all-to-all-start
  387.3 2.7 all-to-all-done
  394.6 2.0 multiply_add_fusion.4
  396.6 1.9 multiply_add_fusion.5
  (321 shorter events, 103.0 us)
Async XLA Ops:
  5.8 12.2 %collective-permute-start = (bf16[160,768]{1,0:T(8,128)(2,1)S(1)}, bf16[160,768]{1,0:T(8,128)(2,1)S(1)}, u32[]{:S(2)}, u32[]{:S(2)}) collective-permute-start(bf16[160,768]{1,0:T(8,128)(2,1)S(1)} %constant_dynamic-update-slice_fusion), channel_id=1, source_target_pairs={{0,8},{1,9},{2,10},{3,11},{4,12},{5,13},{6,14},{7,15},{8,16},{9,17... | collective-permute-start | bytes 737288 | tf_op jit(solution)/shard_map/ppermute | solution.py:589
  9.1 18.6 %collective-permute-start.1 = (bf16[160,768]{1,0:T(8,128)(2,1)S(1)}, bf16[160,768]{1,0:T(8,128)(2,1)S(1)}, u32[]{:S(2)}, u32[]{:S(2)}) collective-permute-start(bf16[160,768]{1,0:T(8,128)(2,1)S(1)} %constant_dynamic-update-slice_fusion), channel_id=1, source_target_pairs={{0,16},{1,17},{2,18},{3,19},{4,20},{5,21},{6,22},{7,23},{8,24},{9,... | collective-permute-start | bytes 737288 | tf_op jit(solution)/shard_map/ppermute | solution.py:589
  11.7 16.1 %collective-permute-start.2 = (bf16[160,768]{1,0:T(8,128)(2,1)S(1)}, bf16[160,768]{1,0:T(8,128)(2,1)S(1)}, u32[]{:S(2)}, u32[]{:S(2)}) collective-permute-start(bf16[160,768]{1,0:T(8,128)(2,1)S(1)} %constant_dynamic-update-slice_fusion), channel_id=1, source_target_pairs={{0,24},{1,25},{2,26},{3,27},{4,28},{5,29},{6,30},{7,31},{8,0},{9,1... | collective-permute-start | bytes 737288 | tf_op jit(solution)/shard_map/ppermute | solution.py:589
  28.0 18.6 %collective-permute-start.3 = (bf16[4,80,768]{2,1,0:T(8,128)(2,1)S(1)}, bf16[4,80,768]{2,1,0:T(8,128)(2,1)S(1)}, u32[]{:S(2)}, u32[]{:S(2)}) collective-permute-start(bf16[4,80,768]{2,1,0:T(8,128)(2,1)S(1)} %get-tuple-element.399), channel_id=1, source_target_pairs={{0,2},{1,3},{2,0},{3,1},{4,6},{5,7},{6,4},{7,5},{8,10},{9,11},{10,... | collective-permute-start | bytes 1474568 | tf_op jit(solution)/shard_map/ppermute | solution.py:576
  29.6 17.1 %collective-permute-start.4 = (bf16[4,80,768]{2,1,0:T(8,128)(2,1)S(1)}, bf16[4,80,768]{2,1,0:T(8,128)(2,1)S(1)}, u32[]{:S(2)}, u32[]{:S(2)}) collective-permute-start(bf16[4,80,768]{2,1,0:T(8,128)(2,1)S(1)} %get-tuple-element.398), channel_id=1, source_target_pairs={{0,4},{1,5},{2,6},{3,7},{4,0},{5,1},{6,2},{7,3},{8,12},{9,13},{10,... | collective-permute-start | bytes 1474568 | tf_op jit(solution)/shard_map/ppermute | solution.py:576
  31.1 11.3 %collective-permute-start.5 = (bf16[176,384]{1,0:T(8,128)(2,1)S(1)}, bf16[176,384]{1,0:T(8,128)(2,1)S(1)}, u32[]{:S(2)}, u32[]{:S(2)}) collective-permute-start(bf16[176,384]{1,0:T(8,128)(2,1)S(1)} %pad_maximum_fusion.38), channel_id=1, source_target_pairs={{0,8},{1,9},{2,10},{3,11},{4,12},{5,13},{6,14},{7,15},{8,16},{9,17... | collective-permute-start | bytes 405512 | tf_op jit(solution)/shard_map/ppermute | solution.py:589
  36.8 9.7 %collective-permute-start.6 = (bf16[176,384]{1,0:T(8,128)(2,1)S(1)}, bf16[176,384]{1,0:T(8,128)(2,1)S(1)}, u32[]{:S(2)}, u32[]{:S(2)}) collective-permute-start(bf16[176,384]{1,0:T(8,128)(2,1)S(1)} %pad_maximum_fusion.38), channel_id=1, source_target_pairs={{0,16},{1,17},{2,18},{3,19},{4,20},{5,21},{6,22},{7,23},{8,24},{9,... | collective-permute-start | bytes 405512 | tf_op jit(solution)/shard_map/ppermute | solution.py:589
  38.4 8.1 %collective-permute-start.7 = (bf16[176,384]{1,0:T(8,128)(2,1)S(1)}, bf16[176,384]{1,0:T(8,128)(2,1)S(1)}, u32[]{:S(2)}, u32[]{:S(2)}) collective-permute-start(bf16[176,384]{1,0:T(8,128)(2,1)S(1)} %pad_maximum_fusion.38), channel_id=1, source_target_pairs={{0,24},{1,25},{2,26},{3,27},{4,28},{5,29},{6,30},{7,31},{8,0},{9,1... | collective-permute-start | bytes 405512 | tf_op jit(solution)/shard_map/ppermute | solution.py:589
  46.8 32.0 %collective-permute-start.9 = (bf16[2,4,80,768]{3,2,1,0:T(8,128)(2,1)S(1)}, bf16[2,4,80,768]{3,2,1,0:T(8,128)(2,1)S(1)}, u32[]{:S(2)}, u32[]{:S(2)}) collective-permute-start(bf16[2,4,80,768]{3,2,1,0:T(8,128)(2,1)S(1)} %get-tuple-element.395), channel_id=1, source_target_pairs={{0,2},{1,3},{2,0},{3,1},{4,6},{5,7},{6,4},{7,5},{8,10},{9,11},{10,... | collective-permute-start | bytes 2949128 | tf_op jit(solution)/shard_map/ppermute | solution.py:576
  47.5 31.2 %collective-permute-start.8 = (bf16[2,4,80,768]{3,2,1,0:T(8,128)(2,1)S(1)}, bf16[2,4,80,768]{3,2,1,0:T(8,128)(2,1)S(1)}, u32[]{:S(2)}, u32[]{:S(2)}) collective-permute-start(bf16[2,4,80,768]{3,2,1,0:T(8,128)(2,1)S(1)} %get-tuple-element.393), channel_id=1, source_target_pairs={{0,4},{1,5},{2,6},{3,7},{4,0},{5,1},{6,2},{7,3},{8,12},{9,13},{10,... | collective-permute-start | bytes 2949128 | tf_op jit(solution)/shard_map/ppermute | solution.py:576
  48.1 12.6 %collective-permute-start.12 = (bf16[192,768]{1,0:T(8,128)(2,1)S(1)}, bf16[192,768]{1,0:T(8,128)(2,1)S(1)}, u32[]{:S(2)}, u32[]{:S(2)}) collective-permute-start(bf16[192,768]{1,0:T(8,128)(2,1)S(1)} %pad_maximum_fusion.22), channel_id=1, source_target_pairs={{0,8},{1,9},{2,10},{3,11},{4,12},{5,13},{6,14},{7,15},{8,16},{9,17... | collective-permute-start | bytes 884744 | tf_op jit(solution)/shard_map/ppermute | solution.py:589
  51.5 19.5 %collective-permute-start.13 = (bf16[192,768]{1,0:T(8,128)(2,1)S(1)}, bf16[192,768]{1,0:T(8,128)(2,1)S(1)}, u32[]{:S(2)}, u32[]{:S(2)}) collective-permute-start(bf16[192,768]{1,0:T(8,128)(2,1)S(1)} %pad_maximum_fusion.22), channel_id=1, source_target_pairs={{0,16},{1,17},{2,18},{3,19},{4,20},{5,21},{6,22},{7,23},{8,24},{9,... | collective-permute-start | bytes 884744 | tf_op jit(solution)/shard_map/ppermute | solution.py:589
  53.2 19.2 %collective-permute-start.14 = (bf16[192,768]{1,0:T(8,128)(2,1)S(1)}, bf16[192,768]{1,0:T(8,128)(2,1)S(1)}, u32[]{:S(2)}, u32[]{:S(2)}) collective-permute-start(bf16[192,768]{1,0:T(8,128)(2,1)S(1)} %pad_maximum_fusion.22), channel_id=1, source_target_pairs={{0,24},{1,25},{2,26},{3,27},{4,28},{5,29},{6,30},{7,31},{8,0},{9,1... | collective-permute-start | bytes 884744 | tf_op jit(solution)/shard_map/ppermute | solution.py:589
  60.7 18.0 %collective-permute-start.10 = (bf16[4,96,384]{2,1,0:T(8,128)(2,1)S(1)}, bf16[4,96,384]{2,1,0:T(8,128)(2,1)S(1)}, u32[]{:S(2)}, u32[]{:S(2)}) collective-permute-start(bf16[4,96,384]{2,1,0:T(8,128)(2,1)S(1)} %get-tuple-element.409), channel_id=1, source_target_pairs={{0,2},{1,3},{2,0},{3,1},{4,6},{5,7},{6,4},{7,5},{8,10},{9,11},{10,... | collective-permute-start | bytes 884744 | tf_op jit(solution)/shard_map/ppermute | solution.py:576
  70.9 7.8 %collective-permute-start.11 = (bf16[4,80,384]{2,1,0:T(8,128)(2,1)S(1)}, bf16[4,80,384]{2,1,0:T(8,128)(2,1)S(1)}, u32[]{:S(2)}, u32[]{:S(2)}) collective-permute-start(bf16[4,80,384]{2,1,0:T(8,128)(2,1)S(1)} %get-tuple-element.407), channel_id=1, source_target_pairs={{0,4},{1,5},{2,6},{3,7},{4,0},{5,1},{6,2},{7,3},{8,12},{9,13},{10,... | collective-permute-start | bytes 737288 | tf_op jit(solution)/shard_map/ppermute | solution.py:576
  81.8 7.1 %collective-permute-start.15 = (bf16[16,160,768]{2,1,0:T(8,128)(2,1)}, bf16[16,160,768]{2,1,0:T(8,128)(2,1)}, u32[]{:S(2)}, u32[]{:S(2)}) collective-permute-start(bf16[16,160,768]{2,1,0:T(8,128)(2,1)} %bitcast.33.begin_own), channel_id=1, source_target_pairs={{0,1},{1,0},{2,3},{3,2},{4,5},{5,4},{6,7},{7,6},{8,9},{9,8},{10,11... | collective-permute-start | bytes 11796488 | tf_op jit(solution)/shard_map/ppermute | solution.py:576
  82.0 27.9 %collective-permute-start.16 = (bf16[2,4,96,384]{3,2,1,0:T(8,128)(2,1)S(1)}, bf16[2,4,96,384]{3,2,1,0:T(8,128)(2,1)S(1)}, u32[]{:S(2)}, u32[]{:S(2)}) collective-permute-start(bf16[2,4,96,384]{3,2,1,0:T(8,128)(2,1)S(1)} %get-tuple-element.405), channel_id=1, source_target_pairs={{0,4},{1,5},{2,6},{3,7},{4,0},{5,1},{6,2},{7,3},{8,12},{9,13},{10,... | collective-permute-start | bytes 1769480 | tf_op jit(solution)/shard_map/ppermute | solution.py:576
  83.8 26.1 %collective-permute-start.18 = (bf16[4,96,768]{2,1,0:T(8,128)(2,1)S(1)}, bf16[4,96,768]{2,1,0:T(8,128)(2,1)S(1)}, u32[]{:S(2)}, u32[]{:S(2)}) collective-permute-start(bf16[4,96,768]{2,1,0:T(8,128)(2,1)S(1)} %get-tuple-element.389), channel_id=1, source_target_pairs={{0,2},{1,3},{2,0},{3,1},{4,6},{5,7},{6,4},{7,5},{8,10},{9,11},{10,... | collective-permute-start | bytes 1769480 | tf_op jit(solution)/shard_map/ppermute | solution.py:576
  85.3 25.1 %collective-permute-start.19 = (bf16[4,96,768]{2,1,0:T(8,128)(2,1)S(1)}, bf16[4,96,768]{2,1,0:T(8,128)(2,1)S(1)}, u32[]{:S(2)}, u32[]{:S(2)}) collective-permute-start(bf16[4,96,768]{2,1,0:T(8,128)(2,1)S(1)} %get-tuple-element.388), channel_id=1, source_target_pairs={{0,4},{1,5},{2,6},{3,7},{4,0},{5,1},{6,2},{7,3},{8,12},{9,13},{10,... | collective-permute-start | bytes 1769480 | tf_op jit(solution)/shard_map/ppermute | solution.py:576
  86.0 23.9 %collective-permute-start.17 = (bf16[2,4,80,384]{3,2,1,0:T(8,128)(2,1)S(1)}, bf16[2,4,80,384]{3,2,1,0:T(8,128)(2,1)S(1)}, u32[]{:S(2)}, u32[]{:S(2)}) collective-permute-start(bf16[2,4,80,384]{3,2,1,0:T(8,128)(2,1)S(1)} %get-tuple-element.411), channel_id=1, source_target_pairs={{0,2},{1,3},{2,0},{3,1},{4,6},{5,7},{6,4},{7,5},{8,10},{9,11},{10,... | collective-permute-start | bytes 1474568 | tf_op jit(solution)/shard_map/ppermute | solution.py:576
  115.0 34.3 %collective-permute-start.21 = (bf16[2,4,96,768]{3,2,1,0:T(8,128)(2,1)}, bf16[2,4,96,768]{3,2,1,0:T(8,128)(2,1)}, u32[]{:S(2)}, u32[]{:S(2)}) collective-permute-start(bf16[2,4,96,768]{3,2,1,0:T(8,128)(2,1)} %pad_maximum_fusion.4), channel_id=1, source_target_pairs={{0,4},{1,5},{2,6},{3,7},{4,0},{5,1},{6,2},{7,3},{8,12},{9,13},{10,... | collective-permute-start | bytes 3538952 | tf_op jit(solution)/shard_map/ppermute | solution.py:576
  116.5 32.8 %collective-permute-start.22 = (bf16[2,4,96,768]{3,2,1,0:T(8,128)(2,1)}, bf16[2,4,96,768]{3,2,1,0:T(8,128)(2,1)}, u32[]{:S(2)}, u32[]{:S(2)}) collective-permute-start(bf16[2,4,96,768]{3,2,1,0:T(8,128)(2,1)} %pad_maximum_fusion.5), channel_id=1, source_target_pairs={{0,2},{1,3},{2,0},{3,1},{4,6},{5,7},{6,4},{7,5},{8,10},{9,11},{10,... | collective-permute-start | bytes 3538952 | tf_op jit(solution)/shard_map/ppermute | solution.py:576
  155.7 8.0 %collective-permute-start.23 = (bf16[16,192,768]{2,1,0:T(8,128)(2,1)S(1)}, bf16[16,192,768]{2,1,0:T(8,128)(2,1)}, u32[]{:S(2)}, u32[]{:S(2)}) collective-permute-start(bf16[16,192,768]{2,1,0:T(8,128)(2,1)S(1)} %bitcast.385), channel_id=1, source_target_pairs={{0,1},{1,0},{2,3},{3,2},{4,5},{5,4},{6,7},{7,6},{8,9},{9,8},{10,11... | collective-permute-start | bytes 14155784 | tf_op jit(solution)/shard_map/ppermute | solution.py:576
  190.1 25.3 %collective-permute-start.24 = (bf16[16,192,768]{2,1,0:T(8,128)(2,1)}, bf16[16,192,768]{2,1,0:T(8,128)(2,1)}, u32[]{:S(2)}, u32[]{:S(2)}) collective-permute-start(bf16[16,192,768]{2,1,0:T(8,128)(2,1)} %get-tuple-element.178), channel_id=1, source_target_pairs={{0,1},{1,0},{2,3},{3,2},{4,5},{5,4},{6,7},{7,6},{8,9},{9,8},{10,11... | collective-permute-start | bytes 14155784 | tf_op jit(solution)/shard_map/ppermute | solution.py:576
  221.4 28.6 %collective-permute-start.26 = (bf16[2,4,96,768]{3,2,1,0:T(8,128)(2,1)}, bf16[2,4,96,768]{3,2,1,0:T(8,128)(2,1)}, u32[]{:S(2)}, u32[]{:S(2)}) collective-permute-start(bf16[2,4,96,768]{3,2,1,0:T(8,128)(2,1)} %fusion.1), channel_id=1, source_target_pairs={{0,2},{1,3},{2,0},{3,1},{4,6},{5,7},{6,4},{7,5},{8,10},{9,11},{10,... | collective-permute-start | bytes 3538952 | tf_op jit(solution)/shard_map/ppermute | solution.py:576
  222.0 28.0 %collective-permute-start.25 = (bf16[2,4,96,768]{3,2,1,0:T(8,128)(2,1)S(1)}, bf16[2,4,96,768]{3,2,1,0:T(8,128)(2,1)}, u32[]{:S(2)}, u32[]{:S(2)}) collective-permute-start(bf16[2,4,96,768]{3,2,1,0:T(8,128)(2,1)S(1)} %fusion), channel_id=1, source_target_pairs={{0,4},{1,5},{2,6},{3,7},{4,0},{5,1},{6,2},{7,3},{8,12},{9,13},{10,... | collective-permute-start | bytes 3538952 | tf_op jit(solution)/shard_map/ppermute | solution.py:576
  250.1 9.2 %collective-permute-start.27 = (bf16[16,136,768]{2,1,0:T(8,128)(2,1)S(1)}, bf16[16,136,768]{2,1,0:T(8,128)(2,1)S(1)}, u32[]{:S(2)}, u32[]{:S(2)}) collective-permute-start(bf16[16,136,768]{2,1,0:T(8,128)(2,1)S(1)} %get-tuple-element.188), channel_id=1, source_target_pairs={{0,1},{1,0},{2,3},{3,2},{4,5},{5,4},{6,7},{7,6},{8,9},{9,8},{10,11... | collective-permute-start | bytes 10027016 | tf_op jit(solution)/shard_map/ppermute | solution.py:576
  252.8 33.4 %collective-permute-start.29 = (bf16[4,96,768]{2,1,0:T(8,128)(2,1)}, bf16[4,96,768]{2,1,0:T(8,128)(2,1)}, u32[]{:S(2)}, u32[]{:S(2)}) collective-permute-start(bf16[4,96,768]{2,1,0:T(8,128)(2,1)} %fusion.6), channel_id=1, source_target_pairs={{0,4},{1,5},{2,6},{3,7},{4,0},{5,1},{6,2},{7,3},{8,12},{9,13},{10,... | collective-permute-start | bytes 1769480 | tf_op jit(solution)/shard_map/ppermute | solution.py:576
  255.4 30.8 %collective-permute-start.28 = (bf16[4,96,768]{2,1,0:T(8,128)(2,1)}, bf16[4,96,768]{2,1,0:T(8,128)(2,1)}, u32[]{:S(2)}, u32[]{:S(2)}) collective-permute-start(bf16[4,96,768]{2,1,0:T(8,128)(2,1)} %fusion.5), channel_id=1, source_target_pairs={{0,2},{1,3},{2,0},{3,1},{4,6},{5,7},{6,4},{7,5},{8,10},{9,11},{10,... | collective-permute-start | bytes 1769480 | tf_op jit(solution)/shard_map/ppermute | solution.py:576
  260.8 29.2 %collective-permute-start.31 = (bf16[2,4,72,768]{3,2,1,0:T(8,128)(2,1)}, bf16[2,4,72,768]{3,2,1,0:T(8,128)(2,1)S(1)}, u32[]{:S(2)}, u32[]{:S(2)}) collective-permute-start(bf16[2,4,72,768]{3,2,1,0:T(8,128)(2,1)} %fusion.2), channel_id=1, source_target_pairs={{0,2},{1,3},{2,0},{3,1},{4,6},{5,7},{6,4},{7,5},{8,10},{9,11},{10,... | collective-permute-start | bytes 2654216 | tf_op jit(solution)/shard_map/ppermute | solution.py:576
  261.5 24.7 %collective-permute-start.30 = (bf16[2,4,64,768]{3,2,1,0:T(8,128)(2,1)S(1)}, bf16[2,4,64,768]{3,2,1,0:T(8,128)(2,1)S(1)}, u32[]{:S(2)}, u32[]{:S(2)}) collective-permute-start(bf16[2,4,64,768]{3,2,1,0:T(8,128)(2,1)S(1)} %fusion.3), channel_id=1, source_target_pairs={{0,4},{1,5},{2,6},{3,7},{4,0},{5,1},{6,2},{7,3},{8,12},{9,13},{10,... | collective-permute-start | bytes 2359304 | tf_op jit(solution)/shard_map/ppermute | solution.py:576
  290.0 23.7 %collective-permute-start.32 = (bf16[16,104,768]{2,1,0:T(8,128)(2,1)S(1)}, bf16[16,104,768]{2,1,0:T(8,128)(2,1)S(1)}, u32[]{:S(2)}, u32[]{:S(2)}) collective-permute-start(bf16[16,104,768]{2,1,0:T(8,128)(2,1)S(1)} %get-tuple-element.207), channel_id=1, source_target_pairs={{0,1},{1,0},{2,3},{3,2},{4,5},{5,4},{6,7},{7,6},{8,9},{9,8},{10,11... | collective-permute-start | bytes 7667720 | tf_op jit(solution)/shard_map/ppermute | solution.py:576
  292.9 23.9 %collective-permute-start.39 = (bf16[192,768]{1,0:T(8,128)(2,1)S(1)}, bf16[192,768]{1,0:T(8,128)(2,1)S(1)}, u32[]{:S(2)}, u32[]{:S(2)}) collective-permute-start(bf16[192,768]{1,0:T(8,128)(2,1)S(1)} %pad_maximum_fusion.25), channel_id=1, source_target_pairs={{0,8},{1,9},{2,10},{3,11},{4,12},{5,13},{6,14},{7,15},{8,16},{9,17... | collective-permute-start | bytes 884744 | tf_op jit(solution)/shard_map/ppermute | solution.py:589
  297.6 23.2 %collective-permute-start.38 = (bf16[192,768]{1,0:T(8,128)(2,1)S(1)}, bf16[192,768]{1,0:T(8,128)(2,1)S(1)}, u32[]{:S(2)}, u32[]{:S(2)}) collective-permute-start(bf16[192,768]{1,0:T(8,128)(2,1)S(1)} %pad_maximum_fusion.24), channel_id=1, source_target_pairs={{0,16},{1,17},{2,18},{3,19},{4,20},{5,21},{6,22},{7,23},{8,24},{9,... | collective-permute-start | bytes 884744 | tf_op jit(solution)/shard_map/ppermute | solution.py:589
  301.2 12.5 %collective-permute-start.34 = (bf16[4,72,768]{2,1,0:T(8,128)(2,1)S(1)}, bf16[4,72,768]{2,1,0:T(8,128)(2,1)S(1)}, u32[]{:S(2)}, u32[]{:S(2)}) collective-permute-start(bf16[4,72,768]{2,1,0:T(8,128)(2,1)S(1)} %fusion.8), channel_id=1, source_target_pairs={{0,4},{1,5},{2,6},{3,7},{4,0},{5,1},{6,2},{7,3},{8,12},{9,13},{10,... | collective-permute-start | bytes 1327112 | tf_op jit(solution)/shard_map/ppermute | solution.py:576
  302.9 10.8 %collective-permute-start.33 = (bf16[4,64,768]{2,1,0:T(8,128)(2,1)S(1)}, bf16[4,64,768]{2,1,0:T(8,128)(2,1)S(1)}, u32[]{:S(2)}, u32[]{:S(2)}) collective-permute-start(bf16[4,64,768]{2,1,0:T(8,128)(2,1)S(1)} %fusion.16), channel_id=1, source_target_pairs={{0,2},{1,3},{2,0},{3,1},{4,6},{5,7},{6,4},{7,5},{8,10},{9,11},{10,... | collective-permute-start | bytes 1179656 | tf_op jit(solution)/shard_map/ppermute | solution.py:576
  313.7 13.3 %collective-permute-start.37 = (bf16[192,768]{1,0:T(8,128)(2,1)S(1)}, bf16[192,768]{1,0:T(8,128)(2,1)S(1)}, u32[]{:S(2)}, u32[]{:S(2)}) collective-permute-start(bf16[192,768]{1,0:T(8,128)(2,1)S(1)} %pad_maximum_fusion.23), channel_id=1, source_target_pairs={{0,24},{1,25},{2,26},{3,27},{4,28},{5,29},{6,30},{7,31},{8,0},{9,1... | collective-permute-start | bytes 884744 | tf_op jit(solution)/shard_map/ppermute | solution.py:589
  314.1 16.5 %collective-permute-start.36 = (bf16[2,4,56,768]{3,2,1,0:T(8,128)(2,1)S(1)}, bf16[2,4,56,768]{3,2,1,0:T(8,128)(2,1)S(1)}, u32[]{:S(2)}, u32[]{:S(2)}) collective-permute-start(bf16[2,4,56,768]{3,2,1,0:T(8,128)(2,1)S(1)} %fusion.4), channel_id=1, source_target_pairs={{0,2},{1,3},{2,0},{3,1},{4,6},{5,7},{6,4},{7,5},{8,10},{9,11},{10,... | collective-permute-start | bytes 2064392 | tf_op jit(solution)/shard_map/ppermute | solution.py:576
  315.6 14.1 %collective-permute-start.35 = (bf16[2,4,48,768]{3,2,1,0:T(8,128)(2,1)S(1)}, bf16[2,4,48,768]{3,2,1,0:T(8,128)(2,1)S(1)}, u32[]{:S(2)}, u32[]{:S(2)}) collective-permute-start(bf16[2,4,48,768]{3,2,1,0:T(8,128)(2,1)S(1)} %fusion.7), channel_id=1, source_target_pairs={{0,4},{1,5},{2,6},{3,7},{4,0},{5,1},{6,2},{7,3},{8,12},{9,13},{10,... | collective-permute-start | bytes 1769480 | tf_op jit(solution)/shard_map/ppermute | solution.py:576
  331.3 10.9 %collective-permute-start.44 = (bf16[136,768]{1,0:T(8,128)(2,1)S(1)}, bf16[136,768]{1,0:T(8,128)(2,1)S(1)}, u32[]{:S(2)}, u32[]{:S(2)}) collective-permute-start(bf16[136,768]{1,0:T(8,128)(2,1)S(1)} %pad_maximum_fusion.29), channel_id=1, source_target_pairs={{0,8},{1,9},{2,10},{3,11},{4,12},{5,13},{6,14},{7,15},{8,16},{9,17... | collective-permute-start | bytes 626696 | tf_op jit(solution)/shard_map/ppermute | solution.py:589
  332.7 14.9 %collective-permute-start.43 = (bf16[136,768]{1,0:T(8,128)(2,1)S(1)}, bf16[136,768]{1,0:T(8,128)(2,1)S(1)}, u32[]{:S(2)}, u32[]{:S(2)}) collective-permute-start(bf16[136,768]{1,0:T(8,128)(2,1)S(1)} %pad_maximum_fusion.28), channel_id=1, source_target_pairs={{0,16},{1,17},{2,18},{3,19},{4,20},{5,21},{6,22},{7,23},{8,24},{9,... | collective-permute-start | bytes 626696 | tf_op jit(solution)/shard_map/ppermute | solution.py:589
  333.5 14.1 %collective-permute-start.42 = (bf16[136,768]{1,0:T(8,128)(2,1)S(1)}, bf16[136,768]{1,0:T(8,128)(2,1)S(1)}, u32[]{:S(2)}, u32[]{:S(2)}) collective-permute-start(bf16[136,768]{1,0:T(8,128)(2,1)S(1)} %pad_maximum_fusion.27), channel_id=1, source_target_pairs={{0,24},{1,25},{2,26},{3,27},{4,28},{5,29},{6,30},{7,31},{8,0},{9,1... | collective-permute-start | bytes 626696 | tf_op jit(solution)/shard_map/ppermute | solution.py:589
  336.1 11.5 %collective-permute-start.41 = (bf16[4,56,768]{2,1,0:T(8,128)(2,1)S(1)}, bf16[4,56,768]{2,1,0:T(8,128)(2,1)S(1)}, u32[]{:S(2)}, u32[]{:S(2)}) collective-permute-start(bf16[4,56,768]{2,1,0:T(8,128)(2,1)S(1)} %fusion.26), channel_id=1, source_target_pairs={{0,4},{1,5},{2,6},{3,7},{4,0},{5,1},{6,2},{7,3},{8,12},{9,13},{10,... | collective-permute-start | bytes 1032200 | tf_op jit(solution)/shard_map/ppermute | solution.py:576
  336.8 10.8 %collective-permute-start.40 = (bf16[4,48,768]{2,1,0:T(8,128)(2,1)S(1)}, bf16[4,48,768]{2,1,0:T(8,128)(2,1)S(1)}, u32[]{:S(2)}, u32[]{:S(2)}) collective-permute-start(bf16[4,48,768]{2,1,0:T(8,128)(2,1)S(1)} %fusion.31), channel_id=1, source_target_pairs={{0,2},{1,3},{2,0},{3,1},{4,6},{5,7},{6,4},{7,5},{8,10},{9,11},{10,... | collective-permute-start | bytes 884744 | tf_op jit(solution)/shard_map/ppermute | solution.py:576
  348.3 9.3 %collective-permute-start.45 = (bf16[104,768]{1,0:T(8,128)(2,1)S(1)}, bf16[104,768]{1,0:T(8,128)(2,1)S(1)}, u32[]{:S(2)}, u32[]{:S(2)}) collective-permute-start(bf16[104,768]{1,0:T(8,128)(2,1)S(1)} %pad_maximum_fusion.32), channel_id=1, source_target_pairs={{0,24},{1,25},{2,26},{3,27},{4,28},{5,29},{6,30},{7,31},{8,0},{9,1... | collective-permute-start | bytes 479240 | tf_op jit(solution)/shard_map/ppermute | solution.py:589
  353.1 15.0 %collective-permute-start.46 = (bf16[104,768]{1,0:T(8,128)(2,1)S(1)}, bf16[104,768]{1,0:T(8,128)(2,1)S(1)}, u32[]{:S(2)}, u32[]{:S(2)}) collective-permute-start(bf16[104,768]{1,0:T(8,128)(2,1)S(1)} %pad_maximum_fusion.33), channel_id=1, source_target_pairs={{0,16},{1,17},{2,18},{3,19},{4,20},{5,21},{6,22},{7,23},{8,24},{9,... | collective-permute-start | bytes 479240 | tf_op jit(solution)/shard_map/ppermute | solution.py:589
  354.4 13.7 %collective-permute-start.47 = (bf16[104,768]{1,0:T(8,128)(2,1)S(1)}, bf16[104,768]{1,0:T(8,128)(2,1)S(1)}, u32[]{:S(2)}, u32[]{:S(2)}) collective-permute-start(bf16[104,768]{1,0:T(8,128)(2,1)S(1)} %pad_maximum_fusion.34), channel_id=1, source_target_pairs={{0,8},{1,9},{2,10},{3,11},{4,12},{5,13},{6,14},{7,15},{8,16},{9,17... | collective-permute-start | bytes 479240 | tf_op jit(solution)/shard_map/ppermute | solution.py:589
  379.5 10.5 %all-to-all-start = ((f32[32,2,16]{2,1,0:T(2,128)}), f32[32,2,16]{2,1,0:T(2,128)}, u32[]{:S(2)}, u32[]{:S(2)}) async-start(f32[32,2,16]{2,1,0:T(2,128)} %broadcast_in_dim.30), calls=%async_computation | async-start | bytes 65536 | tf_op jit(solution)/shard_map/all_to_all | solution.py:1217
  (58 other events, 504.5 us)

commit v3 on v2

v3 whole, which is shorter than its diff:
```python
import functools

import jax
import jax.numpy as jnp
from jax import lax
from jax.experimental import pallas as pl
from jax.experimental.pallas import tpu as pltpu
from jax.sharding import PartitionSpec as P

HEAD = 64
PATCHES = 257
QUERIES = 32
TEXT = 32
SEQ = QUERIES + TEXT
STEP = 10


NORM_EPSILON = 1e-06
ADAM_EPSILON = 1e-06
SQUARE_EPSILON = 1e-06
BETA_ONE = 0.9
BETA_TWO = 0.999
LEARN_RATE = 0.5
DECAY_RATE = 0.01
AVERAGE_RATE = 0.6
MASK_VALUE = -1e30

AXES = ("dp", "mp")
GROUPS = 8
MODEL = 4
SLOTS = 16
NORM_ROWS = 8
LANES = 128
IMAGE_SPLIT = 64
SELF_SPLIT = 48
BLOCK = 256
WIDE = 256
SLOT = 272
MIB = 1024 * 1024

BF16 = jnp.bfloat16
F32 = jnp.float32


def dot_nn(left_side, right_side):
    return lax.dot_general(
        left_side, right_side, (((1,), (0,)), ((), ())), preferred_element_type=F32
    )


def dot_nt(left_side, right_side):
    return lax.dot_general(
        left_side, right_side, (((1,), (1,)), ((), ())), preferred_element_type=F32
    )


def dot_tn(left_side, right_side):
    return lax.dot_general(
        left_side, right_side, (((0,), (0,)), ((), ())), preferred_element_type=F32
    )


def normalise(inputs):
    centred = inputs - jnp.mean(inputs, axis=-1, keepdims=True)
    inverse = lax.rsqrt(jnp.mean(centred * centred, axis=-1, keepdims=True) + NORM_EPSILON)
    return centred * inverse, inverse


def norm_back(gradient, normed, inverse, gain):
    scaled = gradient * gain
    centre_term = jnp.mean(scaled, axis=-1, keepdims=True)
    normed_term = jnp.mean(scaled * normed, axis=-1, keepdims=True)
    return inverse * (scaled - centre_term - normed * normed_term)


def slot_of(place, block, y_rel):
    return place[block] * 8 + y_rel * 4 + place[GROUPS + block]


def softmax(scores):
    exponents = jnp.exp(scores - jnp.max(scores, axis=-1, keepdims=True))
    return exponents / jnp.sum(exponents, axis=-1, keepdims=True)


def block_mask(lengths, first_item):
    per_block = BLOCK // SEQ
    row = lax.broadcasted_iota(jnp.int32, (BLOCK, BLOCK), 0)
    column = lax.broadcasted_iota(jnp.int32, (BLOCK, BLOCK), 1)
    row_item, column_item = lax.shift_right_logical(row, 6), lax.shift_right_logical(column, 6)
    slot = column - column_item * SEQ
    limit = jnp.zeros((BLOCK, BLOCK), jnp.int32)
    for item in range(per_block):
        limit = jnp.where(column_item == item, lengths[first_item + item] + QUERIES, limit)
    return (row_item == column_item) & (slot < limit)


def self_forward_kernel(
    place,
    lengths,
    hidden,
    begin_own,
    begin_other,
    first_in,
    qkv,
    heads,
    w_qkv,
    w_cross,
    w_self_out,
    w_cross_out,
    norm,
    self_rows,
    cross_rows,
):
    rows, features = hidden.shape
    width = features // MODEL
    block_rows = features // GROUPS
    out_rows = width // GROUPS
    half, part = block_rows // 2, begin_own.shape[1] // 2
    norm_sum = jnp.zeros((NORM_ROWS, features), F32)
    for block in range(GROUPS):
        pieces = []
        for model in range(MODEL):
            side, y_rel = divmod(model, 2)
            source, slot = (begin_own, begin_other)[side], slot_of(place, block, y_rel)
            pieces.append(
                jnp.concatenate(
                    [source[slot, :half, :], source[slot, part : part + half, :]], axis=0
                )
            )
            cross_part = source[slot, half:part, :].astype(F32)
            self_part = source[slot, part + half :, :].astype(F32)
            begin = model * width + block * out_rows
            cross_rows[begin : begin + out_rows, :] = cross_part[:out_rows]
            self_rows[begin : begin + out_rows, :] = self_part[:out_rows]
            norm_sum = norm_sum + self_part[out_rows:]
        begin = block * block_rows
        for kind in range(4):
            joined = jnp.concatenate(
                [piece[:, kind * width : (kind + 1) * width] for piece in pieces], axis=1
            )
            if kind < 3:
                w_qkv[begin : begin + block_rows, kind * features : (kind + 1) * features] = joined
            else:
                w_cross[begin : begin + block_rows, :] = joined
    norm[...] = norm_sum
    w_self_out[...] = self_rows[...].astype(BF16)
    w_cross_out[...] = cross_rows[...].astype(BF16)
    tokens = hidden[...]
    for kind in range(3):
        columns = slice(kind * features, (kind + 1) * features)
        qkv[:, columns] = dot_nn(tokens, w_qkv[:, columns]).astype(BF16)
    scale = HEAD ** (-0.5)
    for begin in range(0, rows, BLOCK):
        span = slice(begin, begin + BLOCK)
        mask = block_mask(lengths, begin // SEQ)
        for pair in range(features // (2 * HEAD)):
            results = []
            for head in (2 * pair, 2 * pair + 1):
                parts = [
                    qkv[span, kind * features + head * HEAD : kind * features + (head + 1) * HEAD]
                    for kind in range(3)
                ]
                scores = jnp.where(mask, dot_nt(parts[0], parts[1]) * scale, MASK_VALUE)
                results.append(dot_nn(softmax(scores).astype(BF16), parts[2]).astype(BF16))
            heads[span, pair * 2 * HEAD : (pair + 1) * 2 * HEAD] = jnp.concatenate(results, axis=1)
    first_in[...] = tokens.astype(F32) + dot_nn(heads[...], w_self_out[...])


def assemble_image(place, image_own, image_other, weight):
    block_rows = image_own.shape[1]
    width = image_own.shape[2] // 2
    features = width * MODEL
    for block in range(GROUPS):
        pieces = []
        for model in range(MODEL):
            side, y_rel = divmod(model, 2)
            pieces.append((image_own, image_other)[side][slot_of(place, block, y_rel)])
        begin = block * block_rows
        for kind in range(2):
            weight[begin : begin + block_rows, kind * features : (kind + 1) * features] = (
                jnp.concatenate(
                    [piece[:, kind * width : (kind + 1) * width] for piece in pieces], axis=1
                )
            )


def image_forward_kernel(place, feats, image_own, image_other, key_values, weight):
    @pl.when(pl.program_id(0) == 0)
    def _():
        assemble_image(place, image_own, image_other, weight)

    patches = feats.shape[1]
    key_values[:patches, :] = dot_nn(feats[0], weight[...]).astype(BF16)
    key_values[patches:, :] = jnp.zeros((SLOT - patches, weight.shape[1]), BF16)


def head_rows(values, head_mask):
    stacked = jnp.concatenate([values] * (WIDE // HEAD), axis=0)
    return jnp.where(head_mask, stacked, jnp.zeros_like(stacked))


def fold_heads(values, head_mask):
    kept = jnp.where(head_mask, values, 0.0)
    count = WIDE // HEAD
    size = values.shape[0] // count
    total = kept[:size]
    for index in range(1, count):
        total = total + kept[index * size : (index + 1) * size]
    return total


def query_head_mask():
    shape = (QUERIES * (WIDE // HEAD), WIDE)
    row = lax.broadcasted_iota(jnp.int32, shape, 0)
    column = lax.broadcasted_iota(jnp.int32, shape, 1)
    return lax.shift_right_logical(row, 5) == lax.shift_right_logical(column, 6)


def patch_softmax(queries, keys):
    scores = dot_nt(queries, keys) * HEAD ** (-0.5)
    column = lax.broadcasted_iota(jnp.int32, scores.shape, 1)
    return softmax(jnp.where(column < PATCHES, scores, MASK_VALUE))


def query_rows(values):
    items = values.shape[0] // SEQ
    return jnp.concatenate(
        [values[item * SEQ : item * SEQ + QUERIES] for item in range(items)], axis=0
    )


def cross_forward_kernel(first_in, norm, w_cross, w_cross_out, key_values, second_in, queries, heads):
    features = first_in.shape[1]
    items = key_values.shape[0] // SLOT
    normed, _ = normalise(query_rows(first_in[...]))
    one_query = normed * norm[0:1, :] + norm[1:2, :]
    queries[...] = dot_nn(one_query.astype(BF16), w_cross[...]).astype(BF16)
    head_mask = query_head_mask()

    @pl.loop(0, items)
    def _(item):
        span = pl.ds(pl.multiple_of(item * QUERIES, QUERIES), QUERIES)
        rows = pl.ds(pl.multiple_of(item * SLOT, 16), SLOT)
        for begin in range(0, features, WIDE):
            columns = slice(begin, begin + WIDE)
            value_columns = slice(features + begin, features + begin + WIDE)
            probs = patch_softmax(head_rows(queries[span, columns], head_mask), key_values[rows, columns])
            mixed = dot_nn(probs.astype(BF16), key_values[rows, value_columns])
            heads[span, columns] = fold_heads(mixed, head_mask).astype(BF16)

    second_in[...] = one_query + dot_nn(heads[...], w_cross_out[...])


def gelu_cumulative(inputs):
    return 0.5 * (1.0 + lax.erf(inputs * 0.7071067811865476))


def feed_kernel(
    place,
    lengths,
    first_in,
    second_in,
    norm,
    out_grad,
    feed_own,
    feed_other,
    block_out,
    two_grad,
    keep,
    send,
    norm_grads,
    w_up,
    w_down,
    two_rows,
    pre_act,
    up_sem,
    down_sem,
):
    rows, features = first_in.shape
    items = rows // SEQ
    hidden_width = feed_own.shape[2]
    piece_rows = feed_own.shape[1] // 2
    half = 2 * hidden_width
    for model in range(MODEL):
        side, y_rel = divmod(model, 2)
        source = (feed_own, feed_other)[side]
        for block in range(GROUPS):
            slot = slot_of(place, block, y_rel)
            pltpu.make_async_copy(
                source.at[slot, :piece_rows, :],
                w_up.at[model, pl.ds(block * piece_rows, piece_rows), :],
                up_sem.at[model],
            ).start()
            pltpu.make_async_copy(
                source.at[slot, piece_rows:, :],
                w_down.at[model, pl.ds(block * piece_rows, piece_rows), :],
                down_sem.at[model],
            ).start()
    normed_one, _ = normalise(first_in[...])
    after_one = normed_one * norm[0:1, :] + norm[1:2, :]
    normed_two, _ = normalise(second_in[...])
    after_two = normed_two * norm[2:3, :] + norm[3:4, :]
    for item in range(items):
        begin = item * SEQ
        two_rows[begin : begin + QUERIES, :] = after_two[item * QUERIES : (item + 1) * QUERIES]
        two_rows[begin + QUERIES : begin + SEQ, :] = after_one[begin + QUERIES : begin + SEQ]
    feed_in = two_rows[...].astype(BF16)
    send[:, 2 * half : 2 * half + features] = feed_in
    third_in = two_rows[...]
    for model in range(MODEL):
        target, y_rel = (keep, send)[model // 2], model % 2
        pltpu.make_async_copy(w_up.at[model], w_up.at[model], up_sem.at[model]).wait()
        pre = dot_nn(feed_in, w_up[model])
        pre_act[:, model * hidden_width : (model + 1) * hidden_width] = pre
        act = (pre * gelu_cumulative(pre)).astype(BF16)
        target[:, y_rel * hidden_width : (y_rel + 1) * hidden_width] = act
        pltpu.make_async_copy(w_down.at[model], w_down.at[model], down_sem.at[model]).wait()
        third_in = third_in + dot_nn(act, w_down[model])
    normed, inverse = normalise(third_in)
    block_out[...] = (normed * norm[4:5, :] + norm[5:6, :]).astype(BF16)
    position = lax.broadcasted_iota(jnp.int32, (SEQ, features), 0)
    slope = jnp.concatenate(
        [
            jnp.where(
                position < lengths[item] + QUERIES,
                out_grad[item * SEQ : (item + 1) * SEQ, :].astype(F32),
                0.0,
            )
            for item in range(items)
        ],
        axis=0,
    )
    norm_grads[...] = jnp.zeros_like(norm_grads)
    norm_grads[4:5, :] = jnp.sum(slope * normed, axis=0, keepdims=True)
    norm_grads[5:6, :] = jnp.sum(slope, axis=0, keepdims=True)
    third_grad = norm_back(slope, normed, inverse, norm[4:5, :])
    grad_rows = third_grad.astype(BF16)
    send[:, 2 * half + features :] = grad_rows
    total = third_grad
    for model in range(MODEL):
        target, y_rel = (keep, send)[model // 2], model % 2
        pre = pre_act[:, model * hidden_width : (model + 1) * hidden_width]
        density = jnp.exp(-0.5 * pre * pre) * 0.3989422804014327
        slope_part = gelu_cumulative(pre) + pre * density
        grad_pre = (dot_nt(grad_rows, w_down[model]) * slope_part).astype(BF16)
        target[:, half + y_rel * hidden_width : half + (y_rel + 1) * hidden_width] = grad_pre
        total = total + dot_nt(grad_pre, w_up[model])
    two_grad[...] = total


def put_left(place, block, y_rel, keep, send, value):
    for along_x, target in ((0, keep), (1, send)):

        @pl.when(place[block] == along_x)
        def _(target=target):
            target[y_rel, place[GROUPS + block]] = value


def put_right(place, block, y_rel, keep, send, value):
    (keep, send)[y_rel][place[block], place[GROUPS + block]] = value


def feed_grad_kernel(
    place, hidden, rows, hidden_other, rows_other, left_keep, left_send, right_keep, right_send
):
    piece_rows = left_keep.shape[2]
    kind, y_step = pl.program_id(0), pl.program_id(1)

    @pl.when(kind == 0)
    def _():
        grad_up = dot_tn(rows[...], hidden[...])
        grad_up = (grad_up + dot_tn(rows_other[...], hidden_other[...])).astype(BF16)
        for block in range(GROUPS):
            span = slice(block * piece_rows, (block + 1) * piece_rows)
            put_left(place, block, y_step, left_keep, left_send, grad_up[span])

    for y_rel in range(2):

        @pl.when((kind == 1) & (y_step == y_rel))
        def _(y_rel=y_rel):
            grad_down = dot_tn(hidden[...], rows[...])
            grad_down = (grad_down + dot_tn(hidden_other[...], rows_other[...])).astype(BF16)
            for block in range(GROUPS):
                span = slice(block * piece_rows, (block + 1) * piece_rows)
                put_right(place, block, y_rel, right_keep, right_send, grad_down[span])


def cross_backward_kernel(
    two_grad,
    first_in,
    second_in,
    norm,
    w_cross,
    w_cross_out,
    queries,
    heads,
    key_values,
    norm_grads_in,
    keep,
    send,
    one_query_grad,
    norm_grads,
    head_grads,
    query_grads,
    grad_rows,
):
    features = first_in.shape[1]
    half = features // 2
    count = queries.shape[0]
    step = pl.program_id(0)
    items = pl.num_programs(0) - 3
    scale = HEAD ** (-0.5)

    @pl.when(step == 0)
    def _():
        two_query = query_rows(two_grad[...])
        normed, inverse = normalise(second_in[...])
        norm_grads[...] = norm_grads_in[...]
        norm_grads[2:3, :] = jnp.sum(two_query * normed, axis=0, keepdims=True)
        norm_grads[3:4, :] = jnp.sum(two_query, axis=0, keepdims=True)
        second_grad = norm_back(two_query, normed, inverse, norm[2:3, :])
        one_query_grad[...] = second_grad
        grad_rows[...] = second_grad.astype(BF16)
        head_grads[...] = dot_nt(grad_rows[...], w_cross_out[...]).astype(BF16)

    @pl.when(step < items)
    def _():
        head_mask = query_head_mask()
        span = pl.ds(pl.multiple_of(step * QUERIES, QUERIES), QUERIES)
        for begin in range(0, features, WIDE):
            columns = slice(begin, begin + WIDE)
            value_columns = slice(features + begin, features + begin + WIDE)
            expanded = head_rows(queries[span, columns], head_mask)
            expanded_grad = head_rows(head_grads[span, columns], head_mask)
            keys = key_values[:, columns]
            probs = patch_softmax(expanded, keys)
            grad_probs = dot_nt(expanded_grad, key_values[:, value_columns])
            inner = jnp.sum(grad_probs * probs, axis=-1, keepdims=True)
            grad_scores = (probs * (grad_probs - inner)).astype(BF16)
            grad_values = dot_tn(probs.astype(BF16), expanded_grad).astype(BF16)
            grad_keys = (dot_tn(grad_scores, expanded) * scale).astype(BF16)
            query_grads[span, columns] = (
                fold_heads(dot_nn(grad_scores, keys), head_mask) * scale
            ).astype(BF16)
            for part in range(0, WIDE, WIDE // 2):
                side, place_at = divmod(begin + part, half)
                target, lanes = (keep, send)[side], slice(part, part + WIDE // 2)
                target[:, place_at : place_at + WIDE // 2] = grad_keys[:, lanes]
                place_at += half
                target[:, place_at : place_at + WIDE // 2] = grad_values[:, lanes]

    @pl.when(step >= items)
    def _():
        for target in (keep, send):
            target[count:, :] = jnp.zeros((SLOT - count, features), BF16)

    @pl.when(step == items)
    def _():
        normed_one, _ = normalise(query_rows(first_in[...]))
        query_in = (normed_one * norm[0:1, :] + norm[1:2, :]).astype(BF16)
        for target in (keep, send):
            target[:count, :] = query_in

    @pl.when(step == items + 1)
    def _():
        for target in (keep, send):
            target[:count, :] = grad_rows[...]

    @pl.when(step == items + 2)
    def _():
        for side, target in enumerate((keep, send)):
            columns = slice(side * half, (side + 1) * half)
            target[:count, :half] = query_grads[:, columns]
            target[:count, half:] = heads[:, columns]
        one_query_grad[...] += dot_nt(query_grads[...], w_cross[...])


def image_grad_kernel(
    count,
    place,
    feats,
    keep_rows,
    other_rows,
    keep,
    other,
    left_keep,
    left_send,
    right_keep,
    right_send,
    total,
    spread,
):
    features = keep.shape[1]
    half = features // 2
    width = half // 2
    image_rows = feats.shape[2] // GROUPS
    image_half = image_rows // 2
    block_rows = features // GROUPS
    out_rows = width // GROUPS
    split = left_keep.shape[2]
    step, steps = pl.program_id(0), pl.num_programs(0)

    @pl.when(step == 0)
    def _():
        spread[...] = jnp.zeros_like(spread)

    for item in range(feats.shape[0]):
        spread[item * SLOT : item * SLOT + feats.shape[1], :] = feats[item]

    @pl.when(step == 0)
    def _():
        total[...] = dot_tn(spread[...], keep_rows[...])

    @pl.when((step > 0) & (step < steps // 2))
    def _():
        total[...] += dot_tn(spread[...], keep_rows[...])

    @pl.when(step >= steps // 2)
    def _():
        total[...] += dot_tn(spread[...], other_rows[...])

    @pl.when(step == steps - 1)
    def _():
        inputs, slopes = slice(0, count), slice(SLOT, SLOT + count)
        parts = slice(2 * SLOT, 2 * SLOT + count)
        grad_query = dot_tn(keep[inputs, :], keep[parts, :half]) + dot_tn(
            other[inputs, :], other[parts, :half]
        )
        grad_out = dot_tn(keep[parts, half:], keep[slopes, :]) + dot_tn(
            other[parts, half:], other[slopes, :]
        )
        for block in range(GROUPS):
            for y_rel in range(2):
                columns = slice(y_rel * width, (y_rel + 1) * width)
                image_part = [
                    total[
                        begin : begin + image_half,
                        kind + y_rel * width : kind + (y_rel + 1) * width,
                    ]
                    for begin in (block * image_rows, block * image_rows + image_half)
                    for kind in (0, half)
                ]
                begin = block * block_rows
                cross_part = [
                    grad_query[begin + part * out_rows : begin + (part + 1) * out_rows, columns]
                    for part in range(MODEL)
                ]
                begin = y_rel * width + block * out_rows
                piece = jnp.concatenate(
                    [
                        jnp.concatenate(image_part, axis=1),
                        jnp.concatenate(cross_part, axis=1),
                        grad_out[begin : begin + out_rows],
                    ],
                    axis=0,
                )
                put_left(place, block, y_rel, left_keep, left_send, piece[:split].astype(BF16))
                put_right(place, block, y_rel, right_keep, right_send, piece[split:].astype(BF16))


def self_backward_kernel(
    lengths,
    one_query_grad,
    two_grad,
    first_in,
    norm,
    hidden,
    qkv,
    heads,
    w_qkv,
    w_self_out,
    norm_grads_in,
    input_grad,
    keep,
    send,
    norm_total,
    one_grad,
    head_grads,
    grad_qkv,
):
    rows, features = hidden.shape
    items = rows // SEQ
    half = features // 2
    for item in range(items):
        begin = item * SEQ
        one_grad[begin : begin + QUERIES, :] = one_query_grad[
            item * QUERIES : (item + 1) * QUERIES, :
        ]
        one_grad[begin + QUERIES : begin + SEQ, :] = two_grad[begin + QUERIES : begin + SEQ, :]
    normed, inverse = normalise(first_in[...])
    gradient = one_grad[...]
    norm_sum = norm_grads_in[...] + jnp.concatenate(
        [
            jnp.sum(gradient * normed, axis=0, keepdims=True),
            jnp.sum(gradient, axis=0, keepdims=True),
            jnp.zeros((NORM_ROWS - 2, features), F32),
        ],
        axis=0,
    )
    norm_total[...] = norm_sum
    first_grad = norm_back(gradient, normed, inverse, norm[0:1, :])
    one_grad[...] = first_grad
    grad_rows = first_grad.astype(BF16)
    head_grads[...] = dot_nt(grad_rows, w_self_out[...]).astype(BF16)
    scale = HEAD ** (-0.5)
    for begin in range(0, rows, BLOCK):
        span = slice(begin, begin + BLOCK)
        mask = block_mask(lengths, begin // SEQ)
        for pair in range(features // (2 * HEAD)):
            results = [[], [], []]
            for head in (2 * pair, 2 * pair + 1):
                queries, key_rows, value_rows = [
                    qkv[span, kind * features + head * HEAD : kind * features + (head + 1) * HEAD]
                    for kind in range(3)
                ]
                head_grad = head_grads[span, head * HEAD : (head + 1) * HEAD]
                probs = softmax(jnp.where(mask, dot_nt(queries, key_rows) * scale, MASK_VALUE))
                grad_probs = dot_nt(head_grad, value_rows)
                inner = jnp.sum(grad_probs * probs, axis=-1, keepdims=True)
                grad_scores = (probs * (grad_probs - inner)).astype(BF16)
                results[0].append((dot_nn(grad_scores, key_rows) * scale).astype(BF16))
                results[1].append((dot_tn(grad_scores, queries) * scale).astype(BF16))
                results[2].append(dot_tn(probs.astype(BF16), head_grad).astype(BF16))
            for kind in range(3):
                first = kind * features + pair * 2 * HEAD
                grad_qkv[span, first : first + 2 * HEAD] = jnp.concatenate(results[kind], axis=1)
    total = one_grad[...]
    for kind in range(3):
        columns = slice(kind * features, (kind + 1) * features)
        total = total + dot_nt(grad_qkv[:, columns], w_qkv[:, columns])
        first = kind * features
        keep[:, kind * half : (kind + 1) * half] = grad_qkv[:, first : first + half]
        send[:rows, kind * half : (kind + 1) * half] = grad_qkv[:, first + half : first + features]
    input_grad[...] = total.astype(BF16)
    keep[:, 3 * half :] = heads[:, :half]
    send[:rows, 3 * half : 4 * half] = heads[:, half:]
    send[:rows, 4 * half : 6 * half] = hidden[...]
    send[:rows, 6 * half :] = grad_rows
    send[rows:, :] = jnp.zeros((send.shape[0] - rows, send.shape[1]), BF16)
    send[rows : rows + 16, :features] = jnp.concatenate(
        [norm_sum, jnp.zeros_like(norm_sum)], axis=0
    ).astype(BF16)


def self_grad_kernel(
    place, keep, send, other, norm_total, left_keep, left_send, right_keep, right_send
):
    features = norm_total.shape[1]
    rows = keep.shape[0]
    half = features // 2
    width = half // 2
    block_rows = features // GROUPS
    out_rows = width // GROUPS
    split = left_keep.shape[2]
    inputs, slopes = slice(4 * half, 6 * half), slice(6 * half, 8 * half)
    columns = slice(0, 3 * half)
    grad_in = dot_tn(send[:rows, inputs], keep[:, columns])
    grad_in = grad_in + dot_tn(other[:rows, inputs], other[:rows, columns])
    columns = slice(3 * half, 4 * half)
    grad_out = dot_tn(keep[:, columns], send[:rows, slopes])
    grad_out = grad_out + dot_tn(other[:rows, columns], other[:rows, slopes])
    norm_rows = norm_total[...] + other[rows : rows + 16, :features].astype(F32)[:NORM_ROWS]
    for block in range(GROUPS):
        span = slice(block * block_rows, (block + 1) * block_rows)
        for y_rel in range(2):
            pieces = [
                grad_in[span, kind * half + y_rel * width : kind * half + (y_rel + 1) * width]
                for kind in range(3)
            ]
            begin = y_rel * width + block * out_rows
            out_part = grad_out[begin : begin + out_rows]
            pieces.append(
                jnp.concatenate(
                    [out_part[:, part * width : (part + 1) * width] for part in range(MODEL)],
                    axis=0,
                )
            )
            piece = jnp.concatenate([jnp.concatenate(pieces, axis=1), norm_rows], axis=0)
            put_left(place, block, y_rel, left_keep, left_send, piece[:split].astype(BF16))
            put_right(place, block, y_rel, right_keep, right_send, piece[split:].astype(BF16))


def adam_step(weight, moment_one, moment_two, gradient, decay_rate):
    moment_one = BETA_ONE * moment_one + (1.0 - BETA_ONE) * gradient
    moment_two = BETA_TWO * moment_two + (1.0 - BETA_TWO) * gradient * gradient
    update = (
        moment_one
        / (1.0 - BETA_ONE**STEP)
        / (jnp.sqrt(moment_two / (1.0 - BETA_TWO**STEP)) + ADAM_EPSILON)
        + decay_rate * weight
    )
    return moment_one, moment_two, update


def place_sums(target, sums):
    column = lax.broadcasted_iota(jnp.int32, (1, LANES), 1)
    rows = []
    for kind in range(2):
        row = jnp.zeros((1, LANES), F32)
        for index, pair in sums.items():
            row = jnp.where(column == index, pair[kind], row)
        rows.append(row)
    target[...] = jnp.concatenate(rows, axis=0)


def sum_pair(weight, update):
    return jnp.sum(weight * weight), jnp.sum(update * update)


def feed_update_kernel(
    gradient,
    up,
    up_moments,
    down,
    down_moments,
    up_next,
    down_next,
    up_update,
    down_update,
    squares,
):
    rows = up.shape[0]
    sums = {}
    for index, weight, moments, following, result, span in (
        (8, up, up_moments, up_next, up_update, slice(0, rows)),
        (9, down, down_moments, down_next, down_update, slice(rows, None)),
    ):
        following[0], following[1], update = adam_step(
            weight[...], moments[0], moments[1], gradient[span, :], DECAY_RATE
        )
        result[...] = update
        sums[index] = sum_pair(weight[...], update)
    place_sums(squares, sums)


def image_update_kernel(gradient, weight, moments, following, result, squares):
    width = weight.shape[2]
    half = weight.shape[1] // 2
    sums = {}
    for kind in range(2):
        parts = []
        for part in range(2):
            span = slice(part * half, (part + 1) * half)
            lanes = slice((2 * part + kind) * width, (2 * part + kind + 1) * width)
            following[0, kind, span, :], following[1, kind, span, :], update = adam_step(
                weight[kind, span, :],
                moments[0, kind, span, :],
                moments[1, kind, span, :],
                gradient[:half, lanes],
                DECAY_RATE,
            )
            result[kind, span, :] = update
            parts.append(sum_pair(weight[kind, span, :], update))
        sums[6 + kind] = tuple(left + right for left, right in zip(*parts))
    place_sums(squares, sums)


def last_update_kernel(
    gradient,
    cross_gradient,
    norm_gradient,
    inward,
    inward_moments,
    outward,
    outward_moments,
    norm,
    norm_moments,
    inward_next,
    outward_next,
    norm_next,
    inward_update,
    outward_update,
    norm_update,
    squares,
):
    own_in, width = inward.shape[1:]
    own_out = outward.shape[1]
    cross_rows = cross_gradient.shape[0] - 2 * own_out
    cross_query = cross_gradient[cross_rows : cross_rows + own_out, :]
    gradients = [gradient[:own_in, kind * width : (kind + 1) * width] for kind in range(3)]
    gradients.append(
        jnp.concatenate(
            [cross_query[:, part * width : (part + 1) * width] for part in range(MODEL)], axis=0
        )
    )
    sums = {}
    for kind in range(4):
        inward_next[0, kind], inward_next[1, kind], update = adam_step(
            inward[kind],
            inward_moments[0, kind],
            inward_moments[1, kind],
            gradients[kind],
            DECAY_RATE,
        )
        inward_update[kind] = update
        sums[kind] = sum_pair(inward[kind], update)
    folded = gradient[:own_in, 3 * width :]
    self_out = jnp.concatenate(
        [folded[part * own_out : (part + 1) * own_out] for part in range(MODEL)], axis=1
    )
    for kind, part in enumerate((self_out, cross_gradient[cross_rows + own_out :, :])):
        outward_next[0, kind], outward_next[1, kind], update = adam_step(
            outward[kind], outward_moments[0, kind], outward_moments[1, kind], part, DECAY_RATE
        )
        outward_update[kind] = update
        sums[4 + kind] = sum_pair(outward[kind], update)
    norm_next[0], norm_next[1], update = adam_step(
        norm[...], norm_moments[0], norm_moments[1], norm_gradient[...], 0.0
    )
    norm_update[...] = update
    for kind in range(norm.shape[0]):
        sums[10 + kind] = sum_pair(norm[kind : kind + 1, :], update[kind : kind + 1, :])
    place_sums(squares, sums)


def apply_kernel(squares, *refs):
    groups = len(refs) // 5
    weights, averages, updates = refs[:groups], refs[groups : 2 * groups], refs[2 * groups : 3 * groups]
    new_weights, new_averages = refs[3 * groups : 4 * groups], refs[4 * groups : 5 * groups]
    trust_out, norms_out = refs[5 * groups :]
    sums = jnp.sum(squares[...], axis=0)
    trust = jnp.sqrt(sums[0:1]) * lax.rsqrt(sums[1:2] + SQUARE_EPSILON)
    trust_out[...] = trust
    norms_out[...] = jnp.sqrt(sums)
    column = lax.broadcasted_iota(jnp.int32, trust.shape, 1)

    def ratio(index):
        return jnp.sum(jnp.where(column == index, trust, 0.0), axis=1, keepdims=True)

    index = 0
    for weight, average, update, new_weight, new_average in zip(
        weights, averages, updates, new_weights, new_averages
    ):
        if len(weight.shape) == 3:
            spans = list(range(weight.shape[0]))
        elif weight.shape[0] == 6:
            spans = [slice(row, row + 1) for row in range(6)]
        else:
            spans = [slice(None)]
        for span in spans:
            value = weight[span] - LEARN_RATE * ratio(index) * update[span]
            new_weight[span] = value
            new_average[span] = AVERAGE_RATE * average[span] + (1.0 - AVERAGE_RATE) * value
            index += 1


SCALARS = pl.BlockSpec(memory_space=pltpu.SMEM)
WHOLE = pl.BlockSpec(memory_space=pltpu.VMEM)
ANYWHERE = pl.BlockSpec(memory_space=pl.ANY)


def local_call(kernel, scalars, arrays, out_shapes, scratch, flops, name, limit, loose=()):
    size = sum(a.size * a.dtype.itemsize for a in (*arrays, *loose))
    size += sum(a.size * a.dtype.itemsize for a in out_shapes)
    return pl.pallas_call(
        kernel,
        out_shape=tuple(out_shapes),
        in_specs=[SCALARS] * len(scalars) + [WHOLE] * len(arrays) + [ANYWHERE] * len(loose),
        out_specs=tuple([WHOLE] * len(out_shapes)),
        scratch_shapes=scratch,
        compiler_params=pltpu.CompilerParams(vmem_limit_bytes=limit * MIB),
        cost_estimate=pl.CostEstimate(flops=flops, bytes_accessed=size, transcendentals=0),
        name=name,
    )(*scalars, *arrays, *loose)


def shape_of(*dims, dtype=BF16):
    return jax.ShapeDtypeStruct(dims, dtype)


def part_shapes(left_rows, right_rows, features):
    left, right = shape_of(2, 4, left_rows, features), shape_of(2, 4, right_rows, features)
    return left, left, right, right


def like(array):
    return jax.ShapeDtypeStruct(array.shape, array.dtype)


def update_call(kernel, arrays, moments, weights, name):
    shapes = [like(each) for each in (*moments, *weights)] + [shape_of(2, LANES, dtype=F32)]
    return local_call(kernel, (), arrays, shapes, [], 0, name, 20)


def apply_call(squares, weights, averages, updates):
    shapes = [like(each) for each in (*weights, *averages)]
    shapes += [shape_of(1, LANES, dtype=F32), shape_of(2, LANES, dtype=F32)]
    return local_call(
        apply_kernel, (), (squares, *weights, *averages, *updates), shapes, [], 0, "apply", 60
    )


class Direct:
    def __init__(self, dp, mp):
        self.count = dp * mp
        self.mp = mp
        self.depth = dp // 2
        index = lax.axis_index("dp")
        block = jnp.arange(GROUPS, dtype=jnp.int32)
        along_x = (block % 2) ^ (index % 2)
        along_z = (index // 2 - block // 2) % self.depth
        self.place = jnp.concatenate([along_x, along_z]).astype(jnp.int32)

    def hop(self, values, flip):
        return lax.ppermute(values, AXES, [(i, i ^ flip) for i in range(self.count)])

    def hop_core(self, values):
        return self.hop(values, 1)

    def hop_y(self, values):
        return self.hop(values, 2)

    def hop_x(self, values):
        return self.hop(values, self.mp)

    def hop_z(self, values, distance):
        step = 2 * self.mp * distance
        return lax.ppermute(values, AXES, [(i, (i + step) % self.count) for i in range(self.count)])

    def spread_z(self, piece):
        return jnp.stack([piece] + [self.hop_z(piece, step) for step in range(1, self.depth)])


    def spread_first(self, held, split):
        return self.hop_y(held[:, :split]), self.hop_x(held[:, split:])

    def join_first(self, held, split, others):
        return jnp.stack([held[:, :split], others[0]]), jnp.stack([held[:, split:], others[1]])

    def spread_second(self, parts):
        return self.hop_x(parts[0]), self.hop_y(parts[1])

    def join_second(self, parts, others):
        left = jnp.stack([parts[0], others[0]])
        right = jnp.stack([parts[1], others[1]]).transpose(1, 0, 2, 3, 4)
        whole = jnp.concatenate([left, right], axis=3)
        return whole.reshape(SLOTS, *whole.shape[3:])


    def fold_first(self, grads):
        return self.hop_x(grads[1]), self.hop_y(grads[3])

    def fold_second(self, grads, others):
        return (
            self.hop_y(total([grads[0][1], others[0][1]])),
            self.hop_x(total([grads[2][1], others[1][1]])),
        )

    def kept(self, grads, others, last):
        return [[grads[2 * side][0], others[side][0], last[side]] for side in range(2)]

    def fold_z(self, sides):
        return [
            self.hop_z(total(*[[part[step] for part in parts] for parts in sides]), -step)
            for step in range(1, self.depth)
        ]

    def ring_z(self, sides, step, carried=None):
        addends = [[part[step] for part in parts] for parts in sides]
        own = total(*addends, dtype=F32)
        if carried is not None:
            own = own + carried.astype(F32)
        return self.hop_z(own.astype(BF16), 1)

    def finish(self, sides, others):
        own = total(*[[part[0] for part in parts] for parts in sides], dtype=F32)
        return total([own, *others], dtype=F32)


def total(*sides, dtype=BF16):
    sums = []
    for parts in sides:
        result = parts[0].astype(F32)
        for part in parts[1:]:
            result = result + part.astype(F32)
        sums.append(result.astype(dtype))
    return sums[0] if len(sums) == 1 else jnp.concatenate(sums, axis=0)


class Plain:
    def __init__(self, dp, mp):
        self.dp = dp
        self.mp = mp
        self.side = lax.axis_index("mp") // 2
        block = jnp.arange(GROUPS, dtype=jnp.int32)
        self.place = jnp.concatenate([block % 2, block // 2]).astype(jnp.int32)

    def hop_core(self, values):
        count = self.dp * self.mp
        return lax.ppermute(values, AXES, [(i, i ^ 2) for i in range(count)])

    def collect(self, piece):
        rows, width = piece.shape
        blocks = lax.all_gather(piece, AXES, axis=0).reshape(self.dp, self.mp, rows, width)
        rows = rows * self.dp // GROUPS
        blocks = blocks.transpose(1, 0, 2, 3).reshape(2, 2, 4, 2, rows, width)
        blocks = blocks.transpose(0, 3, 1, 2, 4, 5).reshape(2, SLOTS, rows, width)
        return jnp.where(self.side == 0, blocks, blocks[::-1])

    def joined(self, grads):
        left = jnp.stack(grads[:2])
        right = jnp.stack(grads[2:]).transpose(1, 0, 2, 3, 4)
        return jnp.concatenate([left, right], axis=3)

    def scatter(self, own):
        rows, width = own.shape[3:]
        own = own.transpose(1, 2, 0, 3, 4).reshape(1, 2, GROUPS, rows, width)
        both = jnp.zeros((2, *own.shape[1:]), F32)
        both = lax.dynamic_update_slice_in_dim(both, own.astype(F32), self.side, 0)
        both = both.reshape(self.mp, self.dp, rows * GROUPS // self.dp, width)
        both = both.transpose(1, 0, 2, 3).reshape(-1, width)
        return lax.psum_scatter(both, AXES, scatter_dimension=0, tiled=True)


def tie(*arrays):
    return lax.optimization_barrier(arrays)


def padded(feats):
    pad = ((0, 0), (0, SLOT - PATCHES), (0, 0))
    return jnp.pad(feats, pad).reshape(-1, feats.shape[2])


def tie(*arrays):
    return lax.optimization_barrier(arrays)


def add(left_side, right_side):
    return (left_side.astype(F32) + right_side.astype(F32)).astype(BF16)


def self_forward(place, lengths, hidden, begin):
    rows, features = hidden.shape
    return local_call(
        self_forward_kernel,
        (place, lengths),
        (hidden, *begin),
        (
            shape_of(rows, features, dtype=F32),
            shape_of(rows, 3 * features),
            shape_of(rows, features),
            shape_of(features, 3 * features),
            shape_of(features, features),
            shape_of(features, features),
            shape_of(features, features),
            shape_of(NORM_ROWS, features, dtype=F32),
        ),
        [pltpu.VMEM((features, features), F32), pltpu.VMEM((features, features), F32)],
        10 * rows * features * features,
        "self_forward",
        28,
    )


def image_forward(place, feats, image):
    items, patches, encoded = feats.shape
    items = items // 2
    rows = items * SLOT
    features = image[0].shape[2] // 2 * MODEL
    piece_spec = pl.BlockSpec(image[0].shape, lambda item, where: (0, 0, 0))
    return pl.pallas_call(
        image_forward_kernel,
        out_shape=shape_of(rows, 2 * features),
        grid_spec=pltpu.PrefetchScalarGridSpec(
            num_scalar_prefetch=1,
            grid=(items,),
            in_specs=[
                pl.BlockSpec(
                    (1, patches, encoded), lambda item, where: (where[2 * GROUPS] + item, 0, 0)
                ),
                piece_spec,
                piece_spec,
            ],
            out_specs=pl.BlockSpec((SLOT, 2 * features), lambda item, where: (item, 0)),
            scratch_shapes=[pltpu.VMEM((encoded, 2 * features), BF16)],
        ),
        compiler_params=pltpu.CompilerParams(vmem_limit_bytes=24 * MIB),
        cost_estimate=pl.CostEstimate(
            flops=4 * rows * encoded * features,
            bytes_accessed=2 * rows * (encoded + 2 * features) + 4 * encoded * features,
            transcendentals=0,
        ),
        name="image_forward",
    )(place, feats, *image)


def cross_forward(first_in, norm, w_cross, w_cross_out, key_values):
    features = first_in.shape[1]
    queries = first_in.shape[0] // SEQ * QUERIES
    return local_call(
        cross_forward_kernel,
        (),
        (first_in, norm, w_cross, w_cross_out, key_values),
        (
            shape_of(queries, features, dtype=F32),
            shape_of(queries, features),
            shape_of(queries, features),
        ),
        [],
        4 * queries * features * features,
        "cross_forward",
        18,
    )


def feed(place, lengths, first_in, second_in, norm, out_grad, weights):
    rows, features = first_in.shape
    width = weights[0].shape[2]
    return local_call(
        feed_kernel,
        (place, lengths),
        (first_in, second_in, norm, out_grad),
        (
            shape_of(rows, features),
            shape_of(rows, features, dtype=F32),
            shape_of(rows, 4 * width),
            shape_of(rows, 4 * width + 2 * features),
            shape_of(NORM_ROWS, features, dtype=F32),
        ),
        [
            pltpu.VMEM((MODEL, features, width), BF16),
            pltpu.VMEM((MODEL, width, features), BF16),
            pltpu.VMEM((rows, features), F32),
            pltpu.VMEM((rows, MODEL * width), F32),
            pltpu.SemaphoreType.DMA((MODEL,)),
            pltpu.SemaphoreType.DMA((MODEL,)),
        ],
        8 * rows * features * MODEL * width,
        "feed",
        40,
        loose=weights,
    )


def feed_grad(place, keep, send, other, rows):
    features = (send.shape[1] - keep.shape[1]) // 2
    width = keep.shape[1] // 4
    tokens = keep.shape[0]
    shapes = part_shapes(rows, rows, features)
    hidden_spec = pl.BlockSpec(
        (tokens, width), lambda kind, y_step, where: (0, 2 * (1 - kind) + y_step)
    )
    row_spec = pl.BlockSpec(
        (tokens, features), lambda kind, y_step, where: (0, 4 * width // features + kind)
    )
    return pl.pallas_call(
        feed_grad_kernel,
        out_shape=shapes,
        grid_spec=pltpu.PrefetchScalarGridSpec(
            num_scalar_prefetch=1,
            grid=(2, 2),
            in_specs=[hidden_spec, row_spec, hidden_spec, row_spec],
            out_specs=[fixed(shape.shape) for shape in shapes],
        ),
        compiler_params=pltpu.CompilerParams(vmem_limit_bytes=36 * MIB),
        cost_estimate=pl.CostEstimate(
            flops=4 * tokens * features * keep.shape[1],
            bytes_accessed=24 * tokens * features,
            transcendentals=0,
        ),
        name="feed_grad",
    )(place, keep, send, other, other)


def fixed(shape):
    return pl.BlockSpec(shape, lambda *_: (0,) * len(shape))


def cross_backward(
    two_grad,
    first_in,
    second_in,
    norm,
    w_cross,
    w_cross_out,
    queries,
    heads,
    key_values,
    norm_grads,
):
    features = first_in.shape[1]
    count = queries.shape[0]
    items = key_values.shape[0] // SLOT
    rows = (items + 3) * SLOT
    arrays = (
        two_grad,
        first_in,
        second_in,
        norm,
        w_cross,
        w_cross_out,
        queries,
        heads,
        key_values,
        norm_grads,
    )
    specs = [fixed(each.shape) for each in arrays]
    specs[8] = pl.BlockSpec(
        (SLOT, 2 * features), lambda item: (jnp.minimum(item, items - 1), 0)
    )
    row_spec = pl.BlockSpec((SLOT, features), lambda item: (item, 0))
    return pl.pallas_call(
        cross_backward_kernel,
        grid=(items + 3,),
        out_shape=(
            shape_of(rows, features),
            shape_of(rows, features),
            shape_of(count, features, dtype=F32),
            shape_of(NORM_ROWS, features, dtype=F32),
        ),
        in_specs=specs,
        out_specs=(row_spec, row_spec, fixed((count, features)), fixed((NORM_ROWS, features))),
        scratch_shapes=[pltpu.VMEM((count, features), BF16)] * 3,
        compiler_params=pltpu.CompilerParams(vmem_limit_bytes=36 * MIB),
        cost_estimate=pl.CostEstimate(
            flops=20 * count * features * features,
            bytes_accessed=12 * rows * features,
            transcendentals=0,
        ),
        name="cross_backward",
    )(*arrays)


def image_grad(place, feats, keep, other):
    features = keep.shape[1]
    items, patches, encoded = feats.shape
    rows = items * SLOT
    piece = encoded // GROUPS // 2 + 2 * (features // MODEL // GROUPS)
    steps = 4
    block = rows // steps
    last = steps // 2 - 1
    shapes = part_shapes(IMAGE_SPLIT, piece - IMAGE_SPLIT, features)
    out_specs = [pl.BlockSpec(shape.shape, lambda step, where: (0, 0, 0, 0)) for shape in shapes]
    rest = pl.BlockSpec((block, features), lambda step, where: (steps // 2, 0))
    return pl.pallas_call(
        functools.partial(image_grad_kernel, items // 2 * QUERIES),
        out_shape=shapes,
        grid_spec=pltpu.PrefetchScalarGridSpec(
            num_scalar_prefetch=1,
            grid=(steps,),
            in_specs=[
                pl.BlockSpec(
                    (items // steps, patches, encoded),
                    lambda step, where: (
                        (step + where[2 * GROUPS] // (items // steps)) % steps,
                        0,
                        0,
                    ),
                ),
                pl.BlockSpec((block, features), lambda step, where: (jnp.minimum(step, last), 0)),
                pl.BlockSpec(
                    (block, features), lambda step, where: (jnp.maximum(step - last - 1, 0), 0)
                ),
                rest,
                rest,
            ],
            out_specs=out_specs,
            scratch_shapes=[pltpu.VMEM((encoded, features), F32), pltpu.VMEM((block, encoded), BF16)],
        ),
        compiler_params=pltpu.CompilerParams(vmem_limit_bytes=34 * MIB),
        cost_estimate=pl.CostEstimate(
            flops=2 * rows * encoded * features,
            bytes_accessed=2 * rows * (encoded + features),
            transcendentals=0,
        ),
        name="image_grad",
    )(place, feats, keep, other, keep, other)


def self_backward(
    lengths,
    one_query_grad,
    two_grad,
    first_in,
    norm,
    hidden,
    qkv,
    heads,
    w_qkv,
    w_self_out,
    norm_grads,
):
    rows, features = hidden.shape
    return local_call(
        self_backward_kernel,
        (lengths,),
        (
            one_query_grad,
            two_grad,
            first_in,
            norm,
            hidden,
            qkv,
            heads,
            w_qkv,
            w_self_out,
            norm_grads,
        ),
        (
            shape_of(rows, features),
            shape_of(rows, 2 * features),
            shape_of(rows + 16, 4 * features),
            shape_of(NORM_ROWS, features, dtype=F32),
        ),
        [
            pltpu.VMEM((rows, features), F32),
            pltpu.VMEM((rows, features), BF16),
            pltpu.VMEM((rows, 3 * features), BF16),
        ],
        16 * rows * features * features,
        "self_backward",
        30,
    )


def self_grad(place, keep, send, other, norm_total):
    features = norm_total.shape[1]
    rows = features // GROUPS + NORM_ROWS
    return local_call(
        self_grad_kernel,
        (place,),
        (keep, send, other, norm_total),
        part_shapes(SELF_SPLIT, rows - SELF_SPLIT, features),
        [],
        8 * keep.shape[0] * features * features,
        "self_grad",
        24,
    )


def run_direct(hidden, feats, first_item, lengths, out_grad, image, begin, weights):
    moves = Direct(lax.axis_size("dp"), lax.axis_size("mp"))
    place = moves.place
    feats_place = jnp.concatenate([place, first_item[None].astype(jnp.int32)])
    begin_split = begin.shape[0] // 2
    image_split = image.shape[0] * 96 // 176
    feed_split = weights.shape[0] // 2

    begin = moves.spread_z(begin)
    begin, image, feats = tie(begin, image, feats)
    begin_others = moves.spread_first(begin, begin_split)
    image = moves.spread_z(image)
    begin_others, image, weights, feats = tie(begin_others, image, weights, feats)
    begin_parts = moves.join_first(begin, begin_split, begin_others)
    begin_others = moves.spread_second(begin_parts)
    image_others = moves.spread_first(image, image_split)
    weights = moves.spread_z(weights)
    begin_others, image_others, weights = tie(begin_others, image_others, weights)

    image_parts = moves.join_first(image, image_split, image_others)
    image_others = moves.spread_second(image_parts)
    weight_others = moves.spread_first(weights, feed_split)
    begin = moves.join_second(begin_parts, begin_others)
    begin_other = moves.hop_core(begin)
    first_in, qkv, heads, w_qkv, w_cross, w_self_out, w_cross_out, norm = self_forward(
        place, lengths, hidden, (begin, begin_other)
    )
    first_in, image_others, weight_others = tie(first_in, image_others, weight_others)
    image = moves.join_second(image_parts, image_others)
    weight_parts = moves.join_first(weights, feed_split, weight_others)
    image_other = moves.hop_core(image)
    image_other, weight_parts, first_in = tie(image_other, weight_parts, first_in)
    weight_others = moves.spread_second(weight_parts)
    key_values = image_forward(feats_place, feats, (image, image_other))
    second_in, cross_queries, cross_heads = cross_forward(
        first_in, norm, w_cross, w_cross_out, key_values
    )
    second_in, weight_others = tie(second_in, weight_others)
    weights = moves.join_second(weight_parts, weight_others)
    weights_other = moves.hop_core(weights)
    block_out, two_grad, feed_keep, feed_send, norm_grads = feed(
        place, lengths, first_in, second_in, norm, out_grad, (weights, weights_other)
    )

    feed_other = moves.hop_core(feed_send)
    cross_keep, cross_send, one_query_grad, norm_grads = cross_backward(
        two_grad,
        first_in,
        second_in,
        norm,
        w_cross,
        w_cross_out,
        cross_queries,
        cross_heads,
        key_values,
        norm_grads,
    )
    cross_send, feed_other = tie(cross_send, feed_other)
    cross_other = moves.hop_core(cross_send)
    feed_grads = feed_grad(place, feed_keep, feed_send, feed_other, feed_split)
    cross_other, feed_grads = tie(cross_other, feed_grads)
    feed_first = moves.fold_first(feed_grads)
    image_grads = image_grad(feats_place, feats, cross_keep, cross_other)
    one_query_grad, image_grads, feed_first = tie(one_query_grad, image_grads, feed_first)
    feed_second = moves.fold_second(feed_grads, feed_first)
    image_first = moves.fold_first(image_grads)
    input_grad, self_keep, self_send, norm_total = self_backward(
        lengths,
        one_query_grad,
        two_grad,
        first_in,
        norm,
        hidden,
        qkv,
        heads,
        w_qkv,
        w_self_out,
        norm_grads,
    )
    self_send, image_first, feed_second = tie(self_send, image_first, feed_second)
    self_other = moves.hop_core(self_send)
    feed_kept = moves.kept(feed_grads, feed_first, feed_second)
    feed_other = moves.ring_z(feed_kept, 1)
    image_second = moves.fold_second(image_grads, image_first)
    self_grads = self_grad(place, self_keep, self_send, self_other, norm_total)
    self_grads, feed_other = tie(self_grads, feed_other)
    self_first = moves.fold_first(self_grads)
    feed_other = moves.ring_z(feed_kept, 2, feed_other)
    feed_other, image_second = tie(feed_other, image_second)
    image_kept = moves.kept(image_grads, image_first, image_second)
    feed_other = moves.ring_z(feed_kept, 3, feed_other)
    image_other = moves.ring_z(image_kept, 1)
    self_first, image_other, feed_other = tie(self_first, image_other, feed_other)
    self_second = moves.fold_second(self_grads, self_first)
    image_other = moves.ring_z(image_kept, 2, image_other)
    feed_sum = moves.finish(feed_kept, [feed_other])
    image_other, self_second = tie(image_other, self_second)
    image_other = moves.ring_z(image_kept, 3, image_other)
    self_kept = moves.kept(self_grads, self_first, self_second)
    self_others = moves.fold_z(self_kept)
    image_sum = moves.finish(image_kept, [image_other])
    in_sum = moves.finish(self_kept, self_others)
    return block_out, input_grad, in_sum, image_sum, feed_sum


def run_plain(hidden, feats, first_item, lengths, out_grad, image, begin, weights):
    moves = Plain(lax.axis_size("dp"), lax.axis_size("mp"))
    place = moves.place
    feats_place = jnp.concatenate([place, first_item[None].astype(jnp.int32)])
    features = hidden.shape[1]
    width = features // MODEL
    block_rows, out_rows = features // GROUPS, width // GROUPS
    own_in, own_out = block_rows * GROUPS // moves.dp, out_rows * GROUPS // moves.dp
    half = block_rows // 2
    part = begin.shape[0] - NORM_ROWS
    inward = moves.collect(begin[:own_in])
    cross_out = moves.collect(begin[own_in : own_in + own_out])
    self_out = moves.collect(begin[own_in + own_out : part])
    norm_all = lax.psum(begin[part:].astype(F32), AXES).astype(BF16)
    norm_first = jnp.zeros((2, SLOTS, NORM_ROWS, features), BF16).at[0, 0].set(norm_all)
    begin = jnp.concatenate(
        [
            inward[:, :, :half],
            cross_out,
            jnp.zeros_like(norm_first),
            inward[:, :, half:],
            self_out,
            norm_first,
        ],
        axis=2,
    )
    image = moves.collect(image)
    own_up = weights.shape[0] // 2
    weights = jnp.concatenate(
        [moves.collect(weights[:own_up]), moves.collect(weights[own_up:])], axis=2
    )
    first_in, qkv, heads, w_qkv, w_cross, w_self_out, w_cross_out, norm = self_forward(
        place, lengths, hidden, (begin[0], begin[1])
    )
    key_values = image_forward(feats_place, feats, (image[0], image[1]))
    second_in, cross_queries, cross_heads = cross_forward(
        first_in, norm, w_cross, w_cross_out, key_values
    )
    block_out, two_grad, feed_keep, feed_send, norm_grads = feed(
        place, lengths, first_in, second_in, norm, out_grad, (weights[0], weights[1])
    )
    feed_half = weights.shape[2] // 2
    feed_grads = feed_grad(place, feed_keep, feed_send, moves.hop_core(feed_send), feed_half)
    cross_keep, cross_send, one_query_grad, norm_grads = cross_backward(
        two_grad,
        first_in,
        second_in,
        norm,
        w_cross,
        w_cross_out,
        cross_queries,
        cross_heads,
        key_values,
        norm_grads,
    )
    image_grads = image_grad(feats_place, feats, cross_keep, moves.hop_core(cross_send))
    input_grad, self_keep, self_send, norm_total = self_backward(
        lengths,
        one_query_grad,
        two_grad,
        first_in,
        norm,
        hidden,
        qkv,
        heads,
        w_qkv,
        w_self_out,
        norm_grads,
    )
    self_grads = self_grad(place, self_keep, self_send, moves.hop_core(self_send), norm_total)

    def beside(values):
        count = values.shape[-2] // MODEL
        return jnp.concatenate(
            [values[..., part * count : (part + 1) * count, :] for part in range(MODEL)], axis=-1
        )

    def below(values):
        count = values.shape[-1] // MODEL
        return jnp.concatenate(
            [values[..., part * count : (part + 1) * count] for part in range(MODEL)], axis=-2
        )

    grads = moves.joined(self_grads)
    in_part = moves.scatter(grads[..., :block_rows, : 3 * width])
    self_out = moves.scatter(beside(grads[..., :block_rows, 3 * width :]))
    norm_sum = lax.psum(norm_total, AXES)
    in_sum = jnp.concatenate([jnp.concatenate([in_part, below(self_out)], axis=1), norm_sum])
    grads = moves.joined(image_grads)
    image_rows = grads.shape[3] - 2 * out_rows
    image_part = grads[..., :image_rows, :]
    image_part = jnp.concatenate(
        [image_part[..., : features // 2], image_part[..., features // 2 :]], axis=3
    )
    image_part = moves.scatter(image_part)
    image_half = image_part.shape[0] // 2
    image_part = jnp.concatenate([image_part[:image_half], image_part[image_half:]], axis=1)
    cross_query = moves.scatter(below(grads[..., image_rows : image_rows + out_rows, :]))
    cross_out = moves.scatter(grads[..., image_rows + out_rows :, :])
    image_sum = jnp.concatenate([image_part, beside(cross_query), cross_out])
    grads = moves.joined(feed_grads)
    feed_sum = jnp.concatenate(
        [moves.scatter(jnp.stack(feed_grads[:2])), moves.scatter(grads[..., feed_half:, :])]
    )
    return block_out, input_grad, in_sum, image_sum, feed_sum


def per_device(
    hidden_in,
    image_feats,
    caption_lengths,
    out_grad,
    proj_in,
    proj_in_moments,
    proj_in_average,
    proj_out,
    proj_out_moments,
    proj_out_average,
    image_kv,
    image_kv_moments,
    image_kv_average,
    feed_up,
    feed_up_moments,
    feed_up_average,
    feed_down,
    feed_down_moments,
    feed_down_average,
    norm_params,
    norm_params_moments,
    norm_params_average,
):
    data_ways, model_ways = lax.axis_size("dp"), lax.axis_size("mp")
    data_index, model_index = lax.axis_index("dp"), lax.axis_index("mp")
    rows, features = hidden_in.shape
    items = rows // SEQ
    width = features // model_ways
    own_norm = norm_params.shape[1]
    norm_begin = (model_index * data_ways + data_index) * own_norm
    lengths = lax.dynamic_slice_in_dim(caption_lengths, model_index * items, items, 0)
    direct = data_ways == GROUPS and model_ways == MODEL
    if direct:
        feats = lax.dynamic_slice_in_dim(image_feats, model_index // 2 * 2 * items, 2 * items, 0)
        first_item = model_index % 2 * items
    else:
        feats = jnp.concatenate(
            [
                lax.dynamic_slice_in_dim(image_feats, (model_index % 2 + 2 * side) * items, items, 0)
                for side in range(2)
            ]
        )
        first_item = model_index // 2 * items
    image_piece = jnp.concatenate([image_kv[0], image_kv[1]], axis=1).astype(BF16)
    in_piece = jnp.concatenate([proj_in[kind] for kind in range(4)], axis=1).astype(BF16)
    out_pieces = [proj_out[kind].astype(BF16) for kind in range(2)]
    feed_piece = jnp.concatenate([feed_up, feed_down], axis=0).astype(BF16)
    norm_rows = lax.dynamic_update_slice(
        jnp.zeros((NORM_ROWS, features), F32), norm_params, (0, norm_begin)
    ).astype(BF16)
    own_in, own_out, own_image = proj_in.shape[1], proj_out.shape[1], image_kv.shape[1]
    if direct:
        run, half = run_direct, own_in // 2
        begin_piece = jnp.concatenate(
            [
                in_piece[:half],
                out_pieces[1],
                jnp.zeros_like(norm_rows),
                in_piece[half:],
                out_pieces[0],
                norm_rows,
            ],
            axis=0,
        )
    else:
        run = run_plain
        begin_piece = jnp.concatenate(
            [in_piece, out_pieces[1], out_pieces[0], norm_rows], axis=0
        )
    block_out, input_grad, in_sum, image_sum, feed_sum = run(
        hidden_in, feats, first_item, lengths, out_grad, image_piece, begin_piece, feed_piece
    )
    norm_shard = lax.dynamic_slice(in_sum[own_in:], (0, norm_begin), norm_params.shape)
    up_next, down_next, up_update, down_update, feed_squares = update_call(
        feed_update_kernel,
        (feed_sum, feed_up, feed_up_moments, feed_down, feed_down_moments),
        (feed_up_moments, feed_down_moments),
        (feed_up, feed_down),
        "feed_update",
    )
    image_next, image_update, image_squares = update_call(
        image_update_kernel,
        (image_sum, image_kv, image_kv_moments),
        (image_kv_moments,),
        (image_kv,),
        "image_update",
    )
    in_next, out_next, norm_next, in_update, out_update, norm_update, last_squares = update_call(
        last_update_kernel,
        (
            in_sum,
            image_sum,
            norm_shard,
            proj_in,
            proj_in_moments,
            proj_out,
            proj_out_moments,
            norm_params,
            norm_params_moments,
        ),
        (proj_in_moments, proj_out_moments, norm_params_moments),
        (proj_in, proj_out, norm_params),
        "last_update",
    )
    own_squares = feed_squares + image_squares + last_squares
    ways = data_ways * model_ways
    copies = jnp.broadcast_to(own_squares[None], (ways,) + own_squares.shape)
    squares = lax.all_to_all(copies, AXES, 0, 0, tiled=True)
    results = apply_call(
        squares,
        (proj_in, proj_out, image_kv, feed_up, feed_down, norm_params),
        (
            proj_in_average,
            proj_out_average,
            image_kv_average,
            feed_up_average,
            feed_down_average,
            norm_params_average,
        ),
        (in_update, out_update, image_update, up_update, down_update, norm_update),
    )
    new_weights, new_averages, (trust, norms) = results[:6], results[6:12], results[12:]
    moments = (in_next, out_next, image_next, up_next, down_next, norm_next)
    outputs = [
        each for group in zip(new_weights, moments, new_averages) for each in group
    ]
    tensors = sum(each.shape[0] for each in (proj_in, proj_out, image_kv, norm_params)) + 2
    return (block_out, input_grad, *outputs, trust[0, :tensors], norms[:, :tensors])


def solution(mesh):
    rows = P(AXES, None)
    by_column = P(None, "dp", "mp")
    by_row = P(None, ("mp", "dp"), None)
    weights = (
        by_column,
        P(None, None, "dp", "mp"),
        by_column,
        by_row,
        P(None, None, ("mp", "dp"), None),
        by_row,
        by_column,
        P(None, None, "dp", "mp"),
        by_column,
        P("dp", "mp"),
        P(None, "dp", "mp"),
        P("dp", "mp"),
        P(("mp", "dp"), None),
        P(None, ("mp", "dp"), None),
        P(("mp", "dp"), None),
        P(None, ("mp", "dp")),
        P(None, None, ("mp", "dp")),
        P(None, ("mp", "dp")),
    )
    return jax.shard_map(
        per_device,
        mesh=mesh,
        in_specs=(rows, P("dp", None, None), P("dp"), rows, *weights),
        out_specs=(rows, rows, *weights, P(), P()),
        check_vma=False,
    )
```

time: 406 us -> 370 us (0.911)
  other arithmetic: 50.6 us -> 12.5 us
  starting transfers between devices: 71.1 us -> 57.3 us
  Pallas kernels: 126 us -> 138 us
  local copies, waits for them, and re-layouts: 41.3 us -> 45.4 us
    pallas_call x2 -> x4, Pallas kernels: 35.9 us -> 61.2 us  [the longest x1 20.3 us: cross_backward(): pl.pallas_call(cross_backward_kernel, grid=(items + 3,), out_shape=(shape...]
    pallas_call x5 -> x9, Pallas kernels: 90.4 us -> 76.7 us  [local_call(): pl.pallas_call(kernel, out_shape=tuple(out_shapes), in_specs=[SCALARS] *...]
    ppermute x18, starting transfers between devices: 39.9 us -> 29.6 us  [hop_z(): lax.ppermute(values, AXES, [(i, (i + step) % self.count) for i in range(s...]
    convert_element_type x12 -> x8, other arithmetic: 10.8 us -> 0.9 us  [total(): sums.append(result.astype(dtype))]
    add x9 -> x1, other arithmetic: 9.66 us -> 0.01 us  [per_device(): own_squares = feed_squares + image_squares + last_squares]
    reduce_sum x8 -> x0, other arithmetic: 8.9 us -> none  [the longest x7 8.1 us: tensor_squares(): return jnp.sum(values * values, axis=tuple(range(1, values.ndim)))]
    optimization_barrier x0 -> x1, local copies, waits for them, and re-layouts: none -> 7.74 us  [tie(): return lax.optimization_barrier(arrays)]
    ppermute x30, waiting for transfers between devices: 42.9 us -> 35.9 us  [hop(): lax.ppermute(values, AXES, [(i, i ^ flip) for i in range(self.count)])]
  transfers between devices with their start and end apart: 49 -> 49, of which waited for: 23 -> 21; matrix products, arithmetic and copies ran while one was open for 8% -> 6% of each run, Pallas kernels for 25% -> 31%
where the time goes in v3:
time: 370 us; the launch traced here: 366 us
  Pallas kernels  138 us (37%)
  waiting for transfers between devices  110 us (30%)
  starting transfers between devices  57.3 us (15%)
  local copies, waits for them, and re-layouts  45.4 us (12%)
  other arithmetic  12.5 us (3%)
    pallas_call x9, Pallas kernels, local_call(): pl.pallas_call(kernel, out_shape=tuple(out_shapes), in_specs=[SCALARS] *...  76.7 us
    ppermute x18, waiting for transfers between devices, hop_z(): lax.ppermute(values, AXES, [(i, (i + step) % self.count) for i in range(s...  67.8 us
    ppermute x30, waiting for transfers between devices, hop(): lax.ppermute(values, AXES, [(i, i ^ flip) for i in range(self.count)])  35.9 us
    ppermute x18, starting transfers between devices, hop_z(): lax.ppermute(values, AXES, [(i, (i + step) % self.count) for i in range(s...  29.6 us
    ppermute x30, starting transfers between devices, hop(): lax.ppermute(values, AXES, [(i, i ^ flip) for i in range(self.count)])  25.1 us
    unnamed x117, local copies, waits for them, and re-layouts  23.8 us
    pallas_call x1, Pallas kernels, cross_backward(): pl.pallas_call(cross_backward_kernel, grid=(items + 3,), out_shape=(shape...  20.3 us
    pallas_call x1, Pallas kernels, image_grad(): pl.pallas_call(functools.partial(image_grad_kernel, items // 2 * QUERIES)...  19.1 us
  transfers between devices with their start and end apart: 49, of which 21 were waited for; matrix products, arithmetic and copies ran while one was open for 6% of the time, Pallas kernels for 31%

profile of v3, /device:TPU:0, one launch (start us, length us, event | category | flops | bytes accessed | tf_op | source)
XLA Modules:
  0.0 365.5 jit_solution(5481699318988912590)
XLA Ops:
  4.4 3.2 collective-permute-start
  7.6 2.6 collective-permute-start.1
  11.6 5.9 %constant_dynamic-slice_fusion.1 = bf16[16,257,1408]{2,0,1:T(8,128)(2,1)S(1)} fusion(bf16[32,257,1408]{2,0,1:T(8,128)(2,1)} %param.23, s32[]{:T(128)S(6)} %select_n.51), kind=kLoop, calls=%fused_computation.111 | loop fusion | bytes 23158788 | tf_op jit(solution)/shard_map/dynamic_slice | solution.py:1577
  17.5 7.7 %copy.52.feats = bf16[16,257,1408]{2,1,0:T(8,128)(2,1)} copy(bf16[16,257,1408]{2,0,1:T(8,128)(2,1)S(1)} %constant_dynamic-slice_fusion.1) | data formatting | bytes 23158784 | tf_op jit(solution)/shard_map/optimization_barrier | solution.py:1025
  29.6 5.7 %collective-permute-start.5 = (bf16[176,384]{1,0:T(8,128)(2,1)S(1)}, bf16[176,384]{1,0:T(8,128)(2,1)S(1)}, u32[]{:S(2)}, u32[]{:S(2)}) collective-permute-start(bf16[176,384]{1,0:T(8,128)(2,1)S(1)} %pad_maximum_fusion.19), channel_id=1, source_target_pairs={{0,8},{1,9},{2,10},{3,11},{4,12},{5,13},{6,14},{7,15},{8,16},{9,17... | collective-permute-start | bytes 405512 | tf_op jit(solution)/shard_map/ppermute | solution.py:918
  37.8 3.1 collective-permute-done.5
  40.9 4.2 %collective-permute-done.6 = bf16[176,384]{1,0:T(8,128)(2,1)S(1)} collective-permute-done((bf16[176,384]{1,0:T(8,128)(2,1)S(1)}, bf16[176,384]{1,0:T(8,128)(2,1)S(1)}, u32[]{:S(2)}, u32[]{:S(2)}) %collective-permute-start.6) | collective-permute-done | bytes 135200 | tf_op jit(solution)/shard_map/ppermute | solution.py:918
  46.6 3.4 collective-permute-start.12
  50.0 1.7 collective-permute-start.13
  53.1 6.1 %collective-permute-done.12 = bf16[192,768]{1,0:T(8,128)(2,1)S(1)} collective-permute-done((bf16[192,768]{1,0:T(8,128)(2,1)S(1)}, bf16[192,768]{1,0:T(8,128)(2,1)S(1)}, u32[]{:S(2)}, u32[]{:S(2)}) %collective-permute-start.12) | collective-permute-done | bytes 294944 | tf_op jit(solution)/shard_map/ppermute | solution.py:918
  61.5 8.0 %collective-permute-done.13 = bf16[192,768]{1,0:T(8,128)(2,1)S(1)} collective-permute-done((bf16[192,768]{1,0:T(8,128)(2,1)S(1)}, bf16[192,768]{1,0:T(8,128)(2,1)S(1)}, u32[]{:S(2)}, u32[]{:S(2)}) %collective-permute-start.13) | collective-permute-done | bytes 294944 | tf_op jit(solution)/shard_map/ppermute | solution.py:918
  71.1 6.1 %collective-permute-done.11 = bf16[4,80,384]{2,1,0:T(8,128)(2,1)S(1)} collective-permute-done((bf16[4,80,384]{2,1,0:T(8,128)(2,1)S(1)}, bf16[4,80,384]{2,1,0:T(8,128)(2,1)S(1)}, u32[]{:S(2)}, u32[]{:S(2)}) %collective-permute-start.11) | collective-permute-done | bytes 245792 | tf_op jit(solution)/shard_map/ppermute | solution.py:905
  78.7 2.1 copy.46
  85.7 2.2 collective-permute-done.15.begin_other
  88.0 13.6 %self_forward.1 = (f32[512,768]{1,0:T(8,128)S(1)}, bf16[512,2304]{1,0:T(8,128)(2,1)S(1)}, bf16[512,768]{1,0:T(8,128)(2,1)S(1)}, bf16[768,2304]{1,0:T(8,128)(2,1)...) custom-call(s32[16]{0:T(128)S(1)} %pad_add_fusion.place, ...), custom_call_target="tpu_custom_call" | custom-call | flops 3019898880 | bytes 20471808 | tf_op jit(solution)/shard_map/self_forward/pallas_call | solution.py:855
  101.6 1.7 copy-done.35
  104.4 4.5 %collective-permute-done.17 = bf16[2,4,80,384]{3,2,1,0:T(8,128)(2,1)S(1)} collective-permute-done((bf16[2,4,80,384]{3,2,1,0:T(8,128)(2,1)S(1)}, bf16[2,4,80,384]{3,2,1,0:T(8,128)(2,1)S(1)}, u32[]{:S(2)}, u32[]{:S(2)}) %collective-permute-start.17) | collective-permute-done | bytes 491552 | tf_op jit(solution)/shard_map/ppermute | solution.py:905
  112.3 1.8 collective-permute-done.20.image_other
  118.6 4.4 %copy-done.1 = bf16[16,257,1408]{2,1,0:T(8,128)(2,1)S(1)} copy-done((bf16[16,257,1408]{2,1,0:T(8,128)(2,1)S(1)}, bf16[16,257,1408]{2,1,0:T(8,128)(2,1)}, u32[]{:S(2)}) %copy-start.1) | copy-done | bytes 11579416
  126.2 13.3 %image_forward.1.key_values = bf16[2176,1536]{1,0:T(8,128)(2,1)S(1)} custom-call(s32[17]{0:T(128)S(1)} %pad_add_fusion.1.place, bf16[16,257,1408]{2,1,0:T(8,128)(2,1)S(1)} %copy-done.1, bf16[16,176,384]{2,1,0:T(8,128)(2,1)S(1)} %bitcast.218, bf16[16,176,384]{2,1,0:T(8,128)(2,1)S(1)} %copy-done.27), custom_call_target="tpu_custom_call" | custom-call | flops 9412018176 | bytes 17137664 | tf_op jit(solution)/shard_map/image_forward/pallas_call | solution.py:1061
  139.5 11.3 %cross_forward.1 = (f32[256,768]{1,0:T(8,128)S(1)}, bf16[256,768]{1,0:T(8,128)(2,1)S(1)}, bf16[256,768]{1,0:T(8,128)(2,1)S(1)}) custom-call(f32[512,768]{1,0:T(8,128)S(1)} %get-tuple-element.164.first_in, f32[8,768]{1,0:T(8,128)S(1)} %get-tuple-element.165.norm, bf16[768,768]{1,0:T(8,128)(2,1)S(1)} %get-tuple-element.166.w_cross, ...), custom_call_target="tpu_custom_call" | custom-call | flops 603979776 | bytes 12214272 | tf_op jit(solution)/shard_map/cross_forward/pallas_call | solution.py:855
  150.8 1.8 maximum_bitcast_fusion
  152.6 2.0 pad_maximum_fusion
  155.2 8.0 %collective-permute-done.23.feed_other = bf16[16,192,768]{2,1,0:T(8,128)(2,1)} collective-permute-done((bf16[16,192,768]{2,1,0:T(8,128)(2,1)S(1)}, bf16[16,192,768]{2,1,0:T(8,128)(2,1)}, u32[]{:S(2)}, u32[]{:S(2)}) %collective-permute-start.23) | collective-permute-done | bytes 4718624 | tf_op jit(solution)/shard_map/ppermute | solution.py:905
  163.2 17.0 %feed.1 = (bf16[512,768]{1,0:T(8,128)(2,1)}, f32[512,768]{1,0:T(8,128)S(1)}, bf16[512,3072]{1,0:T(8,128)(2,1)S(1)}, bf16[512,4608]{1,0:T(8,128)(2,1)S(1)}, f32[8,768]{1,0:T(8,128)S(1)}) custom-call(s32[16]{0:T(128)S(1)} %pad_add_fusion.place, s32[8]{0:T(128)S(1)} %dynamic_slice.9.lengths, f32[512,768]{1,0:T(8,128)S(1)} %get-tuple-element.164.first_in, ...), custom_call_target="tpu_custom_call" | custom-call | flops 9663676416 | bytes 22855680 | tf_op jit(solution)/shard_map/feed/pallas_call | solution.py:855
  180.3 1.7 copy-done.33
  182.0 20.3 %cross_backward.1 = (bf16[2992,768]{1,0:T(8,128)(2,1)S(1)}, bf16[2992,768]{1,0:T(8,128)(2,1)}, f32[256,768]{1,0:T(8,128)S(1)}, f32[8,768]{1,0:T(8,128)S(1)}) custom-call(f32[512,768]{1,0:T(8,128)S(1)} %get-tuple-element.177.two_grad, f32[512,768]{1,0:T(8,128)S(1)} %get-tuple-element.164.first_in, f32[256,768]{1,0:T(8,128)S(1)} %get-tuple-element.173.second_in, ...), custom_call_target="tpu_custom_call" | custom-call | flops 3019898880 | bytes 27574272 | tf_op jit(solution)/shard_map/cross_backward/pallas_call | solution.py:1202
  202.3 2.1 copy-done.24
  204.9 8.5 %feed_grad.1 = (bf16[2,4,96,768]{3,2,1,0:T(8,128)(2,1)S(1)}, bf16[2,4,96,768]{3,2,1,0:T(8,128)(2,1)S(1)}, bf16[2,4,96,768]{3,2,1,0:T(8,128)(2,1)S(1)}, bf16[2,4,96,768]{3,2,1,0:T(8,128)(2,1)S(1)}) custom-call(s32[16]{0:T(128)S(1)} %pad_add_fusion.place, bf16[512,3072]{1,0:T(8,128)(2,1)S(1)} %copy-done.34, bf16[512,4608]{1,0:T(8,128)(2,1)S(1)} %get-tuple-element.184.rows, ...), custom_call_target="tpu_custom_call" | custom-call | flops 4831838208 | bytes 9437184 | tf_op jit(solution)/shard_map/feed_grad/pallas_call | solution.py:1146
  214.6 2.3 copy-done.25
  216.9 19.1 %image_grad.1 = (bf16[2,4,64,768]{3,2,1,0:T(8,128)(2,1)S(1)}, bf16[2,4,64,768]{3,2,1,0:T(8,128)(2,1)S(1)}, bf16[2,4,72,768]{3,2,1,0:T(8,128)(2,1)S(1)}, bf16[2,4,72,768]{3,2,1,0:T(8,128)(2,1)S(1)}) custom-call(s32[17]{0:T(128)S(1)} %pad_add_fusion.1.place, bf16[16,257,1408]{2,1,0:T(8,128)(2,1)} %copy.52.feats, bf16[2992,768]{1,0:T(8,128)(2,1)S(1)} %copy-done.25, ...), custom_call_target="tpu_custom_call" | custom-call | flops 9412018176 | bytes 18939904 | tf_op jit(solution)/shard_map/image_grad/pallas_call | solution.py:1235
  236.0 5.5 %collective-permute-done.26 = bf16[2,4,96,768]{3,2,1,0:T(8,128)(2,1)S(1)} collective-permute-done((bf16[2,4,96,768]{3,2,1,0:T(8,128)(2,1)S(1)}, bf16[2,4,96,768]{3,2,1,0:T(8,128)(2,1)S(1)}, u32[]{:S(2)}, u32[]{:S(2)}) %collective-permute-start.26) | collective-permute-done | bytes 1179680 | tf_op jit(solution)/shard_map/ppermute | solution.py:905
  246.3 1.7 copy-done.38
  248.0 20.3 %self_backward.1 = (bf16[512,768]{1,0:T(8,128)(2,1)}, bf16[512,1536]{1,0:T(8,128)(2,1)S(1)}, bf16[528,3072]{1,0:T(8,128)(2,1)S(1)}, f32[8,768]{1,0:T(8,128)S(1)}) custom-call(s32[8]{0:T(128)S(1)} %dynamic_slice.9.lengths, f32[256,768]{1,0:T(8,128)S(1)} %copy-done.32, f32[512,768]{1,0:T(8,128)S(1)} %get-tuple-element.177.two_grad, ...), custom_call_target="tpu_custom_call" | custom-call | flops 4831838208 | bytes 18259968 | tf_op jit(solution)/shard_map/self_backward/pallas_call | solution.py:855
  268.2 6.8 %collective-permute-done.30 = bf16[4,96,768]{2,1,0:T(8,128)(2,1)S(1)} collective-permute-done((bf16[4,96,768]{2,1,0:T(8,128)(2,1)S(1)}, bf16[4,96,768]{2,1,0:T(8,128)(2,1)S(1)}, u32[]{:S(2)}, u32[]{:S(2)}) %collective-permute-start.30) | collective-permute-done | bytes 589856 | tf_op jit(solution)/shard_map/ppermute | solution.py:905
  277.1 4.6 %collective-permute-start.33 = (bf16[192,768]{1,0:T(8,128)(2,1)S(1)}, bf16[192,768]{1,0:T(8,128)(2,1)S(1)}, u32[]{:S(2)}, u32[]{:S(2)}) collective-permute-start(bf16[192,768]{1,0:T(8,128)(2,1)S(1)} %pad_maximum_fusion.13), channel_id=1, source_target_pairs={{0,8},{1,9},{2,10},{3,11},{4,12},{5,13},{6,14},{7,15},{8,16},{9,17... | collective-permute-start | bytes 884744 | tf_op jit(solution)/shard_map/ppermute | solution.py:918
  282.4 5.9 %self_grad.1 = (bf16[2,4,48,768]{3,2,1,0:T(8,128)(2,1)S(1)}, bf16[2,4,48,768]{3,2,1,0:T(8,128)(2,1)S(1)}, bf16[2,4,56,768]{3,2,1,0:T(8,128)(2,1)S(1)}, bf16[2,4,56,768]{3,2,1,0:T(8,128)(2,1)S(1)}) custom-call(s32[16]{0:T(128)S(1)} %pad_add_fusion.place, bf16[512,1536]{1,0:T(8,128)(2,1)S(1)} %get-tuple-element.215.keep, ...), custom_call_target="tpu_custom_call" | custom-call | flops 2415919104 | bytes 10641408 | tf_op jit(solution)/shard_map/self_grad/pallas_call | solution.py:855
  288.3 3.6 collective-permute-done.33
  293.3 9.1 %collective-permute-done.36 = bf16[192,768]{1,0:T(8,128)(2,1)S(1)} collective-permute-done((bf16[192,768]{1,0:T(8,128)(2,1)S(1)}, bf16[192,768]{1,0:T(8,128)(2,1)S(1)}, u32[]{:S(2)}, u32[]{:S(2)}) %collective-permute-start.36) | collective-permute-done | bytes 294944 | tf_op jit(solution)/shard_map/ppermute | solution.py:918
  303.2 13.4 %collective-permute-done.39 = bf16[136,768]{1,0:T(8,128)(2,1)S(1)} collective-permute-done((bf16[136,768]{1,0:T(8,128)(2,1)S(1)}, bf16[136,768]{1,0:T(8,128)(2,1)S(1)}, u32[]{:S(2)}, u32[]{:S(2)}) %collective-permute-start.39) | collective-permute-done | bytes 208928 | tf_op jit(solution)/shard_map/ppermute | solution.py:918
  318.3 1.7 feed_update.1
  320.1 7.4 %collective-permute-done.41 = bf16[136,768]{1,0:T(8,128)(2,1)S(1)} collective-permute-done((bf16[136,768]{1,0:T(8,128)(2,1)S(1)}, bf16[136,768]{1,0:T(8,128)(2,1)S(1)}, u32[]{:S(2)}, u32[]{:S(2)}) %collective-permute-start.41) | collective-permute-done | bytes 208928 | tf_op jit(solution)/shard_map/ppermute | solution.py:918
  327.9 2.1 collective-permute-start.47
  331.6 4.6 %collective-permute-done.45 = bf16[104,768]{1,0:T(8,128)(2,1)S(1)} collective-permute-done((bf16[104,768]{1,0:T(8,128)(2,1)S(1)}, bf16[104,768]{1,0:T(8,128)(2,1)S(1)}, u32[]{:S(2)}, u32[]{:S(2)}) %collective-permute-start.45) | collective-permute-done | bytes 159776 | tf_op jit(solution)/shard_map/ppermute | solution.py:918
  336.2 7.4 %collective-permute-done.46 = bf16[104,768]{1,0:T(8,128)(2,1)S(1)} collective-permute-done((bf16[104,768]{1,0:T(8,128)(2,1)S(1)}, bf16[104,768]{1,0:T(8,128)(2,1)S(1)}, u32[]{:S(2)}, u32[]{:S(2)}) %collective-permute-start.46) | collective-permute-done | bytes 159776 | tf_op jit(solution)/shard_map/ppermute | solution.py:918
  349.4 2.6 all-to-all-start
  352.6 6.7 %all-to-all-done.squares = f32[32,2,128]{2,1,0:T(2,128)S(1)} async-done(((f32[32,2,128]{2,1,0:T(2,128)}), f32[32,2,128]{2,1,0:T(2,128)S(1)}, u32[]{:S(2)}, u32[]{:S(2)}) %all-to-all-start) | async-done | bytes 32800 | tf_op jit(solution)/shard_map/all_to_all | solution.py:1651
  359.9 4.0 %apply.1 = (f32[4,96,192]{2,1,0:T(8,128)}, f32[2,24,768]{2,1,0:T(8,128)}, f32[2,176,192]{2,1,0:T(8,128)}, f32[96,768]{1,0:T(8,128)}, f32[96,768]{1,0:T(8,128)}, ...) custom-call(f32[32,2,128]{2,1,0:T(2,128)} %copy-done.52, ...), custom_call_target="tpu_custom_call" | custom-call | bytes 6549824 | tf_op jit(solution)/shard_map/apply/pallas_call | solution.py:855
  (248 shorter events, 60.3 us)
Async XLA Ops:
  4.4 21.0 %collective-permute-start = (bf16[160,768]{1,0:T(8,128)(2,1)S(1)}, bf16[160,768]{1,0:T(8,128)(2,1)S(1)}, u32[]{:S(2)}, u32[]{:S(2)}) collective-permute-start(bf16[160,768]{1,0:T(8,128)(2,1)S(1)} %constant_dynamic-update-slice_fusion), channel_id=1, source_target_pairs={{0,8},{1,9},{2,10},{3,11},{4,12},{5,13},{6,14},{7,15},{8,16},{9,17... | collective-permute-start | bytes 737288 | tf_op jit(solution)/shard_map/ppermute | solution.py:918
  7.6 18.6 %collective-permute-start.1 = (bf16[160,768]{1,0:T(8,128)(2,1)S(1)}, bf16[160,768]{1,0:T(8,128)(2,1)S(1)}, u32[]{:S(2)}, u32[]{:S(2)}) collective-permute-start(bf16[160,768]{1,0:T(8,128)(2,1)S(1)} %constant_dynamic-update-slice_fusion), channel_id=1, source_target_pairs={{0,16},{1,17},{2,18},{3,19},{4,20},{5,21},{6,22},{7,23},{8,24},{9,... | collective-permute-start | bytes 737288 | tf_op jit(solution)/shard_map/ppermute | solution.py:918
  10.2 16.1 %collective-permute-start.2 = (bf16[160,768]{1,0:T(8,128)(2,1)S(1)}, bf16[160,768]{1,0:T(8,128)(2,1)S(1)}, u32[]{:S(2)}, u32[]{:S(2)}) collective-permute-start(bf16[160,768]{1,0:T(8,128)(2,1)S(1)} %constant_dynamic-update-slice_fusion), channel_id=1, source_target_pairs={{0,24},{1,25},{2,26},{3,27},{4,28},{5,29},{6,30},{7,31},{8,0},{9,1... | collective-permute-start | bytes 737288 | tf_op jit(solution)/shard_map/ppermute | solution.py:918
  26.6 18.6 %collective-permute-start.3 = (bf16[4,80,768]{2,1,0:T(8,128)(2,1)S(1)}, bf16[4,80,768]{2,1,0:T(8,128)(2,1)S(1)}, u32[]{:S(2)}, u32[]{:S(2)}) collective-permute-start(bf16[4,80,768]{2,1,0:T(8,128)(2,1)S(1)} %get-tuple-element.327), channel_id=1, source_target_pairs={{0,2},{1,3},{2,0},{3,1},{4,6},{5,7},{6,4},{7,5},{8,10},{9,11},{10,... | collective-permute-start | bytes 1474568 | tf_op jit(solution)/shard_map/ppermute | solution.py:905
  28.1 17.1 %collective-permute-start.4 = (bf16[4,80,768]{2,1,0:T(8,128)(2,1)S(1)}, bf16[4,80,768]{2,1,0:T(8,128)(2,1)S(1)}, u32[]{:S(2)}, u32[]{:S(2)}) collective-permute-start(bf16[4,80,768]{2,1,0:T(8,128)(2,1)S(1)} %get-tuple-element.326), channel_id=1, source_target_pairs={{0,4},{1,5},{2,6},{3,7},{4,0},{5,1},{6,2},{7,3},{8,12},{9,13},{10,... | collective-permute-start | bytes 1474568 | tf_op jit(solution)/shard_map/ppermute | solution.py:905
  29.6 11.3 %collective-permute-start.5 = (bf16[176,384]{1,0:T(8,128)(2,1)S(1)}, bf16[176,384]{1,0:T(8,128)(2,1)S(1)}, u32[]{:S(2)}, u32[]{:S(2)}) collective-permute-start(bf16[176,384]{1,0:T(8,128)(2,1)S(1)} %pad_maximum_fusion.19), channel_id=1, source_target_pairs={{0,8},{1,9},{2,10},{3,11},{4,12},{5,13},{6,14},{7,15},{8,16},{9,17... | collective-permute-start | bytes 405512 | tf_op jit(solution)/shard_map/ppermute | solution.py:918
  35.3 9.7 %collective-permute-start.6 = (bf16[176,384]{1,0:T(8,128)(2,1)S(1)}, bf16[176,384]{1,0:T(8,128)(2,1)S(1)}, u32[]{:S(2)}, u32[]{:S(2)}) collective-permute-start(bf16[176,384]{1,0:T(8,128)(2,1)S(1)} %pad_maximum_fusion.19), channel_id=1, source_target_pairs={{0,16},{1,17},{2,18},{3,19},{4,20},{5,21},{6,22},{7,23},{8,24},{9,... | collective-permute-start | bytes 405512 | tf_op jit(solution)/shard_map/ppermute | solution.py:918
  36.9 8.1 %collective-permute-start.7 = (bf16[176,384]{1,0:T(8,128)(2,1)S(1)}, bf16[176,384]{1,0:T(8,128)(2,1)S(1)}, u32[]{:S(2)}, u32[]{:S(2)}) collective-permute-start(bf16[176,384]{1,0:T(8,128)(2,1)S(1)} %pad_maximum_fusion.19), channel_id=1, source_target_pairs={{0,24},{1,25},{2,26},{3,27},{4,28},{5,29},{6,30},{7,31},{8,0},{9,1... | collective-permute-start | bytes 405512 | tf_op jit(solution)/shard_map/ppermute | solution.py:918
  45.3 32.0 %collective-permute-start.9 = (bf16[2,4,80,768]{3,2,1,0:T(8,128)(2,1)S(1)}, bf16[2,4,80,768]{3,2,1,0:T(8,128)(2,1)S(1)}, u32[]{:S(2)}, u32[]{:S(2)}) collective-permute-start(bf16[2,4,80,768]{3,2,1,0:T(8,128)(2,1)S(1)} %get-tuple-element.323), channel_id=1, source_target_pairs={{0,2},{1,3},{2,0},{3,1},{4,6},{5,7},{6,4},{7,5},{8,10},{9,11},{10,... | collective-permute-start | bytes 2949128 | tf_op jit(solution)/shard_map/ppermute | solution.py:905
  46.0 31.2 %collective-permute-start.8 = (bf16[2,4,80,768]{3,2,1,0:T(8,128)(2,1)S(1)}, bf16[2,4,80,768]{3,2,1,0:T(8,128)(2,1)S(1)}, u32[]{:S(2)}, u32[]{:S(2)}) collective-permute-start(bf16[2,4,80,768]{3,2,1,0:T(8,128)(2,1)S(1)} %get-tuple-element.321), channel_id=1, source_target_pairs={{0,4},{1,5},{2,6},{3,7},{4,0},{5,1},{6,2},{7,3},{8,12},{9,13},{10,... | collective-permute-start | bytes 2949128 | tf_op jit(solution)/shard_map/ppermute | solution.py:905
  46.6 12.6 %collective-permute-start.12 = (bf16[192,768]{1,0:T(8,128)(2,1)S(1)}, bf16[192,768]{1,0:T(8,128)(2,1)S(1)}, u32[]{:S(2)}, u32[]{:S(2)}) collective-permute-start(bf16[192,768]{1,0:T(8,128)(2,1)S(1)} %pad_maximum_fusion.12), channel_id=1, source_target_pairs={{0,8},{1,9},{2,10},{3,11},{4,12},{5,13},{6,14},{7,15},{8,16},{9,17... | collective-permute-start | bytes 884744 | tf_op jit(solution)/shard_map/ppermute | solution.py:918
  50.0 19.5 %collective-permute-start.13 = (bf16[192,768]{1,0:T(8,128)(2,1)S(1)}, bf16[192,768]{1,0:T(8,128)(2,1)S(1)}, u32[]{:S(2)}, u32[]{:S(2)}) collective-permute-start(bf16[192,768]{1,0:T(8,128)(2,1)S(1)} %pad_maximum_fusion.12), channel_id=1, source_target_pairs={{0,16},{1,17},{2,18},{3,19},{4,20},{5,21},{6,22},{7,23},{8,24},{9,... | collective-permute-start | bytes 884744 | tf_op jit(solution)/shard_map/ppermute | solution.py:918
  51.7 19.2 %collective-permute-start.14 = (bf16[192,768]{1,0:T(8,128)(2,1)S(1)}, bf16[192,768]{1,0:T(8,128)(2,1)S(1)}, u32[]{:S(2)}, u32[]{:S(2)}) collective-permute-start(bf16[192,768]{1,0:T(8,128)(2,1)S(1)} %pad_maximum_fusion.12), channel_id=1, source_target_pairs={{0,24},{1,25},{2,26},{3,27},{4,28},{5,29},{6,30},{7,31},{8,0},{9,1... | collective-permute-start | bytes 884744 | tf_op jit(solution)/shard_map/ppermute | solution.py:918
  59.2 18.0 %collective-permute-start.10 = (bf16[4,96,384]{2,1,0:T(8,128)(2,1)S(1)}, bf16[4,96,384]{2,1,0:T(8,128)(2,1)S(1)}, u32[]{:S(2)}, u32[]{:S(2)}) collective-permute-start(bf16[4,96,384]{2,1,0:T(8,128)(2,1)S(1)} %get-tuple-element.333), channel_id=1, source_target_pairs={{0,2},{1,3},{2,0},{3,1},{4,6},{5,7},{6,4},{7,5},{8,10},{9,11},{10,... | collective-permute-start | bytes 884744 | tf_op jit(solution)/shard_map/ppermute | solution.py:905
  69.5 7.8 %collective-permute-start.11 = (bf16[4,80,384]{2,1,0:T(8,128)(2,1)S(1)}, bf16[4,80,384]{2,1,0:T(8,128)(2,1)S(1)}, u32[]{:S(2)}, u32[]{:S(2)}) collective-permute-start(bf16[4,80,384]{2,1,0:T(8,128)(2,1)S(1)} %get-tuple-element.331), channel_id=1, source_target_pairs={{0,4},{1,5},{2,6},{3,7},{4,0},{5,1},{6,2},{7,3},{8,12},{9,13},{10,... | collective-permute-start | bytes 737288 | tf_op jit(solution)/shard_map/ppermute | solution.py:905
  80.8 7.1 %collective-permute-start.15 = (bf16[16,160,768]{2,1,0:T(8,128)(2,1)}, bf16[16,160,768]{2,1,0:T(8,128)(2,1)}, u32[]{:S(2)}, u32[]{:S(2)}) collective-permute-start(bf16[16,160,768]{2,1,0:T(8,128)(2,1)} %bitcast.33.begin_own), channel_id=1, source_target_pairs={{0,1},{1,0},{2,3},{3,2},{4,5},{5,4},{6,7},{7,6},{8,9},{9,8},{10,11... | collective-permute-start | bytes 11796488 | tf_op jit(solution)/shard_map/ppermute | solution.py:905
  81.1 27.9 %collective-permute-start.16 = (bf16[2,4,96,384]{3,2,1,0:T(8,128)(2,1)S(1)}, bf16[2,4,96,384]{3,2,1,0:T(8,128)(2,1)S(1)}, u32[]{:S(2)}, u32[]{:S(2)}) collective-permute-start(bf16[2,4,96,384]{3,2,1,0:T(8,128)(2,1)S(1)} %get-tuple-element.329), channel_id=1, source_target_pairs={{0,4},{1,5},{2,6},{3,7},{4,0},{5,1},{6,2},{7,3},{8,12},{9,13},{10,... | collective-permute-start | bytes 1769480 | tf_op jit(solution)/shard_map/ppermute | solution.py:905
  82.8 26.1 %collective-permute-start.18 = (bf16[4,96,768]{2,1,0:T(8,128)(2,1)S(1)}, bf16[4,96,768]{2,1,0:T(8,128)(2,1)S(1)}, u32[]{:S(2)}, u32[]{:S(2)}) collective-permute-start(bf16[4,96,768]{2,1,0:T(8,128)(2,1)S(1)} %get-tuple-element.319), channel_id=1, source_target_pairs={{0,2},{1,3},{2,0},{3,1},{4,6},{5,7},{6,4},{7,5},{8,10},{9,11},{10,... | collective-permute-start | bytes 1769480 | tf_op jit(solution)/shard_map/ppermute | solution.py:905
  84.4 25.1 %collective-permute-start.19 = (bf16[4,96,768]{2,1,0:T(8,128)(2,1)S(1)}, bf16[4,96,768]{2,1,0:T(8,128)(2,1)S(1)}, u32[]{:S(2)}, u32[]{:S(2)}) collective-permute-start(bf16[4,96,768]{2,1,0:T(8,128)(2,1)S(1)} %get-tuple-element.318), channel_id=1, source_target_pairs={{0,4},{1,5},{2,6},{3,7},{4,0},{5,1},{6,2},{7,3},{8,12},{9,13},{10,... | collective-permute-start | bytes 1769480 | tf_op jit(solution)/shard_map/ppermute | solution.py:905
  85.0 23.9 %collective-permute-start.17 = (bf16[2,4,80,384]{3,2,1,0:T(8,128)(2,1)S(1)}, bf16[2,4,80,384]{3,2,1,0:T(8,128)(2,1)S(1)}, u32[]{:S(2)}, u32[]{:S(2)}) collective-permute-start(bf16[2,4,80,384]{3,2,1,0:T(8,128)(2,1)S(1)} %get-tuple-element.335), channel_id=1, source_target_pairs={{0,2},{1,3},{2,0},{3,1},{4,6},{5,7},{6,4},{7,5},{8,10},{9,11},{10,... | collective-permute-start | bytes 1474568 | tf_op jit(solution)/shard_map/ppermute | solution.py:905
  115.5 35.3 %collective-permute-start.21 = (bf16[2,4,96,768]{3,2,1,0:T(8,128)(2,1)}, bf16[2,4,96,768]{3,2,1,0:T(8,128)(2,1)}, u32[]{:S(2)}, u32[]{:S(2)}) collective-permute-start(bf16[2,4,96,768]{3,2,1,0:T(8,128)(2,1)} %pad_maximum_fusion.4), channel_id=1, source_target_pairs={{0,4},{1,5},{2,6},{3,7},{4,0},{5,1},{6,2},{7,3},{8,12},{9,13},{10,... | collective-permute-start | bytes 3538952 | tf_op jit(solution)/shard_map/ppermute | solution.py:905
  117.0 33.8 %collective-permute-start.22 = (bf16[2,4,96,768]{3,2,1,0:T(8,128)(2,1)}, bf16[2,4,96,768]{3,2,1,0:T(8,128)(2,1)}, u32[]{:S(2)}, u32[]{:S(2)}) collective-permute-start(bf16[2,4,96,768]{3,2,1,0:T(8,128)(2,1)} %pad_maximum_fusion.5), channel_id=1, source_target_pairs={{0,2},{1,3},{2,0},{3,1},{4,6},{5,7},{6,4},{7,5},{8,10},{9,11},{10,... | collective-permute-start | bytes 3538952 | tf_op jit(solution)/shard_map/ppermute | solution.py:905
  155.1 8.1 %collective-permute-start.23 = (bf16[16,192,768]{2,1,0:T(8,128)(2,1)S(1)}, bf16[16,192,768]{2,1,0:T(8,128)(2,1)}, u32[]{:S(2)}, u32[]{:S(2)}) collective-permute-start(bf16[16,192,768]{2,1,0:T(8,128)(2,1)S(1)} %bitcast.219), channel_id=1, source_target_pairs={{0,1},{1,0},{2,3},{3,2},{4,5},{5,4},{6,7},{7,6},{8,9},{9,8},{10,11... | collective-permute-start | bytes 14155784 | tf_op jit(solution)/shard_map/ppermute | solution.py:905
  181.9 22.5 %collective-permute-start.24 = (bf16[512,4608]{1,0:T(8,128)(2,1)S(1)}, bf16[512,4608]{1,0:T(8,128)(2,1)}, u32[]{:S(2)}, u32[]{:S(2)}) collective-permute-start(bf16[512,4608]{1,0:T(8,128)(2,1)S(1)} %get-tuple-element.184.rows), channel_id=1, source_target_pairs={{0,1},{1,0},{2,3},{3,2},{4,5},{5,4},{6,7},{7,6},{8,9},{9,8},{10,11... | collective-permute-start | bytes 14155784 | tf_op jit(solution)/shard_map/ppermute | solution.py:905
  204.5 9.0 %collective-permute-start.25 = (bf16[2992,768]{1,0:T(8,128)(2,1)}, bf16[2992,768]{1,0:T(8,128)(2,1)S(1)}, u32[]{:S(2)}, u32[]{:S(2)}) collective-permute-start(bf16[2992,768]{1,0:T(8,128)(2,1)} %get-tuple-element.185), channel_id=1, source_target_pairs={{0,1},{1,0},{2,3},{3,2},{4,5},{5,4},{6,7},{7,6},{8,9},{9,8},{10,11... | collective-permute-start | bytes 13787144 | tf_op jit(solution)/shard_map/ppermute | solution.py:905
  213.4 28.1 %collective-permute-start.26 = (bf16[2,4,96,768]{3,2,1,0:T(8,128)(2,1)S(1)}, bf16[2,4,96,768]{3,2,1,0:T(8,128)(2,1)S(1)}, u32[]{:S(2)}, u32[]{:S(2)}) collective-permute-start(bf16[2,4,96,768]{3,2,1,0:T(8,128)(2,1)S(1)} %get-tuple-element.197), channel_id=1, source_target_pairs={{0,4},{1,5},{2,6},{3,7},{4,0},{5,1},{6,2},{7,3},{8,12},{9,13},{10,... | collective-permute-start | bytes 3538952 | tf_op jit(solution)/shard_map/ppermute | solution.py:905
  214.0 27.7 %collective-permute-start.27 = (bf16[2,4,96,768]{3,2,1,0:T(8,128)(2,1)S(1)}, bf16[2,4,96,768]{3,2,1,0:T(8,128)(2,1)S(1)}, u32[]{:S(2)}, u32[]{:S(2)}) collective-permute-start(bf16[2,4,96,768]{3,2,1,0:T(8,128)(2,1)S(1)} %get-tuple-element.198), channel_id=1, source_target_pairs={{0,2},{1,3},{2,0},{3,1},{4,6},{5,7},{6,4},{7,5},{8,10},{9,11},{10,... | collective-permute-start | bytes 3538952 | tf_op jit(solution)/shard_map/ppermute | solution.py:905
  241.8 33.3 %collective-permute-start.29 = (bf16[2,4,72,768]{3,2,1,0:T(8,128)(2,1)S(1)}, bf16[2,4,72,768]{3,2,1,0:T(8,128)(2,1)S(1)}, u32[]{:S(2)}, u32[]{:S(2)}) collective-permute-start(bf16[2,4,72,768]{3,2,1,0:T(8,128)(2,1)S(1)} %get-tuple-element.210), channel_id=1, source_target_pairs={{0,2},{1,3},{2,0},{3,1},{4,6},{5,7},{6,4},{7,5},{8,10},{9,11},{10,... | collective-permute-start | bytes 2654216 | tf_op jit(solution)/shard_map/ppermute | solution.py:905
  242.4 25.8 %collective-permute-start.31 = (bf16[4,96,768]{2,1,0:T(8,128)(2,1)S(1)}, bf16[4,96,768]{2,1,0:T(8,128)(2,1)S(1)}, u32[]{:S(2)}, u32[]{:S(2)}) collective-permute-start(bf16[4,96,768]{2,1,0:T(8,128)(2,1)S(1)} %fusion.1), channel_id=1, source_target_pairs={{0,4},{1,5},{2,6},{3,7},{4,0},{5,1},{6,2},{7,3},{8,12},{9,13},{10,... | collective-permute-start | bytes 1769480 | tf_op jit(solution)/shard_map/ppermute | solution.py:905
  244.0 31.1 %collective-permute-start.28 = (bf16[2,4,64,768]{3,2,1,0:T(8,128)(2,1)S(1)}, bf16[2,4,64,768]{3,2,1,0:T(8,128)(2,1)S(1)}, u32[]{:S(2)}, u32[]{:S(2)}) collective-permute-start(bf16[2,4,64,768]{3,2,1,0:T(8,128)(2,1)S(1)} %get-tuple-element.209), channel_id=1, source_target_pairs={{0,4},{1,5},{2,6},{3,7},{4,0},{5,1},{6,2},{7,3},{8,12},{9,13},{10,... | collective-permute-start | bytes 2359304 | tf_op jit(solution)/shard_map/ppermute | solution.py:905
  244.7 30.4 %collective-permute-start.30 = (bf16[4,96,768]{2,1,0:T(8,128)(2,1)S(1)}, bf16[4,96,768]{2,1,0:T(8,128)(2,1)S(1)}, u32[]{:S(2)}, u32[]{:S(2)}) collective-permute-start(bf16[4,96,768]{2,1,0:T(8,128)(2,1)S(1)} %fusion), channel_id=1, source_target_pairs={{0,2},{1,3},{2,0},{3,1},{4,6},{5,7},{6,4},{7,5},{8,10},{9,11},{10,... | collective-permute-start | bytes 1769480 | tf_op jit(solution)/shard_map/ppermute | solution.py:905
  275.0 7.4 %collective-permute-start.32 = (bf16[528,3072]{1,0:T(8,128)(2,1)S(1)}, bf16[528,3072]{1,0:T(8,128)(2,1)S(1)}, u32[]{:S(2)}, u32[]{:S(2)}) collective-permute-start(bf16[528,3072]{1,0:T(8,128)(2,1)S(1)} %get-tuple-element.216.send), channel_id=1, source_target_pairs={{0,1},{1,0},{2,3},{3,2},{4,5},{5,4},{6,7},{7,6},{8,9},{9,8},{10,11... | collective-permute-start | bytes 9732104 | tf_op jit(solution)/shard_map/ppermute | solution.py:905
  275.2 18.2 %collective-permute-start.38 = (bf16[4,72,768]{2,1,0:T(8,128)(2,1)S(1)}, bf16[4,72,768]{2,1,0:T(8,128)(2,1)S(1)}, u32[]{:S(2)}, u32[]{:S(2)}) collective-permute-start(bf16[4,72,768]{2,1,0:T(8,128)(2,1)S(1)} %fusion.4), channel_id=1, source_target_pairs={{0,4},{1,5},{2,6},{3,7},{4,0},{5,1},{6,2},{7,3},{8,12},{9,13},{10,... | collective-permute-start | bytes 1327112 | tf_op jit(solution)/shard_map/ppermute | solution.py:905
  277.1 14.8 %collective-permute-start.33 = (bf16[192,768]{1,0:T(8,128)(2,1)S(1)}, bf16[192,768]{1,0:T(8,128)(2,1)S(1)}, u32[]{:S(2)}, u32[]{:S(2)}) collective-permute-start(bf16[192,768]{1,0:T(8,128)(2,1)S(1)} %pad_maximum_fusion.13), channel_id=1, source_target_pairs={{0,8},{1,9},{2,10},{3,11},{4,12},{5,13},{6,14},{7,15},{8,16},{9,17... | collective-permute-start | bytes 884744 | tf_op jit(solution)/shard_map/ppermute | solution.py:918
  281.8 11.5 %collective-permute-start.37 = (bf16[4,64,768]{2,1,0:T(8,128)(2,1)S(1)}, bf16[4,64,768]{2,1,0:T(8,128)(2,1)S(1)}, u32[]{:S(2)}, u32[]{:S(2)}) collective-permute-start(bf16[4,64,768]{2,1,0:T(8,128)(2,1)S(1)} %fusion.7), channel_id=1, source_target_pairs={{0,2},{1,3},{2,0},{3,1},{4,6},{5,7},{6,4},{7,5},{8,10},{9,11},{10,... | collective-permute-start | bytes 1179656 | tf_op jit(solution)/shard_map/ppermute | solution.py:905
  292.0 10.5 %collective-permute-start.36 = (bf16[192,768]{1,0:T(8,128)(2,1)S(1)}, bf16[192,768]{1,0:T(8,128)(2,1)S(1)}, u32[]{:S(2)}, u32[]{:S(2)}) collective-permute-start(bf16[192,768]{1,0:T(8,128)(2,1)S(1)} %fusion.2), channel_id=1, source_target_pairs={{0,8},{1,9},{2,10},{3,11},{4,12},{5,13},{6,14},{7,15},{8,16},{9,17... | collective-permute-start | bytes 884744 | tf_op jit(solution)/shard_map/ppermute | solution.py:918
  292.0 24.6 %collective-permute-start.35 = (bf16[2,4,56,768]{3,2,1,0:T(8,128)(2,1)S(1)}, bf16[2,4,56,768]{3,2,1,0:T(8,128)(2,1)S(1)}, u32[]{:S(2)}, u32[]{:S(2)}) collective-permute-start(bf16[2,4,56,768]{3,2,1,0:T(8,128)(2,1)S(1)} %get-tuple-element.223), channel_id=1, source_target_pairs={{0,2},{1,3},{2,0},{3,1},{4,6},{5,7},{6,4},{7,5},{8,10},{9,11},{10,... | collective-permute-start | bytes 2064392 | tf_op jit(solution)/shard_map/ppermute | solution.py:905
  292.6 24.0 %collective-permute-start.34 = (bf16[2,4,48,768]{3,2,1,0:T(8,128)(2,1)S(1)}, bf16[2,4,48,768]{3,2,1,0:T(8,128)(2,1)S(1)}, u32[]{:S(2)}, u32[]{:S(2)}) collective-permute-start(bf16[2,4,48,768]{3,2,1,0:T(8,128)(2,1)S(1)} %get-tuple-element.222), channel_id=1, source_target_pairs={{0,4},{1,5},{2,6},{3,7},{4,0},{5,1},{6,2},{7,3},{8,12},{9,13},{10,... | collective-permute-start | bytes 1769480 | tf_op jit(solution)/shard_map/ppermute | solution.py:905
  302.5 14.1 %collective-permute-start.40 = (bf16[192,768]{1,0:T(8,128)(2,1)S(1)}, bf16[192,768]{1,0:T(8,128)(2,1)S(1)}, u32[]{:S(2)}, u32[]{:S(2)}) collective-permute-start(bf16[192,768]{1,0:T(8,128)(2,1)S(1)} %fusion.3), channel_id=1, source_target_pairs={{0,8},{1,9},{2,10},{3,11},{4,12},{5,13},{6,14},{7,15},{8,16},{9,17... | collective-permute-start | bytes 884744 | tf_op jit(solution)/shard_map/ppermute | solution.py:918
  303.0 13.6 %collective-permute-start.39 = (bf16[136,768]{1,0:T(8,128)(2,1)S(1)}, bf16[136,768]{1,0:T(8,128)(2,1)S(1)}, u32[]{:S(2)}, u32[]{:S(2)}) collective-permute-start(bf16[136,768]{1,0:T(8,128)(2,1)S(1)} %pad_maximum_fusion.14), channel_id=1, source_target_pairs={{0,8},{1,9},{2,10},{3,11},{4,12},{5,13},{6,14},{7,15},{8,16},{9,17... | collective-permute-start | bytes 626696 | tf_op jit(solution)/shard_map/ppermute | solution.py:918
  316.7 10.7 %collective-permute-start.43 = (bf16[4,56,768]{2,1,0:T(8,128)(2,1)S(1)}, bf16[4,56,768]{2,1,0:T(8,128)(2,1)S(1)}, u32[]{:S(2)}, u32[]{:S(2)}) collective-permute-start(bf16[4,56,768]{2,1,0:T(8,128)(2,1)S(1)} %fusion.8), channel_id=1, source_target_pairs={{0,4},{1,5},{2,6},{3,7},{4,0},{5,1},{6,2},{7,3},{8,12},{9,13},{10,... | collective-permute-start | bytes 1032200 | tf_op jit(solution)/shard_map/ppermute | solution.py:905
  317.5 9.9 %collective-permute-start.42 = (bf16[4,48,768]{2,1,0:T(8,128)(2,1)S(1)}, bf16[4,48,768]{2,1,0:T(8,128)(2,1)S(1)}, u32[]{:S(2)}, u32[]{:S(2)}) collective-permute-start(bf16[4,48,768]{2,1,0:T(8,128)(2,1)S(1)} %fusion.11), channel_id=1, source_target_pairs={{0,2},{1,3},{2,0},{3,1},{4,6},{5,7},{6,4},{7,5},{8,10},{9,11},{10,... | collective-permute-start | bytes 884744 | tf_op jit(solution)/shard_map/ppermute | solution.py:905
  318.2 9.3 %collective-permute-start.41 = (bf16[136,768]{1,0:T(8,128)(2,1)S(1)}, bf16[136,768]{1,0:T(8,128)(2,1)S(1)}, u32[]{:S(2)}, u32[]{:S(2)}) collective-permute-start(bf16[136,768]{1,0:T(8,128)(2,1)S(1)} %fusion.6), channel_id=1, source_target_pairs={{0,8},{1,9},{2,10},{3,11},{4,12},{5,13},{6,14},{7,15},{8,16},{9,17... | collective-permute-start | bytes 626696 | tf_op jit(solution)/shard_map/ppermute | solution.py:918
  327.7 8.5 %collective-permute-start.45 = (bf16[104,768]{1,0:T(8,128)(2,1)S(1)}, bf16[104,768]{1,0:T(8,128)(2,1)S(1)}, u32[]{:S(2)}, u32[]{:S(2)}) collective-permute-start(bf16[104,768]{1,0:T(8,128)(2,1)S(1)} %pad_maximum_fusion.15), channel_id=1, source_target_pairs={{0,24},{1,25},{2,26},{3,27},{4,28},{5,29},{6,30},{7,31},{8,0},{9,1... | collective-permute-start | bytes 479240 | tf_op jit(solution)/shard_map/ppermute | solution.py:918
  327.8 15.8 %collective-permute-start.46 = (bf16[104,768]{1,0:T(8,128)(2,1)S(1)}, bf16[104,768]{1,0:T(8,128)(2,1)S(1)}, u32[]{:S(2)}, u32[]{:S(2)}) collective-permute-start(bf16[104,768]{1,0:T(8,128)(2,1)S(1)} %pad_maximum_fusion.16), channel_id=1, source_target_pairs={{0,16},{1,17},{2,18},{3,19},{4,20},{5,21},{6,22},{7,23},{8,24},{9,... | collective-permute-start | bytes 479240 | tf_op jit(solution)/shard_map/ppermute | solution.py:918
  327.9 15.7 %collective-permute-start.47 = (bf16[104,768]{1,0:T(8,128)(2,1)S(1)}, bf16[104,768]{1,0:T(8,128)(2,1)S(1)}, u32[]{:S(2)}, u32[]{:S(2)}) collective-permute-start(bf16[104,768]{1,0:T(8,128)(2,1)S(1)} %pad_maximum_fusion.17), channel_id=1, source_target_pairs={{0,8},{1,9},{2,10},{3,11},{4,12},{5,13},{6,14},{7,15},{8,16},{9,17... | collective-permute-start | bytes 479240 | tf_op jit(solution)/shard_map/ppermute | solution.py:918
  330.1 13.8 %collective-permute-start.44 = (bf16[136,768]{1,0:T(8,128)(2,1)S(1)}, bf16[136,768]{1,0:T(8,128)(2,1)S(1)}, u32[]{:S(2)}, u32[]{:S(2)}) collective-permute-start(bf16[136,768]{1,0:T(8,128)(2,1)S(1)} %fusion.5), channel_id=1, source_target_pairs={{0,8},{1,9},{2,10},{3,11},{4,12},{5,13},{6,14},{7,15},{8,16},{9,17... | collective-permute-start | bytes 626696 | tf_op jit(solution)/shard_map/ppermute | solution.py:918
  349.4 9.9 %all-to-all-start = ((f32[32,2,128]{2,1,0:T(2,128)}), f32[32,2,128]{2,1,0:T(2,128)S(1)}, u32[]{:S(2)}, u32[]{:S(2)}) async-start(f32[32,2,128]{2,1,0:T(2,128)} %broadcast_in_dim.18), calls=%async_computation | async-start | bytes 65536 | tf_op jit(solution)/shard_map/all_to_all | solution.py:1651
  (56 other events, 441.8 us)
